TPU v7x, 256 devices: a whole 4x4x8 slice. The times are simulated.
256 devices in a mesh: slab: 32 (over x, z_lo, core), kgrp: 8 (over y, z_hi).
Axes of the slice: x: 4, y: 4, z: 8 (z_hi: 2, z_lo: 4; z = z_hi * 4 + z_lo), core: 2. Of those that a mesh axis runs over, the one named last changes fastest.
Arguments:
- atom_descriptors: bfloat16 [32768, 128], P(('slab', 'kgrp')), may hold values from -6 to 6
- atom_locations: float32 [3, 32768], P(None, ('slab', 'kgrp')), may hold values from 0 to 32, as said below
- adjacent_atom_slots: int32 [32768, 64], P(('slab', 'kgrp')), may hold values from 0 to 3071
- neighbour_tally: int32 [32768], P(('slab', 'kgrp')), may hold values from 16 to 64
- filled_slot_tallies: int32 [32], replicated, may hold values from 1 to 1024, 24576 in all
- reciprocal_lattice_modes: float32 [3, 8192], P(None, 'kgrp'), may hold values from -4 to 4
- edge_update_matrix: bfloat16 [2, 128, 128], replicated, may hold values from -0.5 to 0.5
- node_update_matrix: bfloat16 [2, 128, 128], replicated, may hold values from -0.5 to 0.5
- distance_basis_mixing: float32 [2, 8, 128], replicated, may hold values from -2 to 2
- latent_ionic_readout: bfloat16 [128, 16], replicated, may hold values from -0.5 to 0.5
Outputs:
- potential: float32 [16, 32768], P(None, ('slab', 'kgrp'))
- forces: float32 [3, 32768], P(None, ('slab', 'kgrp'))
Inputs may be any that keep to these rules, and one draw needn't show every extreme that they name: `atom_locations`: coordinates of atoms of slab s: first in [s, s+1), others in [0, 1).
All inputs are finite; a program needn't handle non-finite values.
Results may differ from a plain program's by a relative error of at most 0.0028.
Values may be sent and summed in bfloat16 or wider, within the bound.
No kernel may reach another device: no remote copies, remote signals or barrier semaphores. Data moves between devices by JAX's collectives and lax.ppermute only.
A program may use at most 64 MiB of HBM per device.

v0:
```python
import math

import jax
import jax.numpy as jnp
from jax import lax
from jax.experimental import pallas as pl
from jax.experimental.pallas import tpu as pltpu
from jax.sharding import PartitionSpec as P

AXES = ("slab", "kgrp")
F32 = jnp.float32
BF16 = jnp.bfloat16
MIB = 1 << 20

ROWS = 128
PAYLOAD = 144
HALF = 64

CENTRE = 3.04
SINC = (0.4531433647, -0.11001027431, 0.0067080034928, -0.00018563842882, 2.9260279482e-06)
TWOCOS = (-0.504597100576, -0.581178942324, 0.0705470232447, -0.0028677843003, 5.9501086291e-05, -7.504320417652e-07)
SINTURN = (6.283184916495, -41.341589232689, 81.599943329776, -76.614472532619, 41.342882354378, -12.471243534759)
COSTURN = (0.99999921078, -19.738980355764, 64.92865742103, -85.271621534265, 58.790492119989, -21.071105627427)


def horner(coefficients, x):
    value = coefficients[-1] * x + coefficients[-2]
    for c in coefficients[-3::-1]:
        value = value * x + c
    return value


def split(x, parts):
    pieces = []
    for i in range(parts):
        piece = x.astype(BF16)
        pieces.append(piece)
        if i + 1 < parts:
            x = x - piece.astype(F32)
    return pieces


def nt(a, b):
    return lax.dot_general(a, b, (((1,), (1,)), ((), ())), preferred_element_type=F32)


def nn(a, b):
    return jnp.dot(a, b, preferred_element_type=F32)


def call(body, out_shape, *operands, scalars=(), after=(), name, flops=0, limit=12, scratch=()):
    n, m = len(scalars) + len(operands), len(after)
    return pl.pallas_call(
        lambda *refs: body(*refs[:n], *refs[n + m :]),
        out_shape=out_shape,
        in_specs=[pl.BlockSpec(memory_space=pltpu.SMEM)] * len(scalars)
        + [pl.BlockSpec(memory_space=pltpu.VMEM)] * len(operands)
        + [pl.BlockSpec(memory_space=pl.ANY)] * m,
        scratch_shapes=list(scratch),
        name=name,
        cost_estimate=pl.CostEstimate(flops=flops, bytes_accessed=MIB, transcendentals=0),
        compiler_params=pltpu.CompilerParams(vmem_limit_bytes=limit * MIB),
    )(*scalars, *operands, *after)


def pack_body(desc_ref, loc_ref, out_ref):
    out_ref[0:ROWS, :] = desc_ref[...]
    hi, mid, lo = [p.astype(F32) for p in split(loc_ref[...], 3)]
    tail = jnp.concatenate([hi, mid, lo, jnp.zeros((7, ROWS), F32)], axis=0)
    out_ref[ROWS:PAYLOAD, :] = tail.astype(BF16)


def coordinates(payload):
    tail = payload[ROWS:PAYLOAD, :].astype(F32)
    return (tail[0:3] + tail[3:6]) + tail[6:9]


def count_body(scal_ref, slots_ref, cnt0, cnt1, cnt2, cnt3, target_s, low_s):
    y, zh, odd = scal_ref[0], scal_ref[1], scal_ref[2]
    f_prev, f_own, f_next, base = scal_ref[3], scal_ref[4], scal_ref[5], scal_ref[6]
    slots = slots_ref[...]
    shape = slots.shape
    lane = lax.broadcasted_iota(jnp.int32, shape, 1)
    row = lax.broadcasted_iota(jnp.int32, shape, 0)
    local = lane >> 6
    atom = row * 8 + local + base
    region = slots >> 10
    within = slots & 1023
    filled = jnp.where(region == 0, f_prev, jnp.where(region == 1, f_own, f_next))
    usable = (slots >= 0) & (within < filled) & (atom < f_own)
    kblock = within >> 7
    place = jnp.where(region == 1, 0, jnp.where(region == 2 * odd, 2, 4)) + ((kblock & 1) ^ zh)
    target = jnp.where(usable, ((((kblock >> 1) - y) & 3) * 6 + place) * 8 + local, -1)
    target_s[...] = target
    low_s[...] = slots & 127
    iota_p = lax.broadcasted_iota(jnp.int32, (192, 512), 0)
    iota_l = lax.broadcasted_iota(jnp.int32, (128, 512), 0)

    @pl.loop(0, 4)
    def _(step):
        for u in range(4):
            i = step * 4 + u
            p = jnp.where(iota_p == target_s[pl.ds(i, 1), :], 1.0, 0.0).astype(BF16)
            l = jnp.where(iota_l == low_s[pl.ds(i, 1), :], 1.0, 0.0).astype(BF16)
            c = nt(p, l).reshape(24, 8, 128)
            for j, cnt_ref in enumerate((cnt0, cnt1, cnt2, cnt3)):
                cnt_ref[:, pl.ds(pl.multiple_of(8 * i, 8), 8), :] = c[6 * j : 6 * j + 6]


def update(gathered, hidden, self_weight):
    drive = gathered * 0.125 + nn(hidden, self_weight)
    return (hidden.astype(F32) + drive * jax.nn.sigmoid(drive)).astype(BF16)


def mix(acc, mixing):
    total = acc[0:HALF] * mixing[0:1]
    for n in range(1, 8):
        total = total + acc[n * HALF : (n + 1) * HALF] * mixing[n : n + 1]
    return total


def rows_of(h, count):
    return pl.ds(pl.multiple_of(h * count, count), count)


def block_of(y_ref, c_ref, i):
    return y_ref[i] if i < 4 else c_ref[i - 4]


def here_of(near_ref, z, here_s):
    xyz = coordinates(near_ref[z])
    for d in range(3):
        here_s[d] = jnp.broadcast_to(xyz[d : d + 1], (128, ROWS)).T


def basis_half(h, shift_ref, y_ref, c_ref, cnt_ref, g_ref, here_s):
    for i in range(6):
        xyz = coordinates(block_of(y_ref, c_ref, i))
        x = xyz[0:1] + shift_ref[i // 2]
        for r in range(0, HALF, 32):
            rows = pl.ds(pl.multiple_of(h * HALF + r, 32), 32)
            dx = x - here_s[0, rows, :]
            dy = xyz[1:2] - here_s[1, rows, :]
            dz = xyz[2:3] - here_s[2, rows, :]
            v = dx * dx + dy * dy + dz * dz + (0.04 - CENTRE)
            cur = cnt_ref[i, rows, :] * horner(SINC, v)
            turn = horner(TWOCOS, v)
            prev = None
            for n in range(8):
                g_ref[pl.ds(pl.multiple_of(h * 512 + n * HALF + r, 32), 32), i * 128 : (i + 1) * 128] = cur.astype(BF16)
                if n < 7:
                    nxt = turn * cur if prev is None else turn * cur - prev
                    prev, cur = cur, nxt


def messages_of(y_ref, c_ref, weight):
    rows = jnp.concatenate([block_of(y_ref, c_ref, i)[0:ROWS, :] for i in range(6)], axis=0)
    return nn(rows, weight).astype(BF16)


def first_body(shift_ref, y_ref, c_ref, cnt_ref, edge_ref, mixing_ref, g_ref, part_ref, here_s, messages_s):
    messages_s[...] = messages_of(y_ref, c_ref, edge_ref[0])
    here_of(y_ref, 0, here_s)

    @pl.loop(0, 2)
    def _(h):
        basis_half(h, shift_ref, y_ref, c_ref, cnt_ref, g_ref, here_s)
        part_ref[rows_of(h, HALF), :] = mix(nn(g_ref[rows_of(h, 512), :], messages_s[...]), mixing_ref[0])


def first_rest_body(shift_ref, near_ref, y1, y2, y3, c1, c2, c3, n1, n2, n3, edge_ref, mixing_ref, part_ref, node_ref, g1, g2, g3, hidden_ref, here_s, messages_s, total_s):
    for j, (y, c) in enumerate(((y1, c1), (y2, c2), (y3, c3))):
        messages_s[j] = messages_of(y, c, edge_ref[0])
    here_of(near_ref, 0, here_s)

    @pl.loop(0, 2)
    def _(h):
        acc = None
        for j, (y, c, n, g) in enumerate(((y1, c1, n1, g1), (y2, c2, n2, g2), (y3, c3, n3, g3))):
            basis_half(h, shift_ref, y, c, n, g, here_s)
            term = nn(g[rows_of(h, 512), :], messages_s[j])
            acc = term if acc is None else acc + term
        total_s[rows_of(h, HALF), :] = mix(acc, mixing_ref[0])

    hidden_ref[...] = update(part_ref[...] + total_s[...], near_ref[0, 0:ROWS, :], node_ref[0])


def partner_body(shift_ref, near_ref, ya, yb, ca, cb, na, nb, ga, gb, here_s):
    here_of(near_ref, 1, here_s)

    @pl.loop(0, 2)
    def _(h):
        basis_half(h, shift_ref, ya, ca, na, ga, here_s)
        basis_half(h, shift_ref, yb, cb, nb, gb, here_s)


def second_body(y_ref, c_ref, own_ref, partner_ref, edge_ref, mixing_ref, part_ref, messages_s):
    messages_s[...] = messages_of(y_ref, c_ref, edge_ref[1])

    @pl.loop(0, 2)
    def _(h):
        for z, g in enumerate((own_ref, partner_ref)):
            part_ref[z, rows_of(h, HALF), :] = mix(nn(g[rows_of(h, 512), :], messages_s[...]), mixing_ref[1])


def second_rest_body(scal_ref, y1, y2, y3, c1, c2, c3, o1, o2, o3, p1, p2, p3, edge_ref, mixing_ref, part_ref, near_ref, node_ref, readout_ref, charge_ref, messages_s, total_s):
    for j, (y, c) in enumerate(((y1, c1), (y2, c2), (y3, c3))):
        messages_s[j] = messages_of(y, c, edge_ref[1])

    @pl.loop(0, 2)
    def _(h):
        for z, gs in enumerate(((o1, o2, o3), (p1, p2, p3))):
            acc = None
            for j, g in enumerate(gs):
                term = nn(g[rows_of(h, 512), :], messages_s[j])
                acc = term if acc is None else acc + term
            total_s[z, rows_of(h, HALF), :] = mix(acc, mixing_ref[1])

    for z in range(2):
        hidden = update(part_ref[z] + total_s[z], near_ref[z], node_ref[1])
        charges = nt(readout_ref[...], hidden)
        atom = lax.broadcasted_iota(jnp.int32, charges.shape, 1) + scal_ref[6 + z]
        charge_ref[z] = jnp.where(atom < scal_ref[4], charges, 0.0)


def copy_body(in_ref, out_ref):
    out_ref[...] = in_ref[...]


def stack_body(a, b, c, d, out_ref):
    for i, ref in enumerate((a, b, c, d)):
        out_ref[i] = ref[...]


def cross(pieces, left):
    hi, mid, lo = [p.astype(F32) for p in pieces]
    rows = [hi, hi, mid, hi, lo, mid] if left else [hi, mid, hi, lo, hi, mid]
    return jnp.concatenate(rows + [jnp.zeros((6, hi.shape[1]), F32)], axis=0)


def modes_body(modes_ref, out_ref):
    turns = modes_ref[...] * (0.5 / math.pi)
    out_ref[...] = cross(split(turns, 3), True).T.astype(BF16)


def phase_body(y_ref, modes_ref, wave_ref):

    @pl.loop(0, 2)
    def _(b):
        places = cross(split(coordinates(y_ref[b]), 3), False).astype(BF16)
        columns = pl.ds(pl.multiple_of(b * 128, 128), 128)
        for r in range(0, 1024, 64):
            turns = nn(modes_ref[r : r + 64, :], places)
            rest = turns - jnp.round(turns)
            square = rest * rest
            wave_ref[r : r + 64, columns] = horner(COSTURN, square).astype(BF16)
            wave_ref[r + 1024 : r + 1088, columns] = (rest * horner(SINTURN, square)).astype(BF16)


def half_of(ref, half, sine):
    return ref[pl.ds(pl.multiple_of(half * 512 + sine * 1024, 512), 512), :]


def structure_body(half_ref, w0, w1, w2, w3, q0, q1, q2, q3, mine_ref, theirs_ref):
    pieces = [jnp.concatenate(split(jnp.concatenate([q[0], q[1]], axis=1), 3), axis=0) for q in (q0, q1, q2, q3)]
    for half, out_ref in ((1 - half_ref[0], theirs_ref), (half_ref[0], mine_ref)):
        for i in range(2):
            s = None
            for p, w in zip(pieces, (w0, w1, w2, w3)):
                term = nt(p, half_of(w, half, i))
                s = term if s is None else s + term
            out_ref[16 * i : 16 * i + 16, :] = s[0:16] + s[16:32] + s[32:48]


def respond_body(half_ref, place_ref, scale_ref, w0, w1, w2, w3, q0, q1, q2, q3, mine_ref, theirs_ref, modes_ref, out_ref):
    k = modes_ref[...]
    square = k[0:1] * k[0:1] + k[1:2] * k[1:2] + k[2:3] * k[2:3]
    weight = scale_ref[0] * jnp.exp(square * -0.125) / (square + 1.0)
    low = jnp.where(half_ref[0] == 0, mine_ref[...], theirs_ref[...])
    high = jnp.where(half_ref[0] == 0, theirs_ref[...], mine_ref[...])
    total = jnp.concatenate([low, high], axis=1) * weight
    real, imag = total[0:16], total[16:32]
    left = [real] + [imag * k[j : j + 1] for j in range(3)]
    right = [imag] + [real * -k[j : j + 1] for j in range(3)]
    both = jnp.concatenate([jnp.concatenate(left, axis=0), jnp.concatenate(right, axis=0)], axis=1)
    pieces = jnp.concatenate(split(both, 2), axis=0)
    for i, (w, q) in enumerate(zip((w0, w1, w2, w3), (q0, q1, q2, q3))):
        out = nn(pieces, w[...])
        out = out[0:64] + out[64:128]
        for b in range(2):
            mine = out[:, b * 128 : (b + 1) * 128]
            force = [-jnp.sum(mine[16 * j + 16 : 16 * j + 32] * q[b], axis=0, keepdims=True) for j in range(3)]
            out_ref[place_ref[2 * i + b]] = jnp.concatenate([mine[0:16]] + force + [jnp.zeros((5, 128), F32)], axis=0)


def finish_body(parts_ref, potential_ref, forces_ref):
    total = parts_ref[0]
    for i in range(1, 8):
        total = total + parts_ref[i]
    potential_ref[...] = total[0:16]
    forces_ref[...] = total[16:19]


def pairs(n_slab, target):
    return [(s * 8 + k, (target(s, k)[0] % n_slab) * 8 + target(s, k)[1]) for s in range(n_slab) for k in range(8)]


def move(x, target):
    return lax.ppermute(x, AXES, pairs(lax.axis_size("slab"), target))


def over_chip(s):
    return s + 1 if s % 2 else s - 1


def near_blocks(block):
    half = move(block, lambda s, k: (s, k ^ 1))
    near = move(block, lambda s, k: (over_chip(s), k))
    both = move(block, lambda s, k: (over_chip(s), k ^ 1))
    return half, near, both


def surroundings(block, near, name, after):
    stack = call(stack_body, jax.ShapeDtypeStruct((4,) + block.shape, BF16), block, *near, name=name, after=after)
    ys = [stack]
    for j in range(1, 4):
        ys.append(move(stack, lambda s, k: (s, (k - 2 * j) % 8)))
    return ys, [move(y[0:2], lambda s, k: (s ^ 1, k)) for y in ys]


def shards(
    atom_descriptors,
    atom_locations,
    adjacent_atom_slots,
    neighbour_tally,
    filled_slot_tallies,
    reciprocal_lattice_modes,
    edge_update_matrix,
    node_update_matrix,
    distance_basis_mixing,
    latent_ionic_readout,
):
    n_slab = lax.axis_size("slab")
    slab = lax.axis_index("slab")
    group = lax.axis_index("kgrp")
    odd = slab % 2
    y, zh = group // 2, group % 2
    filled = jnp.take(filled_slot_tallies, (slab + jnp.arange(3) - 1) % n_slab)
    scal = jnp.concatenate([jnp.stack([y, zh, odd]), filled, jnp.stack([group * ROWS, (group ^ 1) * ROWS])]).astype(jnp.int32)
    low_edge = jnp.where(slab == 0, -float(n_slab), 0.0)
    high_edge = jnp.where(slab == n_slab - 1, float(n_slab), 0.0)
    shift = jnp.stack([0.0, jnp.where(odd == 1, high_edge, low_edge), jnp.where(odd == 1, low_edge, high_edge)]).astype(F32)
    spots = jnp.arange(8, dtype=jnp.int32)
    place = (((y + spots // 2) % 4) * 2 + ((spots % 2) ^ zh)).astype(jnp.int32)

    shape = jax.ShapeDtypeStruct
    block = call(pack_body, shape((PAYLOAD, ROWS), BF16), atom_descriptors, atom_locations, name="pack")
    near = near_blocks(block)
    used = jnp.arange(64, dtype=jnp.int32)[None, :] < neighbour_tally[:, None]
    slots = jnp.where(used, adjacent_atom_slots, -1).reshape(16, 512)

    def count(slots, base, name, after=()):
        bounds = jnp.concatenate([scal[:6], scal[base : base + 1]])
        return call(
            count_body, [shape((6, ROWS, 128), F32)] * 4, slots, scalars=(bounds,), name=name, flops=10**9, after=after,
            scratch=[pltpu.VMEM((16, 512), jnp.int32)] * 2,
        )

    counts = count(slots, 6, "counts")
    ys, cs = surroundings(block, near, "stack_first", (counts[0],))
    late = call(copy_body, shape((16, 512), jnp.int32), slots, name="late", after=(cs[0],))
    partner_slots = move(late, lambda s, k: (s, k ^ 1))
    wide = shape((8 * ROWS, 6 * ROWS), BF16)
    here = pltpu.VMEM((3, ROWS, 128), F32)
    message = lambda *n: pltpu.VMEM(n + (6 * ROWS, 128), BF16)
    basis = [None] * 4
    basis[0], part = call(
        first_body, (wide, shape((ROWS, 128), F32)),
        ys[0], cs[0], counts[0], edge_update_matrix, distance_basis_mixing,
        scalars=(shift,), name="first_0", flops=10**9, scratch=[here, message()],
    )
    basis[1], basis[2], basis[3], hidden = call(
        first_rest_body, (wide, wide, wide, shape((ROWS, 128), BF16)),
        *ys, *cs[1:], *counts[1:], edge_update_matrix, distance_basis_mixing, part, node_update_matrix,
        scalars=(shift,), name="first_rest", flops=10**9, scratch=[here, message(3), pltpu.VMEM((ROWS, 128), F32)], after=(partner_slots,),
    )
    partner_counts = count(partner_slots, 7, "partner_counts", (hidden,))
    turns = call(modes_body, shape((1024, 24), BF16), reciprocal_lattice_modes, name="modes")

    def phases(j, after):
        return call(phase_body, shape((2048, 256), BF16), ys[j], turns, name=f"phases_{j}", flops=10**9, after=after)

    def partner_basis(a, b, after):
        return call(
            partner_body, [wide, wide], ys[0], ys[a], ys[b], cs[a], cs[b], partner_counts[a], partner_counts[b],
            scalars=(shift,), name=f"partner_{a}", flops=10**9, scratch=[here], after=after,
        )

    near = near_blocks(hidden)
    partner = [*partner_basis(0, 1, (hidden,))]
    ms, ns = surroundings(hidden, near, "stack_second", partner[:1])
    partner += [*partner_basis(2, 3, (ms[0],))]
    waves = [phases(j, (ms[0],)) for j in range(2)]
    part = call(
        second_body, shape((2, ROWS, 128), F32),
        ms[0], ns[0], basis[0], partner[0], edge_update_matrix, distance_basis_mixing,
        name="second_0", flops=10**9, scratch=[message()], after=[partner[2], *waves],
    )
    charges = call(
        second_rest_body, shape((2, 16, ROWS), F32),
        *ms[1:], *ns[1:], *basis[1:], *partner[1:], edge_update_matrix, distance_basis_mixing, part, ms[0], node_update_matrix, latent_ionic_readout.T,
        scalars=(scal,), name="second_rest", flops=10**9, scratch=[message(3), pltpu.VMEM((2, ROWS, 128), F32)],
    )
    qs = [charges] + [move(charges, lambda s, k, j=j: (s, (k - 2 * j) % 8)) for j in range(1, 4)]
    waves += [phases(j, (charges,)) for j in range(2, 4)]
    mine = jnp.reshape(odd, (1,)).astype(jnp.int32)
    part, away = call(
        structure_body, (shape((32, 512), F32), shape((32, 512), F32)), *waves, *qs,
        scalars=(mine,), name="structure", flops=10**8,
    )
    part = part + move(away, lambda s, k: (s ^ 1, k))
    half = part.astype(BF16)
    part = part + sum(move(half, lambda s, k, m=m: (s + 8 * m, k)).astype(F32) for m in (1, 2, 3))
    half = part.astype(BF16)
    part = part + sum(move(half, lambda s, k, m=m: (s ^ (2 * m), k)).astype(F32) for m in (1, 2, 3))
    other = move(part, lambda s, k: (s ^ 1, k))
    scale = jnp.full((1,), 4.0 / math.sqrt(n_slab * 1024 * reciprocal_lattice_modes.shape[1] * 8), F32)
    partial = call(
        respond_body, shape((8, 24, ROWS), F32), *waves, *qs, part, other, reciprocal_lattice_modes,
        scalars=(mine, place, scale), name="respond", flops=10**8,
    )
    partial = lax.all_to_all(partial, "kgrp", 0, 0)
    return tuple(call(finish_body, (shape((16, ROWS), F32), shape((3, ROWS), F32)), partial, name="finish"))


def solution(mesh):
    return jax.shard_map(
        shards,
        mesh=mesh,
        in_specs=(
            P(("slab", "kgrp"), None),
            P(None, ("slab", "kgrp")),
            P(("slab", "kgrp"), None),
            P(("slab", "kgrp")),
            P(),
            P(None, "kgrp"),
            P(),
            P(),
            P(),
            P(),
        ),
        out_specs=(P(None, ("slab", "kgrp")), P(None, ("slab", "kgrp"))),
        check_vma=False,
    )
```

profile of v0, /device:TPU:1, one launch (start us, length us, event | category | flops | bytes accessed | tf_op | source)
XLA Modules:
  0.0 110.5 jit_solution(15324629456376842316)
XLA Ops:
  2.1 7.8 %collective-permute-start = (bf16[144,128]{1,0:T(8,128)(2,1)S(1)}, bf16[144,128]{1,0:T(8,128)(2,1)S(1)}, u32[]{:S(2)}, u32[]{:S(2)}) collective-permute-start(bf16[144,128]{1,0:T(8,128)(2,1)S(1)} %pack.1.refs_0_), channel_id=1, source_target_pairs={{0,1},{1,0},{2,3},{3,2},{4,5},{5,4},{6,7},{7,6},{8,9},{9,8},{10,11... | collective-permute-start | bytes 110600 | tf_op jit(solution)/shard_map/ppermute | solution.py:309
  9.9 1.6 %collective-permute-start.1 = (bf16[144,128]{1,0:T(8,128)(2,1)S(1)}, bf16[144,128]{1,0:T(8,128)(2,1)S(1)}, u32[]{:S(2)}, u32[]{:S(2)}) collective-permute-start(bf16[144,128]{1,0:T(8,128)(2,1)S(1)} %pack.1.refs_0_), channel_id=1, source_target_pairs={{0,248},{1,249},{2,250},{3,251},{4,252},{5,253},{6,254},{7,255},{8... | collective-permute-start | bytes 110600 | tf_op jit(solution)/shard_map/ppermute | solution.py:309
  13.2 2.1 %counts.1 = (f32[6,128,128]{2,1,0:T(8,128)S(1)}, f32[6,128,128]{2,1,0:T(8,128)S(1)}, f32[6,128,128]{2,1,0:T(8,128)S(1)}, f32[6,128,128]{2,1,0:T(8,128)S(1)}) custom-call(s32[7]{0:T(128)S(1)} %concatenate.12.refs_0_, s32[16,512]{1,0:T(8,128)S(1)} %reshape.69.refs_1_.refs_0_), custom_call_target="tpu_custom_call" | custom-call | flops 1000000000 | bytes 1048576 | tf_op jit(solution)/shard_map/counts/pallas_call | solution.py:53
  15.4 2.6 %collective-permute-done.2.refs_3_ = bf16[144,128]{1,0:T(8,128)(2,1)S(1)} collective-permute-done((bf16[144,128]{1,0:T(8,128)(2,1)S(1)}, bf16[144,128]{1,0:T(8,128)(2,1)S(1)}, u32[]{:S(2)}, u32[]{:S(2)}) %collective-permute-start.2) | collective-permute-done | bytes 36896 | tf_op jit(solution)/shard_map/ppermute | solution.py:309
  18.0 2.8 %collective-permute-start.3 = (bf16[4,144,128]{2,1,0:T(8,128)(2,1)S(1)}, bf16[4,144,128]{2,1,0:T(8,128)(2,1)S(1)}, u32[]{:S(2)}, u32[]{:S(2)}) collective-permute-start(bf16[4,144,128]{2,1,0:T(8,128)(2,1)S(1)} %stack_first.1.refs_1_.refs_2_.refs_0_), channel_id=1, source_target_pairs={{0,6},{1,7},{2,0},{3,1},{4,2},{5,3},{6,4},{7,5},{8,14},{9,15},{10,... | collective-permute-start | bytes 442376 | tf_op jit(solution)/shard_map/ppermute | solution.py:309
  22.2 4.1 %collective-permute-start.9 = (bf16[2,144,128]{2,1,0:T(8,128)(2,1)S(1)}, bf16[2,144,128]{2,1,0:T(8,128)(2,1)S(1)}, u32[]{:S(2)}, u32[]{:S(2)}) collective-permute-start(bf16[2,144,128]{2,1,0:T(8,128)(2,1)S(1)} %slice.40), channel_id=1, source_target_pairs={{0,8},{1,9},{2,10},{3,11},{4,12},{5,13},{6,14},{7,15},{8,0},{9,1},... | collective-permute-start | bytes 221192 | tf_op jit(solution)/shard_map/ppermute | solution.py:309
  27.2 1.7 %collective-permute-start.10 = (s32[16,512]{1,0:T(8,128)S(1)}, s32[16,512]{1,0:T(8,128)S(1)}, u32[]{:S(2)}, u32[]{:S(2)}) collective-permute-start(s32[16,512]{1,0:T(8,128)S(1)} %late.1), channel_id=1, source_target_pairs={{0,1},{1,0},{2,3},{3,2},{4,5},{5,4},{6,7},{7,6},{8,9},{9,8},{10,11... | collective-permute-start | bytes 98312 | tf_op jit(solution)/shard_map/ppermute | solution.py:309
  29.6 1.4 %collective-permute-start.7 = (bf16[2,144,128]{2,1,0:T(8,128)(2,1)S(1)}, bf16[2,144,128]{2,1,0:T(8,128)(2,1)S(1)}, u32[]{:S(2)}, u32[]{:S(2)}) collective-permute-start(bf16[2,144,128]{2,1,0:T(8,128)(2,1)S(1)} %slice.38), channel_id=1, source_target_pairs={{0,8},{1,9},{2,10},{3,11},{4,12},{5,13},{6,14},{7,15},{8,0},{9,1},... | collective-permute-start | bytes 221192 | tf_op jit(solution)/shard_map/ppermute | solution.py:309
  31.1 1.5 %collective-permute-start.8 = (bf16[2,144,128]{2,1,0:T(8,128)(2,1)S(1)}, bf16[2,144,128]{2,1,0:T(8,128)(2,1)S(1)}, u32[]{:S(2)}, u32[]{:S(2)}) collective-permute-start(bf16[2,144,128]{2,1,0:T(8,128)(2,1)S(1)} %slice.39), channel_id=1, source_target_pairs={{0,8},{1,9},{2,10},{3,11},{4,12},{5,13},{6,14},{7,15},{8,0},{9,1},... | collective-permute-start | bytes 221192 | tf_op jit(solution)/shard_map/ppermute | solution.py:309
  32.6 2.1 %first_0.1 = (bf16[1024,768]{1,0:T(8,128)(2,1)S(1)}, f32[128,128]{1,0:T(8,128)S(1)}) custom-call(f32[3]{0:T(128)S(1)} %pad_maximum_fusion.refs_0_, bf16[4,144,128]{2,1,0:T(8,128)(2,1)S(1)} %stack_first.1.refs_1_.refs_2_.refs_0_, bf16[2,144,128]{2,1,0:T(8,128)(2,1)S(1)} %collective-permute-done.9.refs_2_.refs_1_.refs_4_, ...), custom_call_target="tpu_custom_call" | custom-call | flops 1000000000 | bytes 1048576 | tf_op jit(solution)/shard_map/first_0/pallas_call | solution.py:53
  34.8 4.3 %first_rest.1 = (bf16[1024,768]{1,0:T(8,128)(2,1)S(1)}, bf16[1024,768]{1,0:T(8,128)(2,1)S(1)}, bf16[1024,768]{1,0:T(8,128)(2,1)S(1)}, bf16[128,128]{1,0:T(8,128)(2,1)S(1)}) custom-call(f32[3]{0:T(128)S(1)} %pad_maximum_fusion.refs_0_, bf16[4,144,128]{2,1,0:T(8,128)(2,1)S(1)} %stack_first.1.refs_1_.refs_2_.refs_0_, ...), custom_call_target="tpu_custom_call" | custom-call | flops 1000000000 | bytes 1048576 | tf_op jit(solution)/shard_map/first_rest/pallas_call | solution.py:53
  39.1 1.7 %collective-permute-start.11 = (bf16[128,128]{1,0:T(8,128)(2,1)S(1)}, bf16[128,128]{1,0:T(8,128)(2,1)S(1)}, u32[]{:S(2)}, u32[]{:S(2)}) collective-permute-start(bf16[128,128]{1,0:T(8,128)(2,1)S(1)} %get-tuple-element.27.refs_2_.refs_8_.refs_0_), channel_id=1, source_target_pairs={{0,1},{1,0},{2,3},{3,2},{4,5},{5,4},{6,7},{7,6},{8,9},{9,8},{10,11... | collective-permute-start | bytes 98312 | tf_op jit(solution)/shard_map/ppermute | solution.py:309
  41.1 4.0 %collective-permute-start.13 = (bf16[128,128]{1,0:T(8,128)(2,1)S(1)}, bf16[128,128]{1,0:T(8,128)(2,1)S(1)}, u32[]{:S(2)}, u32[]{:S(2)}) collective-permute-start(bf16[128,128]{1,0:T(8,128)(2,1)S(1)} %get-tuple-element.27.refs_2_.refs_8_.refs_0_), channel_id=1, source_target_pairs={{0,249},{1,248},{2,251},{3,250},{4,253},{5,252},{6,255},{7,254},{8... | collective-permute-start | bytes 98312 | tf_op jit(solution)/shard_map/ppermute | solution.py:309
  45.1 2.1 %partner_counts.1 = (f32[6,128,128]{2,1,0:T(8,128)S(1)}, f32[6,128,128]{2,1,0:T(8,128)S(1)}, f32[6,128,128]{2,1,0:T(8,128)S(1)}, f32[6,128,128]{2,1,0:T(8,128)S(1)}) custom-call(s32[7]{0:T(128)S(1)} %concatenate.13.refs_0_, s32[16,512]{1,0:T(8,128)S(1)} %collective-permute-done.10.refs_15_.refs_1_, bf16[128,128]{1,0:T(8,128)(2,1)S(1)} %get-tuple-element.27.refs_2_.refs_8_.refs_0_), custom_call_target="tpu_custom_call" | custom-call | flops 1000000000 | bytes 1048576 | tf_op jit(solution)/shard_map/partner_counts/pallas_call | solution.py:53
  47.2 2.2 %partner_0.1 = (bf16[1024,768]{1,0:T(8,128)(2,1)S(1)}, bf16[1024,768]{1,0:T(8,128)(2,1)S(1)}) custom-call(f32[3]{0:T(128)S(1)} %pad_maximum_fusion.refs_0_, bf16[4,144,128]{2,1,0:T(8,128)(2,1)S(1)} %stack_first.1.refs_1_.refs_2_.refs_0_, bf16[4,144,128]{2,1,0:T(8,128)(2,1)S(1)} %stack_first.1.refs_1_.refs_2_.refs_0_, ...), custom_call_target="tpu_custom_call" | custom-call | flops 1000000000 | bytes 1048576 | tf_op jit(solution)/shard_map/partner_0/pallas_call | solution.py:53
  50.7 1.4 %collective-permute-start.15 = (bf16[4,128,128]{2,1,0:T(8,128)(2,1)S(1)}, bf16[4,128,128]{2,1,0:T(8,128)(2,1)S(1)}, u32[]{:S(2)}, u32[]{:S(2)}) collective-permute-start(bf16[4,128,128]{2,1,0:T(8,128)(2,1)S(1)} %stack_second.1.refs_2_.refs_8_.refs_0_.refs_16_), channel_id=1, source_target_pairs={{0,4},{1,5},{2,6},{3,7},{4,0},{5,1},{6,2},{7,3},{8,12},{9,13},{10,... | collective-permute-start | bytes 393224 | tf_op jit(solution)/shard_map/ppermute | solution.py:309
  52.1 1.2 %phases_0.1.refs_7_.refs_1_.refs_3_ = bf16[2048,256]{1,0:T(8,128)(2,1)S(1)} custom-call(bf16[4,144,128]{2,1,0:T(8,128)(2,1)S(1)} %stack_first.1.refs_1_.refs_2_.refs_0_, bf16[1024,24]{1,0:T(8,128)(2,1)S(1)} %modes.1.refs_1_, bf16[4,128,128]{2,1,0:T(8,128)(2,1)S(1)} %stack_second.1.refs_2_.refs_8_.refs_0_.refs_16_), custom_call_target="tpu_custom_call" | custom-call | flops 1000000000 | bytes 1048576 | tf_op jit(solution)/shard_map/phases_0/pallas_call | solution.py:53
  53.3 4.5 %collective-permute-start.20 = (bf16[2,128,128]{2,1,0:T(8,128)(2,1)S(1)}, bf16[2,128,128]{2,1,0:T(8,128)(2,1)S(1)}, u32[]{:S(2)}, u32[]{:S(2)}) collective-permute-start(bf16[2,128,128]{2,1,0:T(8,128)(2,1)S(1)} %slice.44), channel_id=1, source_target_pairs={{0,8},{1,9},{2,10},{3,11},{4,12},{5,13},{6,14},{7,15},{8,0},{9,1},... | collective-permute-start | bytes 196616 | tf_op jit(solution)/shard_map/ppermute | solution.py:309
  59.0 2.2 %partner_2.1 = (bf16[1024,768]{1,0:T(8,128)(2,1)S(1)}, bf16[1024,768]{1,0:T(8,128)(2,1)S(1)}) custom-call(f32[3]{0:T(128)S(1)} %pad_maximum_fusion.refs_0_, bf16[4,144,128]{2,1,0:T(8,128)(2,1)S(1)} %stack_first.1.refs_1_.refs_2_.refs_0_, bf16[4,144,128]{2,1,0:T(8,128)(2,1)S(1)} %collective-permute-done.4.refs_3_.refs_2_.refs_0_, ...), custom_call_target="tpu_custom_call" | custom-call | flops 1000000000 | bytes 1048576 | tf_op jit(solution)/shard_map/partner_2/pallas_call | solution.py:53
  62.8 1.3 %second_0.1.refs_15_ = f32[2,128,128]{2,1,0:T(8,128)S(1)} custom-call(bf16[4,128,128]{2,1,0:T(8,128)(2,1)S(1)} %stack_second.1.refs_2_.refs_8_.refs_0_.refs_16_, bf16[2,128,128]{2,1,0:T(8,128)(2,1)S(1)} %collective-permute-done.20.refs_1_, bf16[1024,768]{1,0:T(8,128)(2,1)S(1)} %get-tuple-element.39.refs_2_, ...), custom_call_target="tpu_custom_call" | custom-call | flops 1000000000 | bytes 1048576 | tf_op jit(solution)/shard_map/second_0/pallas_call | solution.py:53
  64.1 3.9 %second_rest.1.refs_2_.refs_5_.refs_7_ = f32[2,16,128]{2,1,0:T(8,128)S(1)} custom-call(s32[8]{0:T(128)S(1)} %concatenate.14.refs_0_, bf16[4,128,128]{2,1,0:T(8,128)(2,1)S(1)} %collective-permute-done.14.refs_1_, bf16[4,128,128]{2,1,0:T(8,128)(2,1)S(1)} %collective-permute-done.15.refs_2_, bf16[4,128,128]{2,1,0:T(8,128)(2,1)S(1)} %collective-permute-done.16.refs_3_, ...), custom_call_target="tpu_custom_call" | custom-call | flops 1000000000 | bytes 1048576 | tf_op jit(solution)/shard_map/second_rest/pallas_call | solution.py:53
  68.0 2.3 %collective-permute-start.21 = (f32[2,16,128]{2,1,0:T(8,128)S(1)}, f32[2,16,128]{2,1,0:T(8,128)S(1)}, u32[]{:S(2)}, u32[]{:S(2)}) collective-permute-start(f32[2,16,128]{2,1,0:T(8,128)S(1)} %second_rest.1.refs_2_.refs_5_.refs_7_), channel_id=1, source_target_pairs={{0,6},{1,7},{2,0},{3,1},{4,2},{5,3},{6,4},{7,5},{8,14},{9,15},{10,... | collective-permute-start | bytes 49160 | tf_op jit(solution)/shard_map/ppermute | solution.py:309
  72.2 1.2 %phases_2.1.refs_3_.refs_5_ = bf16[2048,256]{1,0:T(8,128)(2,1)S(1)} custom-call(bf16[4,144,128]{2,1,0:T(8,128)(2,1)S(1)} %collective-permute-done.4.refs_3_.refs_2_.refs_0_, bf16[1024,24]{1,0:T(8,128)(2,1)S(1)} %modes.1.refs_1_, f32[2,16,128]{2,1,0:T(8,128)S(1)} %second_rest.1.refs_2_.refs_5_.refs_7_), custom_call_target="tpu_custom_call" | custom-call | flops 1000000000 | bytes 1048576 | tf_op jit(solution)/shard_map/phases_2/pallas_call | solution.py:53
  74.6 1.3 %structure.1 = (f32[32,512]{1,0:T(8,128)S(1)}, f32[32,512]{1,0:T(8,128)S(1)}) custom-call(s32[1]{0:T(128)} %bitcast.refs_0_, bf16[2048,256]{1,0:T(8,128)(2,1)S(1)} %phases_0.1.refs_7_.refs_1_.refs_3_, bf16[2048,256]{1,0:T(8,128)(2,1)S(1)} %phases_1.1.refs_8_.refs_2_.refs_4_, bf16[2048,256]{1,0:T(8,128)(2,1)S(1)} %phases_2.1.refs_3_.refs_5_, ...), custom_call_target="tpu_custom_call" | custom-call | flops 100000000 | bytes 1048576 | tf_op jit(solution)/shard_map/structure/pallas_call | solution.py:53
  75.9 2.1 %collective-permute-start.24 = (f32[32,512]{1,0:T(8,128)S(1)}, f32[32,512]{1,0:T(8,128)S(1)}, u32[]{:S(2)}, u32[]{:S(2)}) collective-permute-start(f32[32,512]{1,0:T(8,128)S(1)} %get-tuple-element.41), channel_id=1, source_target_pairs={{0,8},{1,9},{2,10},{3,11},{4,12},{5,13},{6,14},{7,15},{8,0},{9,1},... | collective-permute-start | bytes 196616 | tf_op jit(solution)/shard_map/ppermute | solution.py:309
  79.1 2.6 %collective-permute-start.27 = (bf16[32,512]{1,0:T(8,128)(2,1)S(1)}, bf16[32,512]{1,0:T(8,128)(2,1)S(1)}, u32[]{:S(2)}, u32[]{:S(2)}) collective-permute-start(bf16[32,512]{1,0:T(8,128)(2,1)S(1)} %get-tuple-element.42), channel_id=1, source_target_pairs={{0,192},{1,193},{2,194},{3,195},{4,196},{5,197},{6,198},{7,199},{8... | collective-permute-start | bytes 98312 | tf_op jit(solution)/shard_map/ppermute | solution.py:309
  81.7 1.3 %collective-permute-done.25 = bf16[32,512]{1,0:T(8,128)(2,1)S(1)} collective-permute-done((bf16[32,512]{1,0:T(8,128)(2,1)S(1)}, bf16[32,512]{1,0:T(8,128)(2,1)S(1)}, u32[]{:S(2)}, u32[]{:S(2)}) %collective-permute-start.25) | collective-permute-done | bytes 32800 | tf_op jit(solution)/shard_map/ppermute | solution.py:309
  84.5 3.4 %collective-permute-start.30 = (bf16[32,512]{1,0:T(8,128)(2,1)S(1)}, bf16[32,512]{1,0:T(8,128)(2,1)S(1)}, u32[]{:S(2)}, u32[]{:S(2)}) collective-permute-start(bf16[32,512]{1,0:T(8,128)(2,1)S(1)} %fusion.1), channel_id=1, source_target_pairs={{0,48},{1,49},{2,50},{3,51},{4,52},{5,53},{6,54},{7,55},{8,56},{9,... | collective-permute-start | bytes 98312 | tf_op jit(solution)/shard_map/ppermute | solution.py:309
  88.1 1.4 %collective-permute-done.30 = bf16[32,512]{1,0:T(8,128)(2,1)S(1)} collective-permute-done((bf16[32,512]{1,0:T(8,128)(2,1)S(1)}, bf16[32,512]{1,0:T(8,128)(2,1)S(1)}, u32[]{:S(2)}, u32[]{:S(2)}) %collective-permute-start.30) | collective-permute-done | bytes 32800 | tf_op jit(solution)/shard_map/ppermute | solution.py:309
  89.6 3.0 %collective-permute-start.31 = (f32[32,512]{1,0:T(8,128)S(1)}, f32[32,512]{1,0:T(8,128)S(1)}, u32[]{:S(2)}, u32[]{:S(2)}) collective-permute-start(f32[32,512]{1,0:T(8,128)S(1)} %add_add_fusion.refs_11_), channel_id=1, source_target_pairs={{0,8},{1,9},{2,10},{3,11},{4,12},{5,13},{6,14},{7,15},{8,0},{9,1},... | collective-permute-start | bytes 196616 | tf_op jit(solution)/shard_map/ppermute | solution.py:309
  93.5 1.3 %respond.1 = f32[8,24,128]{2,1,0:T(8,128)S(1)} custom-call(s32[1]{0:T(128)} %bitcast.refs_0_, s32[8]{0:T(128)S(1)} %fusion.3.refs_1_, f32[1]{0:T(128)} %constant.107.clone.1.refs_2_, bf16[2048,256]{1,0:T(8,128)(2,1)S(1)} %phases_0.1.refs_7_.refs_1_.refs_3_, bf16[2048,256]{1,0:T(8,128)(2,1)S(1)} %phases_1.1.refs_8_.refs_2_.refs_4_, ...), custom_call_target="tpu_custom_call" | custom-call | flops 100000000 | bytes 1048576 | tf_op jit(solution)/shard_map/respond/pallas_call | solution.py:53
  94.8 15.1 %all_to_all.5.refs_0_ = f32[8,24,128]{2,1,0:T(8,128)S(1)} all-to-all(f32[8,24,128]{2,1,0:T(8,128)S(1)} %respond.1), channel_id=1, replica_groups=mesh['slab'=32,'kgrp'=8] {'kgrp'}, dimensions={0} | all-to-all | bytes 196608 | tf_op jit(solution)/shard_map/all_to_all | solution.py:432
  (92 shorter events, 17.7 us)
Async XLA Ops:
  2.1 13.3 %collective-permute-start = (bf16[144,128]{1,0:T(8,128)(2,1)S(1)}, bf16[144,128]{1,0:T(8,128)(2,1)S(1)}, u32[]{:S(2)}, u32[]{:S(2)}) collective-permute-start(bf16[144,128]{1,0:T(8,128)(2,1)S(1)} %pack.1.refs_0_), channel_id=1, source_target_pairs={{0,1},{1,0},{2,3},{3,2},{4,5},{5,4},{6,7},{7,6},{8,9},{9,8},{10,11... | collective-permute-start | bytes 110600 | tf_op jit(solution)/shard_map/ppermute | solution.py:309
  9.9 5.5 %collective-permute-start.1 = (bf16[144,128]{1,0:T(8,128)(2,1)S(1)}, bf16[144,128]{1,0:T(8,128)(2,1)S(1)}, u32[]{:S(2)}, u32[]{:S(2)}) collective-permute-start(bf16[144,128]{1,0:T(8,128)(2,1)S(1)} %pack.1.refs_0_), channel_id=1, source_target_pairs={{0,248},{1,249},{2,250},{3,251},{4,252},{5,253},{6,254},{7,255},{8... | collective-permute-start | bytes 110600 | tf_op jit(solution)/shard_map/ppermute | solution.py:309
  11.5 6.5 %collective-permute-start.2 = (bf16[144,128]{1,0:T(8,128)(2,1)S(1)}, bf16[144,128]{1,0:T(8,128)(2,1)S(1)}, u32[]{:S(2)}, u32[]{:S(2)}) collective-permute-start(bf16[144,128]{1,0:T(8,128)(2,1)S(1)} %pack.1.refs_0_), channel_id=1, source_target_pairs={{0,249},{1,248},{2,251},{3,250},{4,253},{5,252},{6,255},{7,254},{8... | collective-permute-start | bytes 110600 | tf_op jit(solution)/shard_map/ppermute | solution.py:309
  18.0 10.9 %collective-permute-start.3 = (bf16[4,144,128]{2,1,0:T(8,128)(2,1)S(1)}, bf16[4,144,128]{2,1,0:T(8,128)(2,1)S(1)}, u32[]{:S(2)}, u32[]{:S(2)}) collective-permute-start(bf16[4,144,128]{2,1,0:T(8,128)(2,1)S(1)} %stack_first.1.refs_1_.refs_2_.refs_0_), channel_id=1, source_target_pairs={{0,6},{1,7},{2,0},{3,1},{4,2},{5,3},{6,4},{7,5},{8,14},{9,15},{10,... | collective-permute-start | bytes 442376 | tf_op jit(solution)/shard_map/ppermute | solution.py:309
  20.8 8.8 %collective-permute-start.4 = (bf16[4,144,128]{2,1,0:T(8,128)(2,1)S(1)}, bf16[4,144,128]{2,1,0:T(8,128)(2,1)S(1)}, u32[]{:S(2)}, u32[]{:S(2)}) collective-permute-start(bf16[4,144,128]{2,1,0:T(8,128)(2,1)S(1)} %stack_first.1.refs_1_.refs_2_.refs_0_), channel_id=1, source_target_pairs={{0,4},{1,5},{2,6},{3,7},{4,0},{5,1},{6,2},{7,3},{8,12},{9,13},{10,... | collective-permute-start | bytes 442376 | tf_op jit(solution)/shard_map/ppermute | solution.py:309
  21.2 9.9 %collective-permute-start.5 = (bf16[4,144,128]{2,1,0:T(8,128)(2,1)S(1)}, bf16[4,144,128]{2,1,0:T(8,128)(2,1)S(1)}, u32[]{:S(2)}, u32[]{:S(2)}) collective-permute-start(bf16[4,144,128]{2,1,0:T(8,128)(2,1)S(1)} %stack_first.1.refs_1_.refs_2_.refs_0_), channel_id=1, source_target_pairs={{0,2},{1,3},{2,4},{3,5},{4,6},{5,7},{6,0},{7,1},{8,10},{9,11},{10,... | collective-permute-start | bytes 442376 | tf_op jit(solution)/shard_map/ppermute | solution.py:309
  22.2 5.0 %collective-permute-start.9 = (bf16[2,144,128]{2,1,0:T(8,128)(2,1)S(1)}, bf16[2,144,128]{2,1,0:T(8,128)(2,1)S(1)}, u32[]{:S(2)}, u32[]{:S(2)}) collective-permute-start(bf16[2,144,128]{2,1,0:T(8,128)(2,1)S(1)} %slice.40), channel_id=1, source_target_pairs={{0,8},{1,9},{2,10},{3,11},{4,12},{5,13},{6,14},{7,15},{8,0},{9,1},... | collective-permute-start | bytes 221192 | tf_op jit(solution)/shard_map/ppermute | solution.py:309
  27.2 7.5 %collective-permute-start.10 = (s32[16,512]{1,0:T(8,128)S(1)}, s32[16,512]{1,0:T(8,128)S(1)}, u32[]{:S(2)}, u32[]{:S(2)}) collective-permute-start(s32[16,512]{1,0:T(8,128)S(1)} %late.1), channel_id=1, source_target_pairs={{0,1},{1,0},{2,3},{3,2},{4,5},{5,4},{6,7},{7,6},{8,9},{9,8},{10,11... | collective-permute-start | bytes 98312 | tf_op jit(solution)/shard_map/ppermute | solution.py:309
  28.9 5.9 %collective-permute-start.6 = (bf16[2,144,128]{2,1,0:T(8,128)(2,1)S(1)}, bf16[2,144,128]{2,1,0:T(8,128)(2,1)S(1)}, u32[]{:S(2)}, u32[]{:S(2)}) collective-permute-start(bf16[2,144,128]{2,1,0:T(8,128)(2,1)S(1)} %slice.37), channel_id=1, source_target_pairs={{0,8},{1,9},{2,10},{3,11},{4,12},{5,13},{6,14},{7,15},{8,0},{9,1},... | collective-permute-start | bytes 221192 | tf_op jit(solution)/shard_map/ppermute | solution.py:309
  29.6 5.2 %collective-permute-start.7 = (bf16[2,144,128]{2,1,0:T(8,128)(2,1)S(1)}, bf16[2,144,128]{2,1,0:T(8,128)(2,1)S(1)}, u32[]{:S(2)}, u32[]{:S(2)}) collective-permute-start(bf16[2,144,128]{2,1,0:T(8,128)(2,1)S(1)} %slice.38), channel_id=1, source_target_pairs={{0,8},{1,9},{2,10},{3,11},{4,12},{5,13},{6,14},{7,15},{8,0},{9,1},... | collective-permute-start | bytes 221192 | tf_op jit(solution)/shard_map/ppermute | solution.py:309
  31.1 3.7 %collective-permute-start.8 = (bf16[2,144,128]{2,1,0:T(8,128)(2,1)S(1)}, bf16[2,144,128]{2,1,0:T(8,128)(2,1)S(1)}, u32[]{:S(2)}, u32[]{:S(2)}) collective-permute-start(bf16[2,144,128]{2,1,0:T(8,128)(2,1)S(1)} %slice.39), channel_id=1, source_target_pairs={{0,8},{1,9},{2,10},{3,11},{4,12},{5,13},{6,14},{7,15},{8,0},{9,1},... | collective-permute-start | bytes 221192 | tf_op jit(solution)/shard_map/ppermute | solution.py:309
  39.1 10.3 %collective-permute-start.11 = (bf16[128,128]{1,0:T(8,128)(2,1)S(1)}, bf16[128,128]{1,0:T(8,128)(2,1)S(1)}, u32[]{:S(2)}, u32[]{:S(2)}) collective-permute-start(bf16[128,128]{1,0:T(8,128)(2,1)S(1)} %get-tuple-element.27.refs_2_.refs_8_.refs_0_), channel_id=1, source_target_pairs={{0,1},{1,0},{2,3},{3,2},{4,5},{5,4},{6,7},{7,6},{8,9},{9,8},{10,11... | collective-permute-start | bytes 98312 | tf_op jit(solution)/shard_map/ppermute | solution.py:309
  40.8 8.6 %collective-permute-start.12 = (bf16[128,128]{1,0:T(8,128)(2,1)S(1)}, bf16[128,128]{1,0:T(8,128)(2,1)S(1)}, u32[]{:S(2)}, u32[]{:S(2)}) collective-permute-start(bf16[128,128]{1,0:T(8,128)(2,1)S(1)} %get-tuple-element.27.refs_2_.refs_8_.refs_0_), channel_id=1, source_target_pairs={{0,248},{1,249},{2,250},{3,251},{4,252},{5,253},{6,254},{7,255},{8... | collective-permute-start | bytes 98312 | tf_op jit(solution)/shard_map/ppermute | solution.py:309
  41.1 8.3 %collective-permute-start.13 = (bf16[128,128]{1,0:T(8,128)(2,1)S(1)}, bf16[128,128]{1,0:T(8,128)(2,1)S(1)}, u32[]{:S(2)}, u32[]{:S(2)}) collective-permute-start(bf16[128,128]{1,0:T(8,128)(2,1)S(1)} %get-tuple-element.27.refs_2_.refs_8_.refs_0_), channel_id=1, source_target_pairs={{0,249},{1,248},{2,251},{3,250},{4,253},{5,252},{6,255},{7,254},{8... | collective-permute-start | bytes 98312 | tf_op jit(solution)/shard_map/ppermute | solution.py:309
  49.5 11.7 %collective-permute-start.14 = (bf16[4,128,128]{2,1,0:T(8,128)(2,1)S(1)}, bf16[4,128,128]{2,1,0:T(8,128)(2,1)S(1)}, u32[]{:S(2)}, u32[]{:S(2)}) collective-permute-start(bf16[4,128,128]{2,1,0:T(8,128)(2,1)S(1)} %stack_second.1.refs_2_.refs_8_.refs_0_.refs_16_), channel_id=1, source_target_pairs={{0,6},{1,7},{2,0},{3,1},{4,2},{5,3},{6,4},{7,5},{8,14},{9,15},{10,... | collective-permute-start | bytes 393224 | tf_op jit(solution)/shard_map/ppermute | solution.py:309
  50.7 10.7 %collective-permute-start.15 = (bf16[4,128,128]{2,1,0:T(8,128)(2,1)S(1)}, bf16[4,128,128]{2,1,0:T(8,128)(2,1)S(1)}, u32[]{:S(2)}, u32[]{:S(2)}) collective-permute-start(bf16[4,128,128]{2,1,0:T(8,128)(2,1)S(1)} %stack_second.1.refs_2_.refs_8_.refs_0_.refs_16_), channel_id=1, source_target_pairs={{0,4},{1,5},{2,6},{3,7},{4,0},{5,1},{6,2},{7,3},{8,12},{9,13},{10,... | collective-permute-start | bytes 393224 | tf_op jit(solution)/shard_map/ppermute | solution.py:309
  52.1 9.9 %collective-permute-start.16 = (bf16[4,128,128]{2,1,0:T(8,128)(2,1)S(1)}, bf16[4,128,128]{2,1,0:T(8,128)(2,1)S(1)}, u32[]{:S(2)}, u32[]{:S(2)}) collective-permute-start(bf16[4,128,128]{2,1,0:T(8,128)(2,1)S(1)} %stack_second.1.refs_2_.refs_8_.refs_0_.refs_16_), channel_id=1, source_target_pairs={{0,2},{1,3},{2,4},{3,5},{4,6},{5,7},{6,0},{7,1},{8,10},{9,11},{10,... | collective-permute-start | bytes 393224 | tf_op jit(solution)/shard_map/ppermute | solution.py:309
  53.3 9.4 %collective-permute-start.20 = (bf16[2,128,128]{2,1,0:T(8,128)(2,1)S(1)}, bf16[2,128,128]{2,1,0:T(8,128)(2,1)S(1)}, u32[]{:S(2)}, u32[]{:S(2)}) collective-permute-start(bf16[2,128,128]{2,1,0:T(8,128)(2,1)S(1)} %slice.44), channel_id=1, source_target_pairs={{0,8},{1,9},{2,10},{3,11},{4,12},{5,13},{6,14},{7,15},{8,0},{9,1},... | collective-permute-start | bytes 196616 | tf_op jit(solution)/shard_map/ppermute | solution.py:309
  61.3 2.8 %collective-permute-start.17 = (bf16[2,128,128]{2,1,0:T(8,128)(2,1)S(1)}, bf16[2,128,128]{2,1,0:T(8,128)(2,1)S(1)}, u32[]{:S(2)}, u32[]{:S(2)}) collective-permute-start(bf16[2,128,128]{2,1,0:T(8,128)(2,1)S(1)} %slice.41), channel_id=1, source_target_pairs={{0,8},{1,9},{2,10},{3,11},{4,12},{5,13},{6,14},{7,15},{8,0},{9,1},... | collective-permute-start | bytes 196616 | tf_op jit(solution)/shard_map/ppermute | solution.py:309
  61.4 2.7 %collective-permute-start.18 = (bf16[2,128,128]{2,1,0:T(8,128)(2,1)S(1)}, bf16[2,128,128]{2,1,0:T(8,128)(2,1)S(1)}, u32[]{:S(2)}, u32[]{:S(2)}) collective-permute-start(bf16[2,128,128]{2,1,0:T(8,128)(2,1)S(1)} %slice.42), channel_id=1, source_target_pairs={{0,8},{1,9},{2,10},{3,11},{4,12},{5,13},{6,14},{7,15},{8,0},{9,1},... | collective-permute-start | bytes 196616 | tf_op jit(solution)/shard_map/ppermute | solution.py:309
  62.0 2.1 %collective-permute-start.19 = (bf16[2,128,128]{2,1,0:T(8,128)(2,1)S(1)}, bf16[2,128,128]{2,1,0:T(8,128)(2,1)S(1)}, u32[]{:S(2)}, u32[]{:S(2)}) collective-permute-start(bf16[2,128,128]{2,1,0:T(8,128)(2,1)S(1)} %slice.43), channel_id=1, source_target_pairs={{0,8},{1,9},{2,10},{3,11},{4,12},{5,13},{6,14},{7,15},{8,0},{9,1},... | collective-permute-start | bytes 196616 | tf_op jit(solution)/shard_map/ppermute | solution.py:309
  68.0 5.4 %collective-permute-start.21 = (f32[2,16,128]{2,1,0:T(8,128)S(1)}, f32[2,16,128]{2,1,0:T(8,128)S(1)}, u32[]{:S(2)}, u32[]{:S(2)}) collective-permute-start(f32[2,16,128]{2,1,0:T(8,128)S(1)} %second_rest.1.refs_2_.refs_5_.refs_7_), channel_id=1, source_target_pairs={{0,6},{1,7},{2,0},{3,1},{4,2},{5,3},{6,4},{7,5},{8,14},{9,15},{10,... | collective-permute-start | bytes 49160 | tf_op jit(solution)/shard_map/ppermute | solution.py:309
  70.4 4.1 %collective-permute-start.22 = (f32[2,16,128]{2,1,0:T(8,128)S(1)}, f32[2,16,128]{2,1,0:T(8,128)S(1)}, u32[]{:S(2)}, u32[]{:S(2)}) collective-permute-start(f32[2,16,128]{2,1,0:T(8,128)S(1)} %second_rest.1.refs_2_.refs_5_.refs_7_), channel_id=1, source_target_pairs={{0,4},{1,5},{2,6},{3,7},{4,0},{5,1},{6,2},{7,3},{8,12},{9,13},{10,... | collective-permute-start | bytes 49160 | tf_op jit(solution)/shard_map/ppermute | solution.py:309
  70.7 3.9 %collective-permute-start.23 = (f32[2,16,128]{2,1,0:T(8,128)S(1)}, f32[2,16,128]{2,1,0:T(8,128)S(1)}, u32[]{:S(2)}, u32[]{:S(2)}) collective-permute-start(f32[2,16,128]{2,1,0:T(8,128)S(1)} %second_rest.1.refs_2_.refs_5_.refs_7_), channel_id=1, source_target_pairs={{0,2},{1,3},{2,4},{3,5},{4,6},{5,7},{6,0},{7,1},{8,10},{9,11},{10,... | collective-permute-start | bytes 49160 | tf_op jit(solution)/shard_map/ppermute | solution.py:309
  75.9 3.0 %collective-permute-start.24 = (f32[32,512]{1,0:T(8,128)S(1)}, f32[32,512]{1,0:T(8,128)S(1)}, u32[]{:S(2)}, u32[]{:S(2)}) collective-permute-start(f32[32,512]{1,0:T(8,128)S(1)} %get-tuple-element.41), channel_id=1, source_target_pairs={{0,8},{1,9},{2,10},{3,11},{4,12},{5,13},{6,14},{7,15},{8,0},{9,1},... | collective-permute-start | bytes 196616 | tf_op jit(solution)/shard_map/ppermute | solution.py:309
  79.0 4.1 %collective-permute-start.25 = (bf16[32,512]{1,0:T(8,128)(2,1)S(1)}, bf16[32,512]{1,0:T(8,128)(2,1)S(1)}, u32[]{:S(2)}, u32[]{:S(2)}) collective-permute-start(bf16[32,512]{1,0:T(8,128)(2,1)S(1)} %get-tuple-element.42), channel_id=1, source_target_pairs={{0,64},{1,65},{2,66},{3,67},{4,68},{5,69},{6,70},{7,71},{8,72},{9,... | collective-permute-start | bytes 98312 | tf_op jit(solution)/shard_map/ppermute | solution.py:309
  79.0 4.4 %collective-permute-start.26 = (bf16[32,512]{1,0:T(8,128)(2,1)S(1)}, bf16[32,512]{1,0:T(8,128)(2,1)S(1)}, u32[]{:S(2)}, u32[]{:S(2)}) collective-permute-start(bf16[32,512]{1,0:T(8,128)(2,1)S(1)} %get-tuple-element.42), channel_id=1, source_target_pairs={{0,128},{1,129},{2,130},{3,131},{4,132},{5,133},{6,134},{7,135},{8... | collective-permute-start | bytes 98312 | tf_op jit(solution)/shard_map/ppermute | solution.py:309
  79.1 5.1 %collective-permute-start.27 = (bf16[32,512]{1,0:T(8,128)(2,1)S(1)}, bf16[32,512]{1,0:T(8,128)(2,1)S(1)}, u32[]{:S(2)}, u32[]{:S(2)}) collective-permute-start(bf16[32,512]{1,0:T(8,128)(2,1)S(1)} %get-tuple-element.42), channel_id=1, source_target_pairs={{0,192},{1,193},{2,194},{3,195},{4,196},{5,197},{6,198},{7,199},{8... | collective-permute-start | bytes 98312 | tf_op jit(solution)/shard_map/ppermute | solution.py:309
  84.3 3.6 %collective-permute-start.28 = (bf16[32,512]{1,0:T(8,128)(2,1)S(1)}, bf16[32,512]{1,0:T(8,128)(2,1)S(1)}, u32[]{:S(2)}, u32[]{:S(2)}) collective-permute-start(bf16[32,512]{1,0:T(8,128)(2,1)S(1)} %fusion.1), channel_id=1, source_target_pairs={{0,16},{1,17},{2,18},{3,19},{4,20},{5,21},{6,22},{7,23},{8,24},{9,... | collective-permute-start | bytes 98312 | tf_op jit(solution)/shard_map/ppermute | solution.py:309
  84.4 3.8 %collective-permute-start.29 = (bf16[32,512]{1,0:T(8,128)(2,1)S(1)}, bf16[32,512]{1,0:T(8,128)(2,1)S(1)}, u32[]{:S(2)}, u32[]{:S(2)}) collective-permute-start(bf16[32,512]{1,0:T(8,128)(2,1)S(1)} %fusion.1), channel_id=1, source_target_pairs={{0,32},{1,33},{2,34},{3,35},{4,36},{5,37},{6,38},{7,39},{8,40},{9,... | collective-permute-start | bytes 98312 | tf_op jit(solution)/shard_map/ppermute | solution.py:309
  84.5 5.1 %collective-permute-start.30 = (bf16[32,512]{1,0:T(8,128)(2,1)S(1)}, bf16[32,512]{1,0:T(8,128)(2,1)S(1)}, u32[]{:S(2)}, u32[]{:S(2)}) collective-permute-start(bf16[32,512]{1,0:T(8,128)(2,1)S(1)} %fusion.1), channel_id=1, source_target_pairs={{0,48},{1,49},{2,50},{3,51},{4,52},{5,53},{6,54},{7,55},{8,56},{9,... | collective-permute-start | bytes 98312 | tf_op jit(solution)/shard_map/ppermute | solution.py:309
  89.6 3.9 %collective-permute-start.31 = (f32[32,512]{1,0:T(8,128)S(1)}, f32[32,512]{1,0:T(8,128)S(1)}, u32[]{:S(2)}, u32[]{:S(2)}) collective-permute-start(f32[32,512]{1,0:T(8,128)S(1)} %add_add_fusion.refs_11_), channel_id=1, source_target_pairs={{0,8},{1,9},{2,10},{3,11},{4,12},{5,13},{6,14},{7,15},{8,0},{9,1},... | collective-permute-start | bytes 196616 | tf_op jit(solution)/shard_map/ppermute | solution.py:309
  (8 other events, 60.8 us)
where the time goes:
time: 111 us
  starting transfers between devices  51.7 us (47%)
  Pallas kernels  28.4 us (26%)
  blocking collectives  15.1 us (14%)
  waiting for transfers between devices  10.7 us (10%)
  local copies, waits for them, and re-layouts  2.56 us (2%)
    ppermute x32, starting transfers between devices, move(): return lax.ppermute(x, AXES, pairs(lax.axis_size('slab'), target))  51.7 us
    pallas_call x20, Pallas kernels, call(): pl.pallas_call(lambda *refs: body(*refs[:n], *refs[n + m:]), out_shape=ou...  28.4 us
    all_to_all x1, blocking collectives, shards(): partial = lax.all_to_all(partial, 'kgrp', 0, 0)  15.1 us
    ppermute x32, waiting for transfers between devices, move(): return lax.ppermute(x, AXES, pairs(lax.axis_size('slab'), target))  10.7 us
  transfers between devices with their start and end apart: 32, of which 11 were waited for; matrix products, arithmetic and copies ran while one was open for 2% of the time, Pallas kernels for 15%

commit v1 on v0

--- a/solution.py
+++ b/solution.py
@@ -1,3 +1,4 @@
+import functools
 import math
 
 import jax
@@ -15,6 +16,9 @@
 ROWS = 128
 PAYLOAD = 144
 HALF = 64
+WIDE = PAYLOAD + 128
+
+Y, ZH, ODD, F_PREV, F_OWN, F_NEXT, BASE, BASE_PARTNER, PLACE = 0, 1, 2, 3, 4, 5, 6, 7, 8
 
 CENTRE = 3.04
 SINC = (0.4531433647, -0.11001027431, 0.0067080034928, -0.00018563842882, 2.9260279482e-06)
@@ -48,7 +52,7 @@
     return jnp.dot(a, b, preferred_element_type=F32)
 
 
-def call(body, out_shape, *operands, scalars=(), after=(), name, flops=0, limit=12, scratch=()):
+def call(body, out_shape, *operands, scalars=(), after=(), name, flops=0, limit=12, scratch=(), **kw):
     n, m = len(scalars) + len(operands), len(after)
     return pl.pallas_call(
         lambda *refs: body(*refs[:n], *refs[n + m :]),
@@ -60,14 +64,44 @@
         name=name,
         cost_estimate=pl.CostEstimate(flops=flops, bytes_accessed=MIB, transcendentals=0),
         compiler_params=pltpu.CompilerParams(vmem_limit_bytes=limit * MIB),
+        **kw,
     )(*scalars, *operands, *after)
 
 
-def pack_body(desc_ref, loc_ref, out_ref):
-    out_ref[0:ROWS, :] = desc_ref[...]
+def pack_body(desc_ref, loc_ref, slots_ref, tally_ref, out_ref, wide_ref):
     hi, mid, lo = [p.astype(F32) for p in split(loc_ref[...], 3)]
-    tail = jnp.concatenate([hi, mid, lo, jnp.zeros((7, ROWS), F32)], axis=0)
-    out_ref[ROWS:PAYLOAD, :] = tail.astype(BF16)
+    tail = jnp.concatenate([hi, mid, lo, jnp.zeros((7, ROWS), F32)], axis=0).astype(BF16)
+    for ref in (out_ref, wide_ref):
+        ref[0:ROWS, :] = desc_ref[...]
+        ref[ROWS:PAYLOAD, :] = tail
+    slots = slots_ref[...]
+    used = lax.broadcasted_iota(jnp.int32, slots.shape, 0) < tally_ref[...]
+    wide_ref[PAYLOAD : PAYLOAD + 64, :] = jnp.where(used, slots >> 7, -1).astype(F32).astype(BF16)
+    wide_ref[PAYLOAD + 64 : WIDE, :] = (slots & 127).astype(F32).astype(BF16)
+
+
+def layout_body(where_ref, filled_ref, scal_ref, shift_ref, odd_ref):
+    slab, group = where_ref[0], where_ref[1]
+    n_slab = filled_ref.shape[0]
+    y, zh, odd = group >> 1, group & 1, slab & 1
+    before = jnp.where(slab == 0, n_slab - 1, slab - 1)
+    behind = jnp.where(slab == n_slab - 1, 0, slab + 1)
+    scal_ref[Y] = y
+    scal_ref[ZH] = zh
+    scal_ref[ODD] = odd
+    scal_ref[F_PREV] = filled_ref[before]
+    scal_ref[F_OWN] = filled_ref[slab]
+    scal_ref[F_NEXT] = filled_ref[behind]
+    scal_ref[BASE] = group * ROWS
+    scal_ref[BASE_PARTNER] = (group ^ 1) * ROWS
+    for i in range(8):
+        scal_ref[PLACE + i] = (((y + i // 2) & 3) << 1) | ((i % 2) ^ zh)
+    low_edge = jnp.where(slab == 0, -float(n_slab), 0.0)
+    high_edge = jnp.where(slab == n_slab - 1, float(n_slab), 0.0)
+    shift_ref[0] = 0.0
+    shift_ref[1] = jnp.where(odd == 1, high_edge, low_edge)
+    shift_ref[2] = jnp.where(odd == 1, low_edge, high_edge)
+    odd_ref[...] = jnp.full((1, 512), odd, jnp.int32)
 
 
 def coordinates(payload):
@@ -75,36 +109,35 @@
     return (tail[0:3] + tail[3:6]) + tail[6:9]
 
 
-def count_body(scal_ref, slots_ref, cnt0, cnt1, cnt2, cnt3, target_s, low_s):
-    y, zh, odd = scal_ref[0], scal_ref[1], scal_ref[2]
-    f_prev, f_own, f_next, base = scal_ref[3], scal_ref[4], scal_ref[5], scal_ref[6]
-    slots = slots_ref[...]
-    shape = slots.shape
-    lane = lax.broadcasted_iota(jnp.int32, shape, 1)
-    row = lax.broadcasted_iota(jnp.int32, shape, 0)
-    local = lane >> 6
-    atom = row * 8 + local + base
-    region = slots >> 10
-    within = slots & 1023
+def count_body(which, scal_ref, wide_ref, cnt0, cnt1, cnt2, cnt3):
+    y, zh, odd = scal_ref[Y], scal_ref[ZH], scal_ref[ODD]
+    f_prev, f_own, f_next, base = scal_ref[F_PREV], scal_ref[F_OWN], scal_ref[F_NEXT], scal_ref[which]
+
+    def paired(rows):
+        t = rows.astype(F32).T
+        return jnp.concatenate([t[0:64], t[64:128]], axis=1).astype(jnp.int32)
+
+    blocks = paired(wide_ref[PAYLOAD : PAYLOAD + 64, :])
+    low = paired(wide_ref[PAYLOAD + 64 : WIDE, :])
+    lane = lax.broadcasted_iota(jnp.int32, blocks.shape, 1)
+    row = lax.broadcasted_iota(jnp.int32, blocks.shape, 0)
+    second = lane >> 6
+    region = blocks >> 3
+    kblock = blocks & 7
     filled = jnp.where(region == 0, f_prev, jnp.where(region == 1, f_own, f_next))
-    usable = (slots >= 0) & (within < filled) & (atom < f_own)
-    kblock = within >> 7
+    usable = (blocks >= 0) & (kblock * 128 + low < filled) & (base + row + 64 * second < f_own)
     place = jnp.where(region == 1, 0, jnp.where(region == 2 * odd, 2, 4)) + ((kblock & 1) ^ zh)
-    target = jnp.where(usable, ((((kblock >> 1) - y) & 3) * 6 + place) * 8 + local, -1)
-    target_s[...] = target
-    low_s[...] = slots & 127
+    target = jnp.where(usable, ((((kblock >> 1) - y) & 3) * 6 + place) * 8 + (row & 3) + 4 * second, -1)
     iota_p = lax.broadcasted_iota(jnp.int32, (192, 512), 0)
     iota_l = lax.broadcasted_iota(jnp.int32, (128, 512), 0)
-
-    @pl.loop(0, 4)
-    def _(step):
-        for u in range(4):
-            i = step * 4 + u
-            p = jnp.where(iota_p == target_s[pl.ds(i, 1), :], 1.0, 0.0).astype(BF16)
-            l = jnp.where(iota_l == low_s[pl.ds(i, 1), :], 1.0, 0.0).astype(BF16)
-            c = nt(p, l).reshape(24, 8, 128)
-            for j, cnt_ref in enumerate((cnt0, cnt1, cnt2, cnt3)):
-                cnt_ref[:, pl.ds(pl.multiple_of(8 * i, 8), 8), :] = c[6 * j : 6 * j + 6]
+    for i in range(16):
+        line = lambda x: jnp.concatenate([x[4 * i + q : 4 * i + q + 1] for q in range(4)], axis=1)
+        p = jnp.where(iota_p == line(target), 1.0, 0.0).astype(BF16)
+        l = jnp.where(iota_l == line(low), 1.0, 0.0).astype(BF16)
+        c = nt(p, l).reshape(24, 8, 128)
+        for j, cnt_ref in enumerate((cnt0, cnt1, cnt2, cnt3)):
+            cnt_ref[:, 4 * i : 4 * i + 4, :] = c[6 * j : 6 * j + 6, 0:4]
+            cnt_ref[:, 64 + 4 * i : 68 + 4 * i, :] = c[6 * j : 6 * j + 6, 4:8]
 
 
 def update(gathered, hidden, self_weight):
@@ -219,17 +252,17 @@
     for z in range(2):
         hidden = update(part_ref[z] + total_s[z], near_ref[z], node_ref[1])
         charges = nt(readout_ref[...], hidden)
-        atom = lax.broadcasted_iota(jnp.int32, charges.shape, 1) + scal_ref[6 + z]
-        charge_ref[z] = jnp.where(atom < scal_ref[4], charges, 0.0)
-
-
-def copy_body(in_ref, out_ref):
-    out_ref[...] = in_ref[...]
+        atom = lax.broadcasted_iota(jnp.int32, charges.shape, 1) + scal_ref[BASE + z]
+        charge_ref[z] = jnp.where(atom < scal_ref[F_OWN], charges, 0.0)
+
+
+def pair_body(in_ref, out_ref):
+    out_ref[...] = in_ref[0:2]
 
 
 def stack_body(a, b, c, d, out_ref):
     for i, ref in enumerate((a, b, c, d)):
-        out_ref[i] = ref[...]
+        out_ref[i] = ref[0 : out_ref.shape[1], :]
 
 
 def cross(pieces, left):
@@ -257,27 +290,27 @@
             wave_ref[r + 1024 : r + 1088, columns] = (rest * horner(SINTURN, square)).astype(BF16)
 
 
-def half_of(ref, half, sine):
-    return ref[pl.ds(pl.multiple_of(half * 512 + sine * 1024, 512), 512), :]
-
-
-def structure_body(half_ref, w0, w1, w2, w3, q0, q1, q2, q3, mine_ref, theirs_ref):
+def structure_body(odd_ref, w0, w1, w2, w3, q0, q1, q2, q3, mine_ref, theirs_ref):
     pieces = [jnp.concatenate(split(jnp.concatenate([q[0], q[1]], axis=1), 3), axis=0) for q in (q0, q1, q2, q3)]
-    for half, out_ref in ((1 - half_ref[0], theirs_ref), (half_ref[0], mine_ref)):
-        for i in range(2):
+    odd = odd_ref[...] == 1
+    for i in range(2):
+        halves = []
+        for r in (i * 1024, i * 1024 + 512):
             s = None
             for p, w in zip(pieces, (w0, w1, w2, w3)):
-                term = nt(p, half_of(w, half, i))
+                term = nt(p, w[r : r + 512, :])
                 s = term if s is None else s + term
-            out_ref[16 * i : 16 * i + 16, :] = s[0:16] + s[16:32] + s[32:48]
-
-
-def respond_body(half_ref, place_ref, scale_ref, w0, w1, w2, w3, q0, q1, q2, q3, mine_ref, theirs_ref, modes_ref, out_ref):
+            halves.append(s[0:16] + s[16:32] + s[32:48])
+        mine_ref[16 * i : 16 * i + 16, :] = jnp.where(odd, halves[1], halves[0])
+        theirs_ref[16 * i : 16 * i + 16, :] = jnp.where(odd, halves[0], halves[1])
+
+
+def respond_body(scale, scal_ref, w0, w1, w2, w3, q0, q1, q2, q3, mine_ref, theirs_ref, modes_ref, out_ref):
     k = modes_ref[...]
     square = k[0:1] * k[0:1] + k[1:2] * k[1:2] + k[2:3] * k[2:3]
-    weight = scale_ref[0] * jnp.exp(square * -0.125) / (square + 1.0)
-    low = jnp.where(half_ref[0] == 0, mine_ref[...], theirs_ref[...])
-    high = jnp.where(half_ref[0] == 0, theirs_ref[...], mine_ref[...])
+    weight = scale * jnp.exp(square * -0.125) / (square + 1.0)
+    low = jnp.where(scal_ref[ODD] == 0, mine_ref[...], theirs_ref[...])
+    high = jnp.where(scal_ref[ODD] == 0, theirs_ref[...], mine_ref[...])
     total = jnp.concatenate([low, high], axis=1) * weight
     real, imag = total[0:16], total[16:32]
     left = [real] + [imag * k[j : j + 1] for j in range(3)]
@@ -290,7 +323,7 @@
         for b in range(2):
             mine = out[:, b * 128 : (b + 1) * 128]
             force = [-jnp.sum(mine[16 * j + 16 : 16 * j + 32] * q[b], axis=0, keepdims=True) for j in range(3)]
-            out_ref[place_ref[2 * i + b]] = jnp.concatenate([mine[0:16]] + force + [jnp.zeros((5, 128), F32)], axis=0)
+            out_ref[scal_ref[PLACE + 2 * i + b]] = jnp.concatenate([mine[0:16]] + force + [jnp.zeros((5, 128), F32)], axis=0)
 
 
 def finish_body(parts_ref, potential_ref, forces_ref):
@@ -313,19 +346,25 @@
     return s + 1 if s % 2 else s - 1
 
 
-def near_blocks(block):
-    half = move(block, lambda s, k: (s, k ^ 1))
+def near_blocks(block, wide):
+    half = move(wide, lambda s, k: (s, k ^ 1))
     near = move(block, lambda s, k: (over_chip(s), k))
     both = move(block, lambda s, k: (over_chip(s), k ^ 1))
     return half, near, both
 
 
-def surroundings(block, near, name, after):
+def along_y(block, near, name, after):
     stack = call(stack_body, jax.ShapeDtypeStruct((4,) + block.shape, BF16), block, *near, name=name, after=after)
-    ys = [stack]
-    for j in range(1, 4):
-        ys.append(move(stack, lambda s, k: (s, (k - 2 * j) % 8)))
-    return ys, [move(y[0:2], lambda s, k: (s ^ 1, k)) for y in ys]
+    return [stack] + [move(stack, lambda s, k, j=j: (s, (k - 2 * j) % 8)) for j in range(1, 4)]
+
+
+def other_core(y):
+    return move(y[0:2], lambda s, k: (s ^ 1, k))
+
+
+def other_core_after(y, name, after):
+    pair = call(pair_body, jax.ShapeDtypeStruct((2,) + y.shape[1:], BF16), y, name=name, after=after)
+    return move(pair, lambda s, k: (s ^ 1, k))
 
 
 def shards(
@@ -341,35 +380,28 @@
     latent_ionic_readout,
 ):
     n_slab = lax.axis_size("slab")
-    slab = lax.axis_index("slab")
-    group = lax.axis_index("kgrp")
-    odd = slab % 2
-    y, zh = group // 2, group % 2
-    filled = jnp.take(filled_slot_tallies, (slab + jnp.arange(3) - 1) % n_slab)
-    scal = jnp.concatenate([jnp.stack([y, zh, odd]), filled, jnp.stack([group * ROWS, (group ^ 1) * ROWS])]).astype(jnp.int32)
-    low_edge = jnp.where(slab == 0, -float(n_slab), 0.0)
-    high_edge = jnp.where(slab == n_slab - 1, float(n_slab), 0.0)
-    shift = jnp.stack([0.0, jnp.where(odd == 1, high_edge, low_edge), jnp.where(odd == 1, low_edge, high_edge)]).astype(F32)
-    spots = jnp.arange(8, dtype=jnp.int32)
-    place = (((y + spots // 2) % 4) * 2 + ((spots % 2) ^ zh)).astype(jnp.int32)
-
     shape = jax.ShapeDtypeStruct
-    block = call(pack_body, shape((PAYLOAD, ROWS), BF16), atom_descriptors, atom_locations, name="pack")
-    near = near_blocks(block)
-    used = jnp.arange(64, dtype=jnp.int32)[None, :] < neighbour_tally[:, None]
-    slots = jnp.where(used, adjacent_atom_slots, -1).reshape(16, 512)
-
-    def count(slots, base, name, after=()):
-        bounds = jnp.concatenate([scal[:6], scal[base : base + 1]])
+    where = jnp.stack([lax.axis_index("slab"), lax.axis_index("kgrp")]).astype(jnp.int32)
+    block, with_slots = call(
+        pack_body, (shape((PAYLOAD, ROWS), BF16), shape((WIDE, ROWS), BF16)),
+        atom_descriptors, atom_locations, adjacent_atom_slots.T, neighbour_tally.reshape(1, ROWS), name="pack",
+    )
+    near = near_blocks(block, with_slots)
+    smem = pl.BlockSpec(memory_space=pltpu.SMEM)
+    scal, shift, odd = call(
+        layout_body, (shape((16,), jnp.int32), shape((3,), F32), shape((1, 512), jnp.int32)),
+        scalars=(where, filled_slot_tallies), name="layout", out_specs=(smem, smem, pl.BlockSpec(memory_space=pltpu.VMEM)),
+    )
+
+    def count(source, which, name):
         return call(
-            count_body, [shape((6, ROWS, 128), F32)] * 4, slots, scalars=(bounds,), name=name, flops=10**9, after=after,
-            scratch=[pltpu.VMEM((16, 512), jnp.int32)] * 2,
+            functools.partial(count_body, which), [shape((6, ROWS, 128), F32)] * 4, source, scalars=(scal,), name=name, flops=10**9
         )
 
-    counts = count(slots, 6, "counts")
-    ys, cs = surroundings(block, near, "stack_first", (counts[0],))
-    late = call(copy_body, shape((16, 512), jnp.int32), slots, name="late", after=(cs[0],))
-    partner_slots = move(late, lambda s, k: (s, k ^ 1))
+    counts = count(with_slots, BASE, "counts")
+    ys = along_y(block, near, "stack_first", (counts[0],))
+    cs = [other_core(ys[0])]
+    partner_counts = count(near[0], BASE_PARTNER, "partner_counts")
     wide = shape((8 * ROWS, 6 * ROWS), BF16)
     here = pltpu.VMEM((3, ROWS, 128), F32)
     message = lambda *n: pltpu.VMEM(n + (6 * ROWS, 128), BF16)
@@ -379,12 +411,12 @@
         ys[0], cs[0], counts[0], edge_update_matrix, distance_basis_mixing,
         scalars=(shift,), name="first_0", flops=10**9, scratch=[here, message()],
     )
+    cs += [other_core_after(ys[1], "pair_first", (part, partner_counts[0])), other_core(ys[2]), other_core(ys[3])]
     basis[1], basis[2], basis[3], hidden = call(
         first_rest_body, (wide, wide, wide, shape((ROWS, 128), BF16)),
         *ys, *cs[1:], *counts[1:], edge_update_matrix, distance_basis_mixing, part, node_update_matrix,
-        scalars=(shift,), name="first_rest", flops=10**9, scratch=[here, message(3), pltpu.VMEM((ROWS, 128), F32)], after=(partner_slots,),
-    )
-    partner_counts = count(partner_slots, 7, "partner_counts", (hidden,))
+        scalars=(shift,), name="first_rest", flops=10**9, scratch=[here, message(3), pltpu.VMEM((ROWS, 128), F32)],
+    )
     turns = call(modes_body, shape((1024, 24), BF16), reciprocal_lattice_modes, name="modes")
 
     def phases(j, after):
@@ -396,16 +428,19 @@
             scalars=(shift,), name=f"partner_{a}", flops=10**9, scratch=[here], after=after,
         )
 
-    near = near_blocks(hidden)
+    near = near_blocks(hidden, hidden)
     partner = [*partner_basis(0, 1, (hidden,))]
-    ms, ns = surroundings(hidden, near, "stack_second", partner[:1])
+    waves = [phases(0, (hidden,))]
+    ms = along_y(hidden, near, "stack_second", (partner[0], waves[0]))
+    ns = [other_core(ms[0])]
     partner += [*partner_basis(2, 3, (ms[0],))]
-    waves = [phases(j, (ms[0],)) for j in range(2)]
+    waves += [phases(1, (ms[0],))]
     part = call(
         second_body, shape((2, ROWS, 128), F32),
         ms[0], ns[0], basis[0], partner[0], edge_update_matrix, distance_basis_mixing,
-        name="second_0", flops=10**9, scratch=[message()], after=[partner[2], *waves],
-    )
+        name="second_0", flops=10**9, scratch=[message()],
+    )
+    ns += [other_core_after(ms[1], "pair_second", (part, partner[2], *waves)), other_core(ms[2]), other_core(ms[3])]
     charges = call(
         second_rest_body, shape((2, 16, ROWS), F32),
         *ms[1:], *ns[1:], *basis[1:], *partner[1:], edge_update_matrix, distance_basis_mixing, part, ms[0], node_update_matrix, latent_ionic_readout.T,
@@ -413,10 +448,9 @@
     )
     qs = [charges] + [move(charges, lambda s, k, j=j: (s, (k - 2 * j) % 8)) for j in range(1, 4)]
     waves += [phases(j, (charges,)) for j in range(2, 4)]
-    mine = jnp.reshape(odd, (1,)).astype(jnp.int32)
     part, away = call(
-        structure_body, (shape((32, 512), F32), shape((32, 512), F32)), *waves, *qs,
-        scalars=(mine,), name="structure", flops=10**8,
+        structure_body, (shape((32, 512), F32), shape((32, 512), F32)), odd, *waves, *qs,
+        name="structure", flops=10**8,
     )
     part = part + move(away, lambda s, k: (s ^ 1, k))
     half = part.astype(BF16)
@@ -424,10 +458,10 @@
     half = part.astype(BF16)
     part = part + sum(move(half, lambda s, k, m=m: (s ^ (2 * m), k)).astype(F32) for m in (1, 2, 3))
     other = move(part, lambda s, k: (s ^ 1, k))
-    scale = jnp.full((1,), 4.0 / math.sqrt(n_slab * 1024 * reciprocal_lattice_modes.shape[1] * 8), F32)
+    scale = 4.0 / math.sqrt(n_slab * 1024 * reciprocal_lattice_modes.shape[1] * 8)
     partial = call(
-        respond_body, shape((8, 24, ROWS), F32), *waves, *qs, part, other, reciprocal_lattice_modes,
-        scalars=(mine, place, scale), name="respond", flops=10**8,
+        functools.partial(respond_body, scale), shape((8, 24, ROWS), F32), *waves, *qs, part, other, reciprocal_lattice_modes,
+        scalars=(scal,), name="respond", flops=10**8,
     )
     partial = lax.all_to_all(partial, "kgrp", 0, 0)
     return tuple(call(finish_body, (shape((16, ROWS), F32), shape((3, ROWS), F32)), partial, name="finish"))

time: 111 us -> 109 us (0.982)
  starting transfers between devices: 51.7 us -> 47.4 us
  waiting for transfers between devices: 10.7 us -> 13.4 us
    ppermute x32 -> x31, starting transfers between devices: 51.7 us -> 47.4 us  [move(): return lax.ppermute(x, AXES, pairs(lax.axis_size('slab'), target))]
    ppermute x32 -> x31, waiting for transfers between devices: 10.7 us -> 13.4 us  [move(): return lax.ppermute(x, AXES, pairs(lax.axis_size('slab'), target))]
    unnamed x16 -> x20, local copies, waits for them, and re-layouts: 1.47 us -> 3.53 us
    pallas_call x20 -> x22, Pallas kernels: 28.4 us -> 28.8 us  [call(): pl.pallas_call(lambda *refs: body(*refs[:n], *refs[n + m:]), out_shape=ou...]
  transfers between devices with their start and end apart: 32 -> 31, of which waited for: 11 -> 12; matrix products, arithmetic and copies ran while one was open for 2% -> 0% of each run, Pallas kernels for 15% -> 16%
where the time goes in v1:
time: 109 us
  starting transfers between devices  47.4 us (43%)
  Pallas kernels  28.8 us (26%)
  blocking collectives  14.5 us (13%)
  waiting for transfers between devices  13.4 us (12%)
  local copies, waits for them, and re-layouts  3.56 us (3%)
    ppermute x31, starting transfers between devices, move(): return lax.ppermute(x, AXES, pairs(lax.axis_size('slab'), target))  47.4 us
    pallas_call x22, Pallas kernels, call(): pl.pallas_call(lambda *refs: body(*refs[:n], *refs[n + m:]), out_shape=ou...  28.8 us
    all_to_all x1, blocking collectives, shards(): partial = lax.all_to_all(partial, 'kgrp', 0, 0)  14.5 us
    ppermute x31, waiting for transfers between devices, move(): return lax.ppermute(x, AXES, pairs(lax.axis_size('slab'), target))  13.4 us
    unnamed x20, local copies, waits for them, and re-layouts  3.53 us
  transfers between devices with their start and end apart: 31, of which 12 were waited for; matrix products, arithmetic and copies ran while one was open for 0% of the time, Pallas kernels for 16%

profile of v1, /device:TPU:1, one launch (start us, length us, event | category | flops | bytes accessed | tf_op | source)
XLA Modules:
  0.0 108.8 jit_solution(8720676156802408011)
XLA Ops:
  3.5 3.1 %collective-permute-start.1 = (bf16[144,128]{1,0:T(8,128)(2,1)S(1)}, bf16[144,128]{1,0:T(8,128)(2,1)S(1)}, u32[]{:S(2)}, u32[]{:S(2)}) collective-permute-start(bf16[144,128]{1,0:T(8,128)(2,1)S(1)} %get-tuple-element.28.refs_0_), channel_id=1, source_target_pairs={{0,248},{1,249},{2,250},{3,251},{4,252},{5,253},{6,254},{7,255},{8... | collective-permute-start | bytes 110600 | tf_op jit(solution)/shard_map/ppermute | solution.py:342
  6.6 5.3 %collective-permute-start.2 = (bf16[144,128]{1,0:T(8,128)(2,1)S(1)}, bf16[144,128]{1,0:T(8,128)(2,1)S(1)}, u32[]{:S(2)}, u32[]{:S(2)}) collective-permute-start(bf16[144,128]{1,0:T(8,128)(2,1)S(1)} %get-tuple-element.28.refs_0_), channel_id=1, source_target_pairs={{0,249},{1,248},{2,251},{3,250},{4,253},{5,252},{6,255},{7,254},{8... | collective-permute-start | bytes 110600 | tf_op jit(solution)/shard_map/ppermute | solution.py:342
  14.5 1.7 %counts.1 = (f32[6,128,128]{2,1,0:T(8,128)S(1)}, f32[6,128,128]{2,1,0:T(8,128)S(1)}, f32[6,128,128]{2,1,0:T(8,128)S(1)}, f32[6,128,128]{2,1,0:T(8,128)S(1)}) custom-call(s32[16]{0:T(128)S(1)} %get-tuple-element.27.refs_0_, bf16[272,128]{1,0:T(8,128)(2,1)S(1)} %get-tuple-element.29.refs_1_), custom_call_target="tpu_custom_call" | custom-call | flops 1000000000 | bytes 1048576 | tf_op jit(solution)/shard_map/counts/pallas_call | solution.py:57
  16.3 3.2 %collective-permute-done.refs_1_ = bf16[272,128]{1,0:T(8,128)(2,1)S(1)} collective-permute-done((bf16[272,128]{1,0:T(8,128)(2,1)S(1)}, bf16[272,128]{1,0:T(8,128)(2,1)S(1)}, u32[]{:S(2)}, u32[]{:S(2)}) %collective-permute-start) | collective-permute-done | bytes 69664 | tf_op jit(solution)/shard_map/ppermute | solution.py:342
  19.5 2.8 %collective-permute-start.3 = (bf16[4,144,128]{2,1,0:T(8,128)(2,1)S(1)}, bf16[4,144,128]{2,1,0:T(8,128)(2,1)S(1)}, u32[]{:S(2)}, u32[]{:S(2)}) collective-permute-start(bf16[4,144,128]{2,1,0:T(8,128)(2,1)S(1)} %stack_first.1.refs_1_.refs_0_.refs_2_), channel_id=1, source_target_pairs={{0,6},{1,7},{2,0},{3,1},{4,2},{5,3},{6,4},{7,5},{8,14},{9,15},{10,... | collective-permute-start | bytes 442376 | tf_op jit(solution)/shard_map/ppermute | solution.py:342
  23.4 4.3 %collective-permute-start.6 = (bf16[2,144,128]{2,1,0:T(8,128)(2,1)S(1)}, bf16[2,144,128]{2,1,0:T(8,128)(2,1)S(1)}, u32[]{:S(2)}, u32[]{:S(2)}) collective-permute-start(bf16[2,144,128]{2,1,0:T(8,128)(2,1)S(1)} %slice.24), channel_id=1, source_target_pairs={{0,8},{1,9},{2,10},{3,11},{4,12},{5,13},{6,14},{7,15},{8,0},{9,1},... | collective-permute-start | bytes 221192 | tf_op jit(solution)/shard_map/ppermute | solution.py:342
  27.7 1.7 %partner_counts.1 = (f32[6,128,128]{2,1,0:T(8,128)S(1)}, f32[6,128,128]{2,1,0:T(8,128)S(1)}, f32[6,128,128]{2,1,0:T(8,128)S(1)}, f32[6,128,128]{2,1,0:T(8,128)S(1)}) custom-call(s32[16]{0:T(128)S(1)} %get-tuple-element.27.refs_0_, bf16[272,128]{1,0:T(8,128)(2,1)S(1)} %collective-permute-done.refs_1_), custom_call_target="tpu_custom_call" | custom-call | flops 1000000000 | bytes 1048576 | tf_op jit(solution)/shard_map/partner_counts/pallas_call | solution.py:57
  29.5 2.1 %first_0.1 = (bf16[1024,768]{1,0:T(8,128)(2,1)S(1)}, f32[128,128]{1,0:T(8,128)S(1)}) custom-call(f32[3]{0:T(128)S(1)} %get-tuple-element.31.refs_0_, bf16[4,144,128]{2,1,0:T(8,128)(2,1)S(1)} %stack_first.1.refs_1_.refs_0_.refs_2_, bf16[2,144,128]{2,1,0:T(8,128)(2,1)S(1)} %collective-permute-done.6.refs_2_.refs_4_, ...), custom_call_target="tpu_custom_call" | custom-call | flops 1000000000 | bytes 1048576 | tf_op jit(solution)/shard_map/first_0/pallas_call | solution.py:57
  32.8 1.5 %collective-permute-start.9 = (bf16[2,144,128]{2,1,0:T(8,128)(2,1)S(1)}, bf16[2,144,128]{2,1,0:T(8,128)(2,1)S(1)}, u32[]{:S(2)}, u32[]{:S(2)}) collective-permute-start(bf16[2,144,128]{2,1,0:T(8,128)(2,1)S(1)} %slice.26), channel_id=1, source_target_pairs={{0,8},{1,9},{2,10},{3,11},{4,12},{5,13},{6,14},{7,15},{8,0},{9,1},... | collective-permute-start | bytes 221192 | tf_op jit(solution)/shard_map/ppermute | solution.py:342
  35.2 4.3 %first_rest.1 = (bf16[1024,768]{1,0:T(8,128)(2,1)S(1)}, bf16[1024,768]{1,0:T(8,128)(2,1)S(1)}, bf16[1024,768]{1,0:T(8,128)(2,1)S(1)}, bf16[128,128]{1,0:T(8,128)(2,1)S(1)}) custom-call(f32[3]{0:T(128)S(1)} %get-tuple-element.31.refs_0_, bf16[4,144,128]{2,1,0:T(8,128)(2,1)S(1)} %stack_first.1.refs_1_.refs_0_.refs_2_, ...), custom_call_target="tpu_custom_call" | custom-call | flops 1000000000 | bytes 1048576 | tf_op jit(solution)/shard_map/first_rest/pallas_call | solution.py:57
  39.4 2.4 %collective-permute-start.10 = (bf16[128,128]{1,0:T(8,128)(2,1)S(1)}, bf16[128,128]{1,0:T(8,128)(2,1)S(1)}, u32[]{:S(2)}, u32[]{:S(2)}) collective-permute-start(bf16[128,128]{1,0:T(8,128)(2,1)S(1)} %get-tuple-element.37.refs_2_.refs_8_.refs_0_), channel_id=1, source_target_pairs={{0,1},{1,0},{2,3},{3,2},{4,5},{5,4},{6,7},{7,6},{8,9},{9,8},{10,11... | collective-permute-start | bytes 98312 | tf_op jit(solution)/shard_map/ppermute | solution.py:342
  41.8 3.6 %collective-permute-start.12 = (bf16[128,128]{1,0:T(8,128)(2,1)S(1)}, bf16[128,128]{1,0:T(8,128)(2,1)S(1)}, u32[]{:S(2)}, u32[]{:S(2)}) collective-permute-start(bf16[128,128]{1,0:T(8,128)(2,1)S(1)} %get-tuple-element.37.refs_2_.refs_8_.refs_0_), channel_id=1, source_target_pairs={{0,249},{1,248},{2,251},{3,250},{4,253},{5,252},{6,255},{7,254},{8... | collective-permute-start | bytes 98312 | tf_op jit(solution)/shard_map/ppermute | solution.py:342
  45.5 1.2 %phases_0.1.refs_5_.refs_3_.refs_1_ = bf16[2048,256]{1,0:T(8,128)(2,1)S(1)} custom-call(bf16[4,144,128]{2,1,0:T(8,128)(2,1)S(1)} %stack_first.1.refs_1_.refs_0_.refs_2_, bf16[1024,24]{1,0:T(8,128)(2,1)S(1)} %modes.1.refs_1_, bf16[128,128]{1,0:T(8,128)(2,1)S(1)} %get-tuple-element.37.refs_2_.refs_8_.refs_0_), custom_call_target="tpu_custom_call" | custom-call | flops 1000000000 | bytes 1048576 | tf_op jit(solution)/shard_map/phases_0/pallas_call | solution.py:57
  46.7 2.2 %partner_0.1 = (bf16[1024,768]{1,0:T(8,128)(2,1)S(1)}, bf16[1024,768]{1,0:T(8,128)(2,1)S(1)}) custom-call(f32[3]{0:T(128)S(1)} %get-tuple-element.31.refs_0_, bf16[4,144,128]{2,1,0:T(8,128)(2,1)S(1)} %stack_first.1.refs_1_.refs_0_.refs_2_, bf16[4,144,128]{2,1,0:T(8,128)(2,1)S(1)} %stack_first.1.refs_1_.refs_0_.refs_2_, ...), custom_call_target="tpu_custom_call" | custom-call | flops 1000000000 | bytes 1048576 | tf_op jit(solution)/shard_map/partner_0/pallas_call | solution.py:57
  49.6 1.4 %collective-permute-start.14 = (bf16[4,128,128]{2,1,0:T(8,128)(2,1)S(1)}, bf16[4,128,128]{2,1,0:T(8,128)(2,1)S(1)}, u32[]{:S(2)}, u32[]{:S(2)}) collective-permute-start(bf16[4,128,128]{2,1,0:T(8,128)(2,1)S(1)} %stack_second.1.refs_2_.refs_0_.refs_8_.refs_16_), channel_id=1, source_target_pairs={{0,4},{1,5},{2,6},{3,7},{4,0},{5,1},{6,2},{7,3},{8,12},{9,13},{10,... | collective-permute-start | bytes 393224 | tf_op jit(solution)/shard_map/ppermute | solution.py:342
  51.0 3.8 %collective-permute-start.16 = (bf16[2,128,128]{2,1,0:T(8,128)(2,1)S(1)}, bf16[2,128,128]{2,1,0:T(8,128)(2,1)S(1)}, u32[]{:S(2)}, u32[]{:S(2)}) collective-permute-start(bf16[2,128,128]{2,1,0:T(8,128)(2,1)S(1)} %slice.27), channel_id=1, source_target_pairs={{0,8},{1,9},{2,10},{3,11},{4,12},{5,13},{6,14},{7,15},{8,0},{9,1},... | collective-permute-start | bytes 196616 | tf_op jit(solution)/shard_map/ppermute | solution.py:342
  54.8 1.2 %phases_1.1.refs_4_.refs_2_ = bf16[2048,256]{1,0:T(8,128)(2,1)S(1)} custom-call(bf16[4,144,128]{2,1,0:T(8,128)(2,1)S(1)} %collective-permute-done.3.refs_0_.refs_2_.refs_3_, bf16[1024,24]{1,0:T(8,128)(2,1)S(1)} %modes.1.refs_1_, bf16[4,128,128]{2,1,0:T(8,128)(2,1)S(1)} %stack_second.1.refs_2_.refs_0_.refs_8_.refs_16_), custom_call_target="tpu_custom_call" | custom-call | flops 1000000000 | bytes 1048576 | tf_op jit(solution)/shard_map/phases_1/pallas_call | solution.py:57
  56.0 2.2 %partner_2.1 = (bf16[1024,768]{1,0:T(8,128)(2,1)S(1)}, bf16[1024,768]{1,0:T(8,128)(2,1)S(1)}) custom-call(f32[3]{0:T(128)S(1)} %get-tuple-element.31.refs_0_, bf16[4,144,128]{2,1,0:T(8,128)(2,1)S(1)} %stack_first.1.refs_1_.refs_0_.refs_2_, bf16[4,144,128]{2,1,0:T(8,128)(2,1)S(1)} %collective-permute-done.4.refs_3_.refs_2_.refs_0_, ...), custom_call_target="tpu_custom_call" | custom-call | flops 1000000000 | bytes 1048576 | tf_op jit(solution)/shard_map/partner_2/pallas_call | solution.py:57
  58.2 1.3 %second_0.1.refs_1_.refs_15_ = f32[2,128,128]{2,1,0:T(8,128)S(1)} custom-call(bf16[4,128,128]{2,1,0:T(8,128)(2,1)S(1)} %stack_second.1.refs_2_.refs_0_.refs_8_.refs_16_, bf16[2,128,128]{2,1,0:T(8,128)(2,1)S(1)} %collective-permute-done.16.refs_1_, bf16[1024,768]{1,0:T(8,128)(2,1)S(1)} %get-tuple-element.40.refs_2_, ...), custom_call_target="tpu_custom_call" | custom-call | flops 1000000000 | bytes 1048576 | tf_op jit(solution)/shard_map/second_0/pallas_call | solution.py:57
  61.8 3.9 %second_rest.1.refs_2_.refs_5_ = f32[2,16,128]{2,1,0:T(8,128)S(1)} custom-call(s32[16]{0:T(128)S(1)} %get-tuple-element.27.refs_0_, bf16[4,128,128]{2,1,0:T(8,128)(2,1)S(1)} %collective-permute-done.13.refs_0_.refs_1_, bf16[4,128,128]{2,1,0:T(8,128)(2,1)S(1)} %collective-permute-done.14.refs_2_, bf16[4,128,128]{2,1,0:T(8,128)(2,1)S(1)} %collective-permute-done.15.refs_3_, ...), custom_call_target="tpu_custom_call" | custom-call | flops 1000000000 | bytes 1048576 | tf_op jit(solution)/shard_map/second_rest/pallas_call | solution.py:57
  65.7 2.3 %collective-permute-start.20 = (f32[2,16,128]{2,1,0:T(8,128)S(1)}, f32[2,16,128]{2,1,0:T(8,128)S(1)}, u32[]{:S(2)}, u32[]{:S(2)}) collective-permute-start(f32[2,16,128]{2,1,0:T(8,128)S(1)} %second_rest.1.refs_2_.refs_5_), channel_id=1, source_target_pairs={{0,6},{1,7},{2,0},{3,1},{4,2},{5,3},{6,4},{7,5},{8,14},{9,15},{10,... | collective-permute-start | bytes 49160 | tf_op jit(solution)/shard_map/ppermute | solution.py:342
  68.0 1.4 %collective-permute-start.21 = (f32[2,16,128]{2,1,0:T(8,128)S(1)}, f32[2,16,128]{2,1,0:T(8,128)S(1)}, u32[]{:S(2)}, u32[]{:S(2)}) collective-permute-start(f32[2,16,128]{2,1,0:T(8,128)S(1)} %second_rest.1.refs_2_.refs_5_), channel_id=1, source_target_pairs={{0,4},{1,5},{2,6},{3,7},{4,0},{5,1},{6,2},{7,3},{8,12},{9,13},{10,... | collective-permute-start | bytes 49160 | tf_op jit(solution)/shard_map/ppermute | solution.py:342
  71.4 1.2 %phases_3.1.refs_4_ = bf16[2048,256]{1,0:T(8,128)(2,1)S(1)} custom-call(bf16[4,144,128]{2,1,0:T(8,128)(2,1)S(1)} %collective-permute-done.5.refs_4_.refs_3_.refs_0_, bf16[1024,24]{1,0:T(8,128)(2,1)S(1)} %modes.1.refs_1_, f32[2,16,128]{2,1,0:T(8,128)S(1)} %second_rest.1.refs_2_.refs_5_), custom_call_target="tpu_custom_call" | custom-call | flops 1000000000 | bytes 1048576 | tf_op jit(solution)/shard_map/phases_3/pallas_call | solution.py:57
  73.3 1.3 %structure.1 = (f32[32,512]{1,0:T(8,128)S(1)}, f32[32,512]{1,0:T(8,128)S(1)}) custom-call(s32[1,512]{1,0:T(1,128)S(1)} %get-tuple-element.49.refs_0_, bf16[2048,256]{1,0:T(8,128)(2,1)S(1)} %phases_0.1.refs_5_.refs_3_.refs_1_, bf16[2048,256]{1,0:T(8,128)(2,1)S(1)} %phases_1.1.refs_4_.refs_2_, bf16[2048,256]{1,0:T(8,128)(2,1)S(1)} %phases_2.1.refs_3_, ...), custom_call_target="tpu_custom_call" | custom-call | flops 100000000 | bytes 1048576 | tf_op jit(solution)/shard_map/structure/pallas_call | solution.py:57
  74.6 1.6 %collective-permute-start.23 = (f32[32,512]{1,0:T(8,128)S(1)}, f32[32,512]{1,0:T(8,128)S(1)}, u32[]{:S(2)}, u32[]{:S(2)}) collective-permute-start(f32[32,512]{1,0:T(8,128)S(1)} %get-tuple-element.51), channel_id=1, source_target_pairs={{0,8},{1,9},{2,10},{3,11},{4,12},{5,13},{6,14},{7,15},{8,0},{9,1},... | collective-permute-start | bytes 196616 | tf_op jit(solution)/shard_map/ppermute | solution.py:342
  78.6 1.3 %collective-permute-done.26 = bf16[32,512]{1,0:T(8,128)(2,1)S(1)} collective-permute-done((bf16[32,512]{1,0:T(8,128)(2,1)S(1)}, bf16[32,512]{1,0:T(8,128)(2,1)S(1)}, u32[]{:S(2)}, u32[]{:S(2)}) %collective-permute-start.26) | collective-permute-done | bytes 32800 | tf_op jit(solution)/shard_map/ppermute | solution.py:342
  79.9 1.6 %collective-permute-done.25 = bf16[32,512]{1,0:T(8,128)(2,1)S(1)} collective-permute-done((bf16[32,512]{1,0:T(8,128)(2,1)S(1)}, bf16[32,512]{1,0:T(8,128)(2,1)S(1)}, u32[]{:S(2)}, u32[]{:S(2)}) %collective-permute-start.25) | collective-permute-done | bytes 32800 | tf_op jit(solution)/shard_map/ppermute | solution.py:342
  82.7 1.6 %collective-permute-start.29 = (bf16[32,512]{1,0:T(8,128)(2,1)S(1)}, bf16[32,512]{1,0:T(8,128)(2,1)S(1)}, u32[]{:S(2)}, u32[]{:S(2)}) collective-permute-start(bf16[32,512]{1,0:T(8,128)(2,1)S(1)} %fusion), channel_id=1, source_target_pairs={{0,48},{1,49},{2,50},{3,51},{4,52},{5,53},{6,54},{7,55},{8,56},{9,... | collective-permute-start | bytes 98312 | tf_op jit(solution)/shard_map/ppermute | solution.py:342
  84.3 2.0 %collective-permute-start.27 = (bf16[32,512]{1,0:T(8,128)(2,1)S(1)}, bf16[32,512]{1,0:T(8,128)(2,1)S(1)}, u32[]{:S(2)}, u32[]{:S(2)}) collective-permute-start(bf16[32,512]{1,0:T(8,128)(2,1)S(1)} %fusion), channel_id=1, source_target_pairs={{0,16},{1,17},{2,18},{3,19},{4,20},{5,21},{6,22},{7,23},{8,24},{9,... | collective-permute-start | bytes 98312 | tf_op jit(solution)/shard_map/ppermute | solution.py:342
  88.3 3.2 %collective-permute-start.30 = (f32[32,512]{1,0:T(8,128)S(1)}, f32[32,512]{1,0:T(8,128)S(1)}, u32[]{:S(2)}, u32[]{:S(2)}) collective-permute-start(f32[32,512]{1,0:T(8,128)S(1)} %add_add_fusion.refs_9_), channel_id=1, source_target_pairs={{0,8},{1,9},{2,10},{3,11},{4,12},{5,13},{6,14},{7,15},{8,0},{9,1},... | collective-permute-start | bytes 196616 | tf_op jit(solution)/shard_map/ppermute | solution.py:342
  92.4 1.3 %respond.1 = f32[8,24,128]{2,1,0:T(8,128)S(1)} custom-call(s32[16]{0:T(128)S(1)} %get-tuple-element.27.refs_0_, bf16[2048,256]{1,0:T(8,128)(2,1)S(1)} %phases_0.1.refs_5_.refs_3_.refs_1_, bf16[2048,256]{1,0:T(8,128)(2,1)S(1)} %phases_1.1.refs_4_.refs_2_, bf16[2048,256]{1,0:T(8,128)(2,1)S(1)} %phases_2.1.refs_3_, bf16[2048,256]{1,0:T(8,128)(2,1)S(1)} %phases_3.1.refs_4_, ...), custom_call_target="tpu_custom_call" | custom-call | flops 100000000 | bytes 1048576 | tf_op jit(solution)/shard_map/respond/pallas_call | solution.py:57
  93.7 14.5 %all_to_all.5.refs_0_ = f32[8,24,128]{2,1,0:T(8,128)S(1)} all-to-all(f32[8,24,128]{2,1,0:T(8,128)S(1)} %respond.1), channel_id=1, replica_groups=mesh['slab'=32,'kgrp'=8] {'kgrp'}, dimensions={0} | all-to-all | bytes 196608 | tf_op jit(solution)/shard_map/all_to_all | solution.py:466
  (83 shorter events, 21.2 us)
Async XLA Ops:
  3.5 12.7 %collective-permute-start.1 = (bf16[144,128]{1,0:T(8,128)(2,1)S(1)}, bf16[144,128]{1,0:T(8,128)(2,1)S(1)}, u32[]{:S(2)}, u32[]{:S(2)}) collective-permute-start(bf16[144,128]{1,0:T(8,128)(2,1)S(1)} %get-tuple-element.28.refs_0_), channel_id=1, source_target_pairs={{0,248},{1,249},{2,250},{3,251},{4,252},{5,253},{6,254},{7,255},{8... | collective-permute-start | bytes 110600 | tf_op jit(solution)/shard_map/ppermute | solution.py:342
  6.6 9.6 %collective-permute-start.2 = (bf16[144,128]{1,0:T(8,128)(2,1)S(1)}, bf16[144,128]{1,0:T(8,128)(2,1)S(1)}, u32[]{:S(2)}, u32[]{:S(2)}) collective-permute-start(bf16[144,128]{1,0:T(8,128)(2,1)S(1)} %get-tuple-element.28.refs_0_), channel_id=1, source_target_pairs={{0,249},{1,248},{2,251},{3,250},{4,253},{5,252},{6,255},{7,254},{8... | collective-permute-start | bytes 110600 | tf_op jit(solution)/shard_map/ppermute | solution.py:342
  11.9 7.6 %collective-permute-start = (bf16[272,128]{1,0:T(8,128)(2,1)S(1)}, bf16[272,128]{1,0:T(8,128)(2,1)S(1)}, u32[]{:S(2)}, u32[]{:S(2)}) collective-permute-start(bf16[272,128]{1,0:T(8,128)(2,1)S(1)} %get-tuple-element.29.refs_1_), channel_id=1, source_target_pairs={{0,1},{1,0},{2,3},{3,2},{4,5},{5,4},{6,7},{7,6},{8,9},{9,8},{10,11... | collective-permute-start | bytes 208904 | tf_op jit(solution)/shard_map/ppermute | solution.py:342
  19.5 12.1 %collective-permute-start.3 = (bf16[4,144,128]{2,1,0:T(8,128)(2,1)S(1)}, bf16[4,144,128]{2,1,0:T(8,128)(2,1)S(1)}, u32[]{:S(2)}, u32[]{:S(2)}) collective-permute-start(bf16[4,144,128]{2,1,0:T(8,128)(2,1)S(1)} %stack_first.1.refs_1_.refs_0_.refs_2_), channel_id=1, source_target_pairs={{0,6},{1,7},{2,0},{3,1},{4,2},{5,3},{6,4},{7,5},{8,14},{9,15},{10,... | collective-permute-start | bytes 442376 | tf_op jit(solution)/shard_map/ppermute | solution.py:342
  22.3 9.4 %collective-permute-start.4 = (bf16[4,144,128]{2,1,0:T(8,128)(2,1)S(1)}, bf16[4,144,128]{2,1,0:T(8,128)(2,1)S(1)}, u32[]{:S(2)}, u32[]{:S(2)}) collective-permute-start(bf16[4,144,128]{2,1,0:T(8,128)(2,1)S(1)} %stack_first.1.refs_1_.refs_0_.refs_2_), channel_id=1, source_target_pairs={{0,4},{1,5},{2,6},{3,7},{4,0},{5,1},{6,2},{7,3},{8,12},{9,13},{10,... | collective-permute-start | bytes 442376 | tf_op jit(solution)/shard_map/ppermute | solution.py:342
  22.7 10.1 %collective-permute-start.5 = (bf16[4,144,128]{2,1,0:T(8,128)(2,1)S(1)}, bf16[4,144,128]{2,1,0:T(8,128)(2,1)S(1)}, u32[]{:S(2)}, u32[]{:S(2)}) collective-permute-start(bf16[4,144,128]{2,1,0:T(8,128)(2,1)S(1)} %stack_first.1.refs_1_.refs_0_.refs_2_), channel_id=1, source_target_pairs={{0,2},{1,3},{2,4},{3,5},{4,6},{5,7},{6,0},{7,1},{8,10},{9,11},{10,... | collective-permute-start | bytes 442376 | tf_op jit(solution)/shard_map/ppermute | solution.py:342
  23.4 6.1 %copy-start.5 = (f32[2,8,128]{2,1,0:T(8,128)S(1)}, f32[2,8,128]{2,1,0:T(8,128)}, u32[]{:S(2)}) copy-start(f32[2,8,128]{2,1,0:T(8,128)} %refs_14_.3) | copy-start | bytes 24580
  23.4 6.0 %collective-permute-start.6 = (bf16[2,144,128]{2,1,0:T(8,128)(2,1)S(1)}, bf16[2,144,128]{2,1,0:T(8,128)(2,1)S(1)}, u32[]{:S(2)}, u32[]{:S(2)}) collective-permute-start(bf16[2,144,128]{2,1,0:T(8,128)(2,1)S(1)} %slice.24), channel_id=1, source_target_pairs={{0,8},{1,9},{2,10},{3,11},{4,12},{5,13},{6,14},{7,15},{8,0},{9,1},... | collective-permute-start | bytes 221192 | tf_op jit(solution)/shard_map/ppermute | solution.py:342
  31.7 2.7 %collective-permute-start.7 = (bf16[2,144,128]{2,1,0:T(8,128)(2,1)S(1)}, bf16[2,144,128]{2,1,0:T(8,128)(2,1)S(1)}, u32[]{:S(2)}, u32[]{:S(2)}) collective-permute-start(bf16[2,144,128]{2,1,0:T(8,128)(2,1)S(1)} %pair_first.1), channel_id=1, source_target_pairs={{0,8},{1,9},{2,10},{3,11},{4,12},{5,13},{6,14},{7,15},{8,0},{9,1},... | collective-permute-start | bytes 221192 | tf_op jit(solution)/shard_map/ppermute | solution.py:342
  31.8 2.6 %collective-permute-start.8 = (bf16[2,144,128]{2,1,0:T(8,128)(2,1)S(1)}, bf16[2,144,128]{2,1,0:T(8,128)(2,1)S(1)}, u32[]{:S(2)}, u32[]{:S(2)}) collective-permute-start(bf16[2,144,128]{2,1,0:T(8,128)(2,1)S(1)} %slice.25), channel_id=1, source_target_pairs={{0,8},{1,9},{2,10},{3,11},{4,12},{5,13},{6,14},{7,15},{8,0},{9,1},... | collective-permute-start | bytes 221192 | tf_op jit(solution)/shard_map/ppermute | solution.py:342
  32.8 2.4 %collective-permute-start.9 = (bf16[2,144,128]{2,1,0:T(8,128)(2,1)S(1)}, bf16[2,144,128]{2,1,0:T(8,128)(2,1)S(1)}, u32[]{:S(2)}, u32[]{:S(2)}) collective-permute-start(bf16[2,144,128]{2,1,0:T(8,128)(2,1)S(1)} %slice.26), channel_id=1, source_target_pairs={{0,8},{1,9},{2,10},{3,11},{4,12},{5,13},{6,14},{7,15},{8,0},{9,1},... | collective-permute-start | bytes 221192 | tf_op jit(solution)/shard_map/ppermute | solution.py:342
  39.4 9.4 %collective-permute-start.10 = (bf16[128,128]{1,0:T(8,128)(2,1)S(1)}, bf16[128,128]{1,0:T(8,128)(2,1)S(1)}, u32[]{:S(2)}, u32[]{:S(2)}) collective-permute-start(bf16[128,128]{1,0:T(8,128)(2,1)S(1)} %get-tuple-element.37.refs_2_.refs_8_.refs_0_), channel_id=1, source_target_pairs={{0,1},{1,0},{2,3},{3,2},{4,5},{5,4},{6,7},{7,6},{8,9},{9,8},{10,11... | collective-permute-start | bytes 98312 | tf_op jit(solution)/shard_map/ppermute | solution.py:342
  41.8 7.1 %collective-permute-start.11 = (bf16[128,128]{1,0:T(8,128)(2,1)S(1)}, bf16[128,128]{1,0:T(8,128)(2,1)S(1)}, u32[]{:S(2)}, u32[]{:S(2)}) collective-permute-start(bf16[128,128]{1,0:T(8,128)(2,1)S(1)} %get-tuple-element.37.refs_2_.refs_8_.refs_0_), channel_id=1, source_target_pairs={{0,248},{1,249},{2,250},{3,251},{4,252},{5,253},{6,254},{7,255},{8... | collective-permute-start | bytes 98312 | tf_op jit(solution)/shard_map/ppermute | solution.py:342
  41.8 7.1 %collective-permute-start.12 = (bf16[128,128]{1,0:T(8,128)(2,1)S(1)}, bf16[128,128]{1,0:T(8,128)(2,1)S(1)}, u32[]{:S(2)}, u32[]{:S(2)}) collective-permute-start(bf16[128,128]{1,0:T(8,128)(2,1)S(1)} %get-tuple-element.37.refs_2_.refs_8_.refs_0_), channel_id=1, source_target_pairs={{0,249},{1,248},{2,251},{3,250},{4,253},{5,252},{6,255},{7,254},{8... | collective-permute-start | bytes 98312 | tf_op jit(solution)/shard_map/ppermute | solution.py:342
  48.9 10.6 %collective-permute-start.13 = (bf16[4,128,128]{2,1,0:T(8,128)(2,1)S(1)}, bf16[4,128,128]{2,1,0:T(8,128)(2,1)S(1)}, u32[]{:S(2)}, u32[]{:S(2)}) collective-permute-start(bf16[4,128,128]{2,1,0:T(8,128)(2,1)S(1)} %stack_second.1.refs_2_.refs_0_.refs_8_.refs_16_), channel_id=1, source_target_pairs={{0,6},{1,7},{2,0},{3,1},{4,2},{5,3},{6,4},{7,5},{8,14},{9,15},{10,... | collective-permute-start | bytes 393224 | tf_op jit(solution)/shard_map/ppermute | solution.py:342
  49.6 10.1 %collective-permute-start.14 = (bf16[4,128,128]{2,1,0:T(8,128)(2,1)S(1)}, bf16[4,128,128]{2,1,0:T(8,128)(2,1)S(1)}, u32[]{:S(2)}, u32[]{:S(2)}) collective-permute-start(bf16[4,128,128]{2,1,0:T(8,128)(2,1)S(1)} %stack_second.1.refs_2_.refs_0_.refs_8_.refs_16_), channel_id=1, source_target_pairs={{0,4},{1,5},{2,6},{3,7},{4,0},{5,1},{6,2},{7,3},{8,12},{9,13},{10,... | collective-permute-start | bytes 393224 | tf_op jit(solution)/shard_map/ppermute | solution.py:342
  51.0 9.3 %collective-permute-start.15 = (bf16[4,128,128]{2,1,0:T(8,128)(2,1)S(1)}, bf16[4,128,128]{2,1,0:T(8,128)(2,1)S(1)}, u32[]{:S(2)}, u32[]{:S(2)}) collective-permute-start(bf16[4,128,128]{2,1,0:T(8,128)(2,1)S(1)} %stack_second.1.refs_2_.refs_0_.refs_8_.refs_16_), channel_id=1, source_target_pairs={{0,2},{1,3},{2,4},{3,5},{4,6},{5,7},{6,0},{7,1},{8,10},{9,11},{10,... | collective-permute-start | bytes 393224 | tf_op jit(solution)/shard_map/ppermute | solution.py:342
  51.0 7.2 %collective-permute-start.16 = (bf16[2,128,128]{2,1,0:T(8,128)(2,1)S(1)}, bf16[2,128,128]{2,1,0:T(8,128)(2,1)S(1)}, u32[]{:S(2)}, u32[]{:S(2)}) collective-permute-start(bf16[2,128,128]{2,1,0:T(8,128)(2,1)S(1)} %slice.27), channel_id=1, source_target_pairs={{0,8},{1,9},{2,10},{3,11},{4,12},{5,13},{6,14},{7,15},{8,0},{9,1},... | collective-permute-start | bytes 196616 | tf_op jit(solution)/shard_map/ppermute | solution.py:342
  59.6 1.3 %collective-permute-start.17 = (bf16[2,128,128]{2,1,0:T(8,128)(2,1)S(1)}, bf16[2,128,128]{2,1,0:T(8,128)(2,1)S(1)}, u32[]{:S(2)}, u32[]{:S(2)}) collective-permute-start(bf16[2,128,128]{2,1,0:T(8,128)(2,1)S(1)} %pair_second.1), channel_id=1, source_target_pairs={{0,8},{1,9},{2,10},{3,11},{4,12},{5,13},{6,14},{7,15},{8,0},{9,1},... | collective-permute-start | bytes 196616 | tf_op jit(solution)/shard_map/ppermute | solution.py:342
  59.7 1.5 %collective-permute-start.18 = (bf16[2,128,128]{2,1,0:T(8,128)(2,1)S(1)}, bf16[2,128,128]{2,1,0:T(8,128)(2,1)S(1)}, u32[]{:S(2)}, u32[]{:S(2)}) collective-permute-start(bf16[2,128,128]{2,1,0:T(8,128)(2,1)S(1)} %slice.28), channel_id=1, source_target_pairs={{0,8},{1,9},{2,10},{3,11},{4,12},{5,13},{6,14},{7,15},{8,0},{9,1},... | collective-permute-start | bytes 196616 | tf_op jit(solution)/shard_map/ppermute | solution.py:342
  60.3 1.5 %collective-permute-start.19 = (bf16[2,128,128]{2,1,0:T(8,128)(2,1)S(1)}, bf16[2,128,128]{2,1,0:T(8,128)(2,1)S(1)}, u32[]{:S(2)}, u32[]{:S(2)}) collective-permute-start(bf16[2,128,128]{2,1,0:T(8,128)(2,1)S(1)} %slice.29), channel_id=1, source_target_pairs={{0,8},{1,9},{2,10},{3,11},{4,12},{5,13},{6,14},{7,15},{8,0},{9,1},... | collective-permute-start | bytes 196616 | tf_op jit(solution)/shard_map/ppermute | solution.py:342
  65.7 6.9 %collective-permute-start.20 = (f32[2,16,128]{2,1,0:T(8,128)S(1)}, f32[2,16,128]{2,1,0:T(8,128)S(1)}, u32[]{:S(2)}, u32[]{:S(2)}) collective-permute-start(f32[2,16,128]{2,1,0:T(8,128)S(1)} %second_rest.1.refs_2_.refs_5_), channel_id=1, source_target_pairs={{0,6},{1,7},{2,0},{3,1},{4,2},{5,3},{6,4},{7,5},{8,14},{9,15},{10,... | collective-permute-start | bytes 49160 | tf_op jit(solution)/shard_map/ppermute | solution.py:342
  68.0 4.6 %collective-permute-start.21 = (f32[2,16,128]{2,1,0:T(8,128)S(1)}, f32[2,16,128]{2,1,0:T(8,128)S(1)}, u32[]{:S(2)}, u32[]{:S(2)}) collective-permute-start(f32[2,16,128]{2,1,0:T(8,128)S(1)} %second_rest.1.refs_2_.refs_5_), channel_id=1, source_target_pairs={{0,4},{1,5},{2,6},{3,7},{4,0},{5,1},{6,2},{7,3},{8,12},{9,13},{10,... | collective-permute-start | bytes 49160 | tf_op jit(solution)/shard_map/ppermute | solution.py:342
  69.4 3.9 %collective-permute-start.22 = (f32[2,16,128]{2,1,0:T(8,128)S(1)}, f32[2,16,128]{2,1,0:T(8,128)S(1)}, u32[]{:S(2)}, u32[]{:S(2)}) collective-permute-start(f32[2,16,128]{2,1,0:T(8,128)S(1)} %second_rest.1.refs_2_.refs_5_), channel_id=1, source_target_pairs={{0,2},{1,3},{2,4},{3,5},{4,6},{5,7},{6,0},{7,1},{8,10},{9,11},{10,... | collective-permute-start | bytes 49160 | tf_op jit(solution)/shard_map/ppermute | solution.py:342
  74.6 2.5 %collective-permute-start.23 = (f32[32,512]{1,0:T(8,128)S(1)}, f32[32,512]{1,0:T(8,128)S(1)}, u32[]{:S(2)}, u32[]{:S(2)}) collective-permute-start(f32[32,512]{1,0:T(8,128)S(1)} %get-tuple-element.51), channel_id=1, source_target_pairs={{0,8},{1,9},{2,10},{3,11},{4,12},{5,13},{6,14},{7,15},{8,0},{9,1},... | collective-permute-start | bytes 196616 | tf_op jit(solution)/shard_map/ppermute | solution.py:342
  77.0 2.8 %collective-permute-start.26 = (bf16[32,512]{1,0:T(8,128)(2,1)S(1)}, bf16[32,512]{1,0:T(8,128)(2,1)S(1)}, u32[]{:S(2)}, u32[]{:S(2)}) collective-permute-start(bf16[32,512]{1,0:T(8,128)(2,1)S(1)} %get-tuple-element.52), channel_id=1, source_target_pairs={{0,192},{1,193},{2,194},{3,195},{4,196},{5,197},{6,198},{7,199},{8... | collective-permute-start | bytes 98312 | tf_op jit(solution)/shard_map/ppermute | solution.py:342
  77.1 4.4 %collective-permute-start.25 = (bf16[32,512]{1,0:T(8,128)(2,1)S(1)}, bf16[32,512]{1,0:T(8,128)(2,1)S(1)}, u32[]{:S(2)}, u32[]{:S(2)}) collective-permute-start(bf16[32,512]{1,0:T(8,128)(2,1)S(1)} %get-tuple-element.52), channel_id=1, source_target_pairs={{0,128},{1,129},{2,130},{3,131},{4,132},{5,133},{6,134},{7,135},{8... | collective-permute-start | bytes 98312 | tf_op jit(solution)/shard_map/ppermute | solution.py:342
  77.9 4.7 %collective-permute-start.24 = (bf16[32,512]{1,0:T(8,128)(2,1)S(1)}, bf16[32,512]{1,0:T(8,128)(2,1)S(1)}, u32[]{:S(2)}, u32[]{:S(2)}) collective-permute-start(bf16[32,512]{1,0:T(8,128)(2,1)S(1)} %get-tuple-element.52), channel_id=1, source_target_pairs={{0,64},{1,65},{2,66},{3,67},{4,68},{5,69},{6,70},{7,71},{8,72},{9,... | collective-permute-start | bytes 98312 | tf_op jit(solution)/shard_map/ppermute | solution.py:342
  82.7 4.8 %collective-permute-start.29 = (bf16[32,512]{1,0:T(8,128)(2,1)S(1)}, bf16[32,512]{1,0:T(8,128)(2,1)S(1)}, u32[]{:S(2)}, u32[]{:S(2)}) collective-permute-start(bf16[32,512]{1,0:T(8,128)(2,1)S(1)} %fusion), channel_id=1, source_target_pairs={{0,48},{1,49},{2,50},{3,51},{4,52},{5,53},{6,54},{7,55},{8,56},{9,... | collective-permute-start | bytes 98312 | tf_op jit(solution)/shard_map/ppermute | solution.py:342
  84.3 4.0 %collective-permute-start.28 = (bf16[32,512]{1,0:T(8,128)(2,1)S(1)}, bf16[32,512]{1,0:T(8,128)(2,1)S(1)}, u32[]{:S(2)}, u32[]{:S(2)}) collective-permute-start(bf16[32,512]{1,0:T(8,128)(2,1)S(1)} %fusion), channel_id=1, source_target_pairs={{0,32},{1,33},{2,34},{3,35},{4,36},{5,37},{6,38},{7,39},{8,40},{9,... | collective-permute-start | bytes 98312 | tf_op jit(solution)/shard_map/ppermute | solution.py:342
  84.3 4.0 %collective-permute-start.27 = (bf16[32,512]{1,0:T(8,128)(2,1)S(1)}, bf16[32,512]{1,0:T(8,128)(2,1)S(1)}, u32[]{:S(2)}, u32[]{:S(2)}) collective-permute-start(bf16[32,512]{1,0:T(8,128)(2,1)S(1)} %fusion), channel_id=1, source_target_pairs={{0,16},{1,17},{2,18},{3,19},{4,20},{5,21},{6,22},{7,23},{8,24},{9,... | collective-permute-start | bytes 98312 | tf_op jit(solution)/shard_map/ppermute | solution.py:342
  88.3 4.1 %collective-permute-start.30 = (f32[32,512]{1,0:T(8,128)S(1)}, f32[32,512]{1,0:T(8,128)S(1)}, u32[]{:S(2)}, u32[]{:S(2)}) collective-permute-start(f32[32,512]{1,0:T(8,128)S(1)} %add_add_fusion.refs_9_), channel_id=1, source_target_pairs={{0,8},{1,9},{2,10},{3,11},{4,12},{5,13},{6,14},{7,15},{8,0},{9,1},... | collective-permute-start | bytes 196616 | tf_op jit(solution)/shard_map/ppermute | solution.py:342
  (9 other events, 22.3 us)

commit v2 on v1

--- a/solution.py
+++ b/solution.py
@@ -152,7 +152,13 @@
     return total
 
 
+def aligned(start):
+    return pl.ds(start if isinstance(start, int) else pl.multiple_of(start, 32), 32)
+
+
 def rows_of(h, count):
+    if isinstance(h, int):
+        return pl.ds(h * count, count)
     return pl.ds(pl.multiple_of(h * count, count), count)
 
 
@@ -171,7 +177,7 @@
         xyz = coordinates(block_of(y_ref, c_ref, i))
         x = xyz[0:1] + shift_ref[i // 2]
         for r in range(0, HALF, 32):
-            rows = pl.ds(pl.multiple_of(h * HALF + r, 32), 32)
+            rows = aligned(h * HALF + r)
             dx = x - here_s[0, rows, :]
             dy = xyz[1:2] - here_s[1, rows, :]
             dz = xyz[2:3] - here_s[2, rows, :]
@@ -180,7 +186,7 @@
             turn = horner(TWOCOS, v)
             prev = None
             for n in range(8):
-                g_ref[pl.ds(pl.multiple_of(h * 512 + n * HALF + r, 32), 32), i * 128 : (i + 1) * 128] = cur.astype(BF16)
+                g_ref[aligned(h * 512 + n * HALF + r), i * 128 : (i + 1) * 128] = cur.astype(BF16)
                 if n < 7:
                     nxt = turn * cur if prev is None else turn * cur - prev
                     prev, cur = cur, nxt
@@ -206,8 +212,7 @@
         messages_s[j] = messages_of(y, c, edge_ref[0])
     here_of(near_ref, 0, here_s)
 
-    @pl.loop(0, 2)
-    def _(h):
+    for h in range(2):
         acc = None
         for j, (y, c, n, g) in enumerate(((y1, c1, n1, g1), (y2, c2, n2, g2), (y3, c3, n3, g3))):
             basis_half(h, shift_ref, y, c, n, g, here_s)
@@ -230,8 +235,7 @@
 def second_body(y_ref, c_ref, own_ref, partner_ref, edge_ref, mixing_ref, part_ref, messages_s):
     messages_s[...] = messages_of(y_ref, c_ref, edge_ref[1])
 
-    @pl.loop(0, 2)
-    def _(h):
+    for h in range(2):
         for z, g in enumerate((own_ref, partner_ref)):
             part_ref[z, rows_of(h, HALF), :] = mix(nn(g[rows_of(h, 512), :], messages_s[...]), mixing_ref[1])
 
@@ -240,8 +244,7 @@
     for j, (y, c) in enumerate(((y1, c1), (y2, c2), (y3, c3))):
         messages_s[j] = messages_of(y, c, edge_ref[1])
 
-    @pl.loop(0, 2)
-    def _(h):
+    for h in range(2):
         for z, gs in enumerate(((o1, o2, o3), (p1, p2, p3))):
             acc = None
             for j, g in enumerate(gs):
@@ -384,7 +387,7 @@
     where = jnp.stack([lax.axis_index("slab"), lax.axis_index("kgrp")]).astype(jnp.int32)
     block, with_slots = call(
         pack_body, (shape((PAYLOAD, ROWS), BF16), shape((WIDE, ROWS), BF16)),
-        atom_descriptors, atom_locations, adjacent_atom_slots.T, neighbour_tally.reshape(1, ROWS), name="pack",
+        atom_descriptors, atom_locations, adjacent_atom_slots.T, neighbour_tally.reshape(1, ROWS), name="pack", limit=56,
     )
     near = near_blocks(block, with_slots)
     smem = pl.BlockSpec(memory_space=pltpu.SMEM)

time: 109 us -> 107 us (0.982)
  local copies, waits for them, and re-layouts: 3.56 us -> 1.6 us
    unnamed x20 -> x16, local copies, waits for them, and re-layouts: 3.53 us -> 1.56 us
where the time goes in v2:
time: 107 us
  starting transfers between devices  48 us (45%)
  Pallas kernels  29.3 us (27%)
  blocking collectives  14.4 us (13%)
  waiting for transfers between devices  12.5 us (12%)
  local copies, waits for them, and re-layouts  1.6 us (1%)
    ppermute x31, starting transfers between devices, move(): return lax.ppermute(x, AXES, pairs(lax.axis_size('slab'), target))  48 us
    pallas_call x22, Pallas kernels, call(): pl.pallas_call(lambda *refs: body(*refs[:n], *refs[n + m:]), out_shape=ou...  29.3 us
    all_to_all x1, blocking collectives, shards(): partial = lax.all_to_all(partial, 'kgrp', 0, 0)  14.4 us
    ppermute x31, waiting for transfers between devices, move(): return lax.ppermute(x, AXES, pairs(lax.axis_size('slab'), target))  12.5 us
  transfers between devices with their start and end apart: 31, of which 12 were waited for; matrix products, arithmetic and copies ran while one was open for 0% of the time, Pallas kernels for 16%

profile of v2, /device:TPU:1, one launch (start us, length us, event | category | flops | bytes accessed | tf_op | source)
XLA Modules:
  0.0 106.9 jit_solution(15047989884418526662)
XLA Ops:
  0.6 1.5 %pack.1 = (bf16[144,128]{1,0:T(8,128)(2,1)}, bf16[272,128]{1,0:T(8,128)(2,1)}) custom-call(bf16[128,128]{1,0:T(8,128)(2,1)} %refs_0_.2, f32[3,128]{1,0:T(4,128)} %refs_1_.3, s32[64,128]{1,0:T(8,128)} %bitcast.6, s32[1,128]{1,0:T(1,128)} %bitcast.7), custom_call_target="tpu_custom_call" | custom-call | bytes 1048576 | tf_op jit(solution)/shard_map/pack/pallas_call | solution.py:57
  2.1 3.0 %collective-permute-start.1 = (bf16[144,128]{1,0:T(8,128)(2,1)}, bf16[144,128]{1,0:T(8,128)(2,1)S(1)}, u32[]{:S(2)}, u32[]{:S(2)}) collective-permute-start(bf16[144,128]{1,0:T(8,128)(2,1)} %get-tuple-element.28.refs_0_), channel_id=1, source_target_pairs={{0,248},{1,249},{2,250},{3,251},{4,252},{5,253},{6,254},{7,255},{8... | collective-permute-start | bytes 110600 | tf_op jit(solution)/shard_map/ppermute | solution.py:345
  5.1 5.3 %collective-permute-start.2 = (bf16[144,128]{1,0:T(8,128)(2,1)}, bf16[144,128]{1,0:T(8,128)(2,1)S(1)}, u32[]{:S(2)}, u32[]{:S(2)}) collective-permute-start(bf16[144,128]{1,0:T(8,128)(2,1)} %get-tuple-element.28.refs_0_), channel_id=1, source_target_pairs={{0,249},{1,248},{2,251},{3,250},{4,253},{5,252},{6,255},{7,254},{8... | collective-permute-start | bytes 110600 | tf_op jit(solution)/shard_map/ppermute | solution.py:345
  13.9 1.7 %counts.1 = (f32[6,128,128]{2,1,0:T(8,128)S(1)}, f32[6,128,128]{2,1,0:T(8,128)S(1)}, f32[6,128,128]{2,1,0:T(8,128)S(1)}, f32[6,128,128]{2,1,0:T(8,128)S(1)}) custom-call(s32[16]{0:T(128)S(1)} %get-tuple-element.27.refs_0_, bf16[272,128]{1,0:T(8,128)(2,1)S(1)} %copy-done.6), custom_call_target="tpu_custom_call" | custom-call | flops 1000000000 | bytes 1048576 | tf_op jit(solution)/shard_map/counts/pallas_call | solution.py:57
  15.7 2.6 %collective-permute-done.refs_1_ = bf16[272,128]{1,0:T(8,128)(2,1)S(1)} collective-permute-done((bf16[272,128]{1,0:T(8,128)(2,1)}, bf16[272,128]{1,0:T(8,128)(2,1)S(1)}, u32[]{:S(2)}, u32[]{:S(2)}) %collective-permute-start) | collective-permute-done | bytes 69664 | tf_op jit(solution)/shard_map/ppermute | solution.py:345
  18.3 2.8 %collective-permute-start.3 = (bf16[4,144,128]{2,1,0:T(8,128)(2,1)S(1)}, bf16[4,144,128]{2,1,0:T(8,128)(2,1)S(1)}, u32[]{:S(2)}, u32[]{:S(2)}) collective-permute-start(bf16[4,144,128]{2,1,0:T(8,128)(2,1)S(1)} %stack_first.1.refs_1_.refs_0_.refs_2_), channel_id=1, source_target_pairs={{0,6},{1,7},{2,0},{3,1},{4,2},{5,3},{6,4},{7,5},{8,14},{9,15},{10,... | collective-permute-start | bytes 442376 | tf_op jit(solution)/shard_map/ppermute | solution.py:345
  22.2 4.3 %collective-permute-start.6 = (bf16[2,144,128]{2,1,0:T(8,128)(2,1)S(1)}, bf16[2,144,128]{2,1,0:T(8,128)(2,1)S(1)}, u32[]{:S(2)}, u32[]{:S(2)}) collective-permute-start(bf16[2,144,128]{2,1,0:T(8,128)(2,1)S(1)} %slice.24), channel_id=1, source_target_pairs={{0,8},{1,9},{2,10},{3,11},{4,12},{5,13},{6,14},{7,15},{8,0},{9,1},... | collective-permute-start | bytes 221192 | tf_op jit(solution)/shard_map/ppermute | solution.py:345
  26.4 1.7 %partner_counts.1 = (f32[6,128,128]{2,1,0:T(8,128)S(1)}, f32[6,128,128]{2,1,0:T(8,128)S(1)}, f32[6,128,128]{2,1,0:T(8,128)S(1)}, f32[6,128,128]{2,1,0:T(8,128)S(1)}) custom-call(s32[16]{0:T(128)S(1)} %get-tuple-element.27.refs_0_, bf16[272,128]{1,0:T(8,128)(2,1)S(1)} %collective-permute-done.refs_1_), custom_call_target="tpu_custom_call" | custom-call | flops 1000000000 | bytes 1048576 | tf_op jit(solution)/shard_map/partner_counts/pallas_call | solution.py:57
  28.2 2.1 %first_0.1 = (bf16[1024,768]{1,0:T(8,128)(2,1)S(1)}, f32[128,128]{1,0:T(8,128)S(1)}) custom-call(f32[3]{0:T(128)S(1)} %get-tuple-element.31.refs_0_, bf16[4,144,128]{2,1,0:T(8,128)(2,1)S(1)} %stack_first.1.refs_1_.refs_0_.refs_2_, bf16[2,144,128]{2,1,0:T(8,128)(2,1)S(1)} %collective-permute-done.6.refs_2_.refs_4_, ...), custom_call_target="tpu_custom_call" | custom-call | flops 1000000000 | bytes 1048576 | tf_op jit(solution)/shard_map/first_0/pallas_call | solution.py:57
  31.5 1.5 %collective-permute-start.9 = (bf16[2,144,128]{2,1,0:T(8,128)(2,1)S(1)}, bf16[2,144,128]{2,1,0:T(8,128)(2,1)S(1)}, u32[]{:S(2)}, u32[]{:S(2)}) collective-permute-start(bf16[2,144,128]{2,1,0:T(8,128)(2,1)S(1)} %slice.26), channel_id=1, source_target_pairs={{0,8},{1,9},{2,10},{3,11},{4,12},{5,13},{6,14},{7,15},{8,0},{9,1},... | collective-permute-start | bytes 221192 | tf_op jit(solution)/shard_map/ppermute | solution.py:345
  33.9 3.8 %first_rest.1 = (bf16[1024,768]{1,0:T(8,128)(2,1)S(1)}, bf16[1024,768]{1,0:T(8,128)(2,1)S(1)}, bf16[1024,768]{1,0:T(8,128)(2,1)S(1)}, bf16[128,128]{1,0:T(8,128)(2,1)S(1)}) custom-call(f32[3]{0:T(128)S(1)} %get-tuple-element.31.refs_0_, bf16[4,144,128]{2,1,0:T(8,128)(2,1)S(1)} %stack_first.1.refs_1_.refs_0_.refs_2_, ...), custom_call_target="tpu_custom_call" | custom-call | flops 1000000000 | bytes 1048576 | tf_op jit(solution)/shard_map/first_rest/pallas_call | solution.py:57
  37.7 2.4 %collective-permute-start.10 = (bf16[128,128]{1,0:T(8,128)(2,1)S(1)}, bf16[128,128]{1,0:T(8,128)(2,1)S(1)}, u32[]{:S(2)}, u32[]{:S(2)}) collective-permute-start(bf16[128,128]{1,0:T(8,128)(2,1)S(1)} %get-tuple-element.37.refs_2_.refs_8_.refs_0_), channel_id=1, source_target_pairs={{0,1},{1,0},{2,3},{3,2},{4,5},{5,4},{6,7},{7,6},{8,9},{9,8},{10,11... | collective-permute-start | bytes 98312 | tf_op jit(solution)/shard_map/ppermute | solution.py:345
  40.1 3.6 %collective-permute-start.12 = (bf16[128,128]{1,0:T(8,128)(2,1)S(1)}, bf16[128,128]{1,0:T(8,128)(2,1)S(1)}, u32[]{:S(2)}, u32[]{:S(2)}) collective-permute-start(bf16[128,128]{1,0:T(8,128)(2,1)S(1)} %get-tuple-element.37.refs_2_.refs_8_.refs_0_), channel_id=1, source_target_pairs={{0,249},{1,248},{2,251},{3,250},{4,253},{5,252},{6,255},{7,254},{8... | collective-permute-start | bytes 98312 | tf_op jit(solution)/shard_map/ppermute | solution.py:345
  43.7 1.2 %phases_0.1.refs_5_.refs_3_.refs_1_ = bf16[2048,256]{1,0:T(8,128)(2,1)S(1)} custom-call(bf16[4,144,128]{2,1,0:T(8,128)(2,1)S(1)} %stack_first.1.refs_1_.refs_0_.refs_2_, bf16[1024,24]{1,0:T(8,128)(2,1)S(1)} %modes.1.refs_1_, bf16[128,128]{1,0:T(8,128)(2,1)S(1)} %get-tuple-element.37.refs_2_.refs_8_.refs_0_), custom_call_target="tpu_custom_call" | custom-call | flops 1000000000 | bytes 1048576 | tf_op jit(solution)/shard_map/phases_0/pallas_call | solution.py:57
  44.9 2.2 %partner_0.1 = (bf16[1024,768]{1,0:T(8,128)(2,1)S(1)}, bf16[1024,768]{1,0:T(8,128)(2,1)S(1)}) custom-call(f32[3]{0:T(128)S(1)} %get-tuple-element.31.refs_0_, bf16[4,144,128]{2,1,0:T(8,128)(2,1)S(1)} %stack_first.1.refs_1_.refs_0_.refs_2_, bf16[4,144,128]{2,1,0:T(8,128)(2,1)S(1)} %stack_first.1.refs_1_.refs_0_.refs_2_, ...), custom_call_target="tpu_custom_call" | custom-call | flops 1000000000 | bytes 1048576 | tf_op jit(solution)/shard_map/partner_0/pallas_call | solution.py:57
  48.0 1.4 %collective-permute-start.14 = (bf16[4,128,128]{2,1,0:T(8,128)(2,1)S(1)}, bf16[4,128,128]{2,1,0:T(8,128)(2,1)S(1)}, u32[]{:S(2)}, u32[]{:S(2)}) collective-permute-start(bf16[4,128,128]{2,1,0:T(8,128)(2,1)S(1)} %stack_second.1.refs_2_.refs_0_.refs_8_.refs_16_), channel_id=1, source_target_pairs={{0,4},{1,5},{2,6},{3,7},{4,0},{5,1},{6,2},{7,3},{8,12},{9,13},{10,... | collective-permute-start | bytes 393224 | tf_op jit(solution)/shard_map/ppermute | solution.py:345
  49.4 4.2 %collective-permute-start.16 = (bf16[2,128,128]{2,1,0:T(8,128)(2,1)S(1)}, bf16[2,128,128]{2,1,0:T(8,128)(2,1)S(1)}, u32[]{:S(2)}, u32[]{:S(2)}) collective-permute-start(bf16[2,128,128]{2,1,0:T(8,128)(2,1)S(1)} %slice.27), channel_id=1, source_target_pairs={{0,8},{1,9},{2,10},{3,11},{4,12},{5,13},{6,14},{7,15},{8,0},{9,1},... | collective-permute-start | bytes 196616 | tf_op jit(solution)/shard_map/ppermute | solution.py:345
  53.6 1.2 %phases_1.1.refs_4_.refs_2_ = bf16[2048,256]{1,0:T(8,128)(2,1)S(1)} custom-call(bf16[4,144,128]{2,1,0:T(8,128)(2,1)S(1)} %collective-permute-done.3.refs_0_.refs_2_.refs_3_, bf16[1024,24]{1,0:T(8,128)(2,1)S(1)} %modes.1.refs_1_, bf16[4,128,128]{2,1,0:T(8,128)(2,1)S(1)} %stack_second.1.refs_2_.refs_0_.refs_8_.refs_16_), custom_call_target="tpu_custom_call" | custom-call | flops 1000000000 | bytes 1048576 | tf_op jit(solution)/shard_map/phases_1/pallas_call | solution.py:57
  54.8 2.2 %partner_2.1 = (bf16[1024,768]{1,0:T(8,128)(2,1)S(1)}, bf16[1024,768]{1,0:T(8,128)(2,1)S(1)}) custom-call(f32[3]{0:T(128)S(1)} %get-tuple-element.31.refs_0_, bf16[4,144,128]{2,1,0:T(8,128)(2,1)S(1)} %stack_first.1.refs_1_.refs_0_.refs_2_, bf16[4,144,128]{2,1,0:T(8,128)(2,1)S(1)} %collective-permute-done.4.refs_3_.refs_2_.refs_0_, ...), custom_call_target="tpu_custom_call" | custom-call | flops 1000000000 | bytes 1048576 | tf_op jit(solution)/shard_map/partner_2/pallas_call | solution.py:57
  60.7 3.6 %second_rest.1.refs_2_.refs_5_ = f32[2,16,128]{2,1,0:T(8,128)S(1)} custom-call(s32[16]{0:T(128)S(1)} %get-tuple-element.27.refs_0_, bf16[4,128,128]{2,1,0:T(8,128)(2,1)S(1)} %collective-permute-done.13.refs_0_.refs_1_, bf16[4,128,128]{2,1,0:T(8,128)(2,1)S(1)} %collective-permute-done.14.refs_2_, bf16[4,128,128]{2,1,0:T(8,128)(2,1)S(1)} %collective-permute-done.15.refs_3_, ...), custom_call_target="tpu_custom_call" | custom-call | flops 1000000000 | bytes 1048576 | tf_op jit(solution)/shard_map/second_rest/pallas_call | solution.py:57
  64.4 2.2 %collective-permute-start.20 = (f32[2,16,128]{2,1,0:T(8,128)S(1)}, f32[2,16,128]{2,1,0:T(8,128)S(1)}, u32[]{:S(2)}, u32[]{:S(2)}) collective-permute-start(f32[2,16,128]{2,1,0:T(8,128)S(1)} %second_rest.1.refs_2_.refs_5_), channel_id=1, source_target_pairs={{0,6},{1,7},{2,0},{3,1},{4,2},{5,3},{6,4},{7,5},{8,14},{9,15},{10,... | collective-permute-start | bytes 49160 | tf_op jit(solution)/shard_map/ppermute | solution.py:345
  66.6 1.4 %collective-permute-start.21 = (f32[2,16,128]{2,1,0:T(8,128)S(1)}, f32[2,16,128]{2,1,0:T(8,128)S(1)}, u32[]{:S(2)}, u32[]{:S(2)}) collective-permute-start(f32[2,16,128]{2,1,0:T(8,128)S(1)} %second_rest.1.refs_2_.refs_5_), channel_id=1, source_target_pairs={{0,4},{1,5},{2,6},{3,7},{4,0},{5,1},{6,2},{7,3},{8,12},{9,13},{10,... | collective-permute-start | bytes 49160 | tf_op jit(solution)/shard_map/ppermute | solution.py:345
  68.8 1.2 %phases_2.1.refs_3_ = bf16[2048,256]{1,0:T(8,128)(2,1)S(1)} custom-call(bf16[4,144,128]{2,1,0:T(8,128)(2,1)S(1)} %collective-permute-done.4.refs_3_.refs_2_.refs_0_, bf16[1024,24]{1,0:T(8,128)(2,1)S(1)} %modes.1.refs_1_, f32[2,16,128]{2,1,0:T(8,128)S(1)} %second_rest.1.refs_2_.refs_5_), custom_call_target="tpu_custom_call" | custom-call | flops 1000000000 | bytes 1048576 | tf_op jit(solution)/shard_map/phases_2/pallas_call | solution.py:57
  70.0 1.2 %phases_3.1.refs_4_ = bf16[2048,256]{1,0:T(8,128)(2,1)S(1)} custom-call(bf16[4,144,128]{2,1,0:T(8,128)(2,1)S(1)} %collective-permute-done.5.refs_4_.refs_3_.refs_0_, bf16[1024,24]{1,0:T(8,128)(2,1)S(1)} %modes.1.refs_1_, f32[2,16,128]{2,1,0:T(8,128)S(1)} %second_rest.1.refs_2_.refs_5_), custom_call_target="tpu_custom_call" | custom-call | flops 1000000000 | bytes 1048576 | tf_op jit(solution)/shard_map/phases_3/pallas_call | solution.py:57
  71.9 1.3 %structure.1 = (f32[32,512]{1,0:T(8,128)S(1)}, f32[32,512]{1,0:T(8,128)S(1)}) custom-call(s32[1,512]{1,0:T(1,128)S(1)} %get-tuple-element.49.refs_0_, bf16[2048,256]{1,0:T(8,128)(2,1)S(1)} %phases_0.1.refs_5_.refs_3_.refs_1_, bf16[2048,256]{1,0:T(8,128)(2,1)S(1)} %phases_1.1.refs_4_.refs_2_, bf16[2048,256]{1,0:T(8,128)(2,1)S(1)} %phases_2.1.refs_3_, ...), custom_call_target="tpu_custom_call" | custom-call | flops 100000000 | bytes 1048576 | tf_op jit(solution)/shard_map/structure/pallas_call | solution.py:57
  73.2 1.6 %collective-permute-start.23 = (f32[32,512]{1,0:T(8,128)S(1)}, f32[32,512]{1,0:T(8,128)S(1)}, u32[]{:S(2)}, u32[]{:S(2)}) collective-permute-start(f32[32,512]{1,0:T(8,128)S(1)} %get-tuple-element.51), channel_id=1, source_target_pairs={{0,8},{1,9},{2,10},{3,11},{4,12},{5,13},{6,14},{7,15},{8,0},{9,1},... | collective-permute-start | bytes 196616 | tf_op jit(solution)/shard_map/ppermute | solution.py:345
  77.2 1.3 %collective-permute-done.26 = bf16[32,512]{1,0:T(8,128)(2,1)S(1)} collective-permute-done((bf16[32,512]{1,0:T(8,128)(2,1)S(1)}, bf16[32,512]{1,0:T(8,128)(2,1)S(1)}, u32[]{:S(2)}, u32[]{:S(2)}) %collective-permute-start.26) | collective-permute-done | bytes 32800 | tf_op jit(solution)/shard_map/ppermute | solution.py:345
  78.5 1.6 %collective-permute-done.25 = bf16[32,512]{1,0:T(8,128)(2,1)S(1)} collective-permute-done((bf16[32,512]{1,0:T(8,128)(2,1)S(1)}, bf16[32,512]{1,0:T(8,128)(2,1)S(1)}, u32[]{:S(2)}, u32[]{:S(2)}) %collective-permute-start.25) | collective-permute-done | bytes 32800 | tf_op jit(solution)/shard_map/ppermute | solution.py:345
  82.4 2.5 %collective-permute-start.27 = (bf16[32,512]{1,0:T(8,128)(2,1)S(1)}, bf16[32,512]{1,0:T(8,128)(2,1)S(1)}, u32[]{:S(2)}, u32[]{:S(2)}) collective-permute-start(bf16[32,512]{1,0:T(8,128)(2,1)S(1)} %fusion), channel_id=1, source_target_pairs={{0,16},{1,17},{2,18},{3,19},{4,20},{5,21},{6,22},{7,23},{8,24},{9,... | collective-permute-start | bytes 98312 | tf_op jit(solution)/shard_map/ppermute | solution.py:345
  86.6 3.0 %collective-permute-start.30 = (f32[32,512]{1,0:T(8,128)S(1)}, f32[32,512]{1,0:T(8,128)S(1)}, u32[]{:S(2)}, u32[]{:S(2)}) collective-permute-start(f32[32,512]{1,0:T(8,128)S(1)} %add_add_fusion.refs_9_), channel_id=1, source_target_pairs={{0,8},{1,9},{2,10},{3,11},{4,12},{5,13},{6,14},{7,15},{8,0},{9,1},... | collective-permute-start | bytes 196616 | tf_op jit(solution)/shard_map/ppermute | solution.py:345
  90.6 1.3 %respond.1 = f32[8,24,128]{2,1,0:T(8,128)S(1)} custom-call(s32[16]{0:T(128)S(1)} %get-tuple-element.27.refs_0_, bf16[2048,256]{1,0:T(8,128)(2,1)S(1)} %phases_0.1.refs_5_.refs_3_.refs_1_, bf16[2048,256]{1,0:T(8,128)(2,1)S(1)} %phases_1.1.refs_4_.refs_2_, bf16[2048,256]{1,0:T(8,128)(2,1)S(1)} %phases_2.1.refs_3_, bf16[2048,256]{1,0:T(8,128)(2,1)S(1)} %phases_3.1.refs_4_, ...), custom_call_target="tpu_custom_call" | custom-call | flops 100000000 | bytes 1048576 | tf_op jit(solution)/shard_map/respond/pallas_call | solution.py:57
  91.9 14.4 %all_to_all.5.refs_0_ = f32[8,24,128]{2,1,0:T(8,128)S(1)} all-to-all(f32[8,24,128]{2,1,0:T(8,128)S(1)} %respond.1), channel_id=1, replica_groups=mesh['slab'=32,'kgrp'=8] {'kgrp'}, dimensions={0} | all-to-all | bytes 196608 | tf_op jit(solution)/shard_map/all_to_all | solution.py:469
  (79 shorter events, 20.7 us)
Async XLA Ops:
  2.1 13.5 %collective-permute-start.1 = (bf16[144,128]{1,0:T(8,128)(2,1)}, bf16[144,128]{1,0:T(8,128)(2,1)S(1)}, u32[]{:S(2)}, u32[]{:S(2)}) collective-permute-start(bf16[144,128]{1,0:T(8,128)(2,1)} %get-tuple-element.28.refs_0_), channel_id=1, source_target_pairs={{0,248},{1,249},{2,250},{3,251},{4,252},{5,253},{6,254},{7,255},{8... | collective-permute-start | bytes 110600 | tf_op jit(solution)/shard_map/ppermute | solution.py:345
  5.1 10.5 %collective-permute-start.2 = (bf16[144,128]{1,0:T(8,128)(2,1)}, bf16[144,128]{1,0:T(8,128)(2,1)S(1)}, u32[]{:S(2)}, u32[]{:S(2)}) collective-permute-start(bf16[144,128]{1,0:T(8,128)(2,1)} %get-tuple-element.28.refs_0_), channel_id=1, source_target_pairs={{0,249},{1,248},{2,251},{3,250},{4,253},{5,252},{6,255},{7,254},{8... | collective-permute-start | bytes 110600 | tf_op jit(solution)/shard_map/ppermute | solution.py:345
  10.4 7.9 %collective-permute-start = (bf16[272,128]{1,0:T(8,128)(2,1)}, bf16[272,128]{1,0:T(8,128)(2,1)S(1)}, u32[]{:S(2)}, u32[]{:S(2)}) collective-permute-start(bf16[272,128]{1,0:T(8,128)(2,1)} %get-tuple-element.29.refs_1_), channel_id=1, source_target_pairs={{0,1},{1,0},{2,3},{3,2},{4,5},{5,4},{6,7},{7,6},{8,9},{9,8},{10,11... | collective-permute-start | bytes 208904 | tf_op jit(solution)/shard_map/ppermute | solution.py:345
  18.3 12.1 %collective-permute-start.3 = (bf16[4,144,128]{2,1,0:T(8,128)(2,1)S(1)}, bf16[4,144,128]{2,1,0:T(8,128)(2,1)S(1)}, u32[]{:S(2)}, u32[]{:S(2)}) collective-permute-start(bf16[4,144,128]{2,1,0:T(8,128)(2,1)S(1)} %stack_first.1.refs_1_.refs_0_.refs_2_), channel_id=1, source_target_pairs={{0,6},{1,7},{2,0},{3,1},{4,2},{5,3},{6,4},{7,5},{8,14},{9,15},{10,... | collective-permute-start | bytes 442376 | tf_op jit(solution)/shard_map/ppermute | solution.py:345
  21.1 9.4 %collective-permute-start.4 = (bf16[4,144,128]{2,1,0:T(8,128)(2,1)S(1)}, bf16[4,144,128]{2,1,0:T(8,128)(2,1)S(1)}, u32[]{:S(2)}, u32[]{:S(2)}) collective-permute-start(bf16[4,144,128]{2,1,0:T(8,128)(2,1)S(1)} %stack_first.1.refs_1_.refs_0_.refs_2_), channel_id=1, source_target_pairs={{0,4},{1,5},{2,6},{3,7},{4,0},{5,1},{6,2},{7,3},{8,12},{9,13},{10,... | collective-permute-start | bytes 442376 | tf_op jit(solution)/shard_map/ppermute | solution.py:345
  21.4 10.0 %collective-permute-start.5 = (bf16[4,144,128]{2,1,0:T(8,128)(2,1)S(1)}, bf16[4,144,128]{2,1,0:T(8,128)(2,1)S(1)}, u32[]{:S(2)}, u32[]{:S(2)}) collective-permute-start(bf16[4,144,128]{2,1,0:T(8,128)(2,1)S(1)} %stack_first.1.refs_1_.refs_0_.refs_2_), channel_id=1, source_target_pairs={{0,2},{1,3},{2,4},{3,5},{4,6},{5,7},{6,0},{7,1},{8,10},{9,11},{10,... | collective-permute-start | bytes 442376 | tf_op jit(solution)/shard_map/ppermute | solution.py:345
  22.1 6.0 %copy-start.4 = (f32[2,8,128]{2,1,0:T(8,128)S(1)}, f32[2,8,128]{2,1,0:T(8,128)}, u32[]{:S(2)}) copy-start(f32[2,8,128]{2,1,0:T(8,128)} %refs_14_.3) | copy-start | bytes 24580
  22.2 6.0 %collective-permute-start.6 = (bf16[2,144,128]{2,1,0:T(8,128)(2,1)S(1)}, bf16[2,144,128]{2,1,0:T(8,128)(2,1)S(1)}, u32[]{:S(2)}, u32[]{:S(2)}) collective-permute-start(bf16[2,144,128]{2,1,0:T(8,128)(2,1)S(1)} %slice.24), channel_id=1, source_target_pairs={{0,8},{1,9},{2,10},{3,11},{4,12},{5,13},{6,14},{7,15},{8,0},{9,1},... | collective-permute-start | bytes 221192 | tf_op jit(solution)/shard_map/ppermute | solution.py:345
  30.4 2.7 %collective-permute-start.7 = (bf16[2,144,128]{2,1,0:T(8,128)(2,1)S(1)}, bf16[2,144,128]{2,1,0:T(8,128)(2,1)S(1)}, u32[]{:S(2)}, u32[]{:S(2)}) collective-permute-start(bf16[2,144,128]{2,1,0:T(8,128)(2,1)S(1)} %pair_first.1), channel_id=1, source_target_pairs={{0,8},{1,9},{2,10},{3,11},{4,12},{5,13},{6,14},{7,15},{8,0},{9,1},... | collective-permute-start | bytes 221192 | tf_op jit(solution)/shard_map/ppermute | solution.py:345
  30.5 2.6 %collective-permute-start.8 = (bf16[2,144,128]{2,1,0:T(8,128)(2,1)S(1)}, bf16[2,144,128]{2,1,0:T(8,128)(2,1)S(1)}, u32[]{:S(2)}, u32[]{:S(2)}) collective-permute-start(bf16[2,144,128]{2,1,0:T(8,128)(2,1)S(1)} %slice.25), channel_id=1, source_target_pairs={{0,8},{1,9},{2,10},{3,11},{4,12},{5,13},{6,14},{7,15},{8,0},{9,1},... | collective-permute-start | bytes 221192 | tf_op jit(solution)/shard_map/ppermute | solution.py:345
  31.5 2.4 %collective-permute-start.9 = (bf16[2,144,128]{2,1,0:T(8,128)(2,1)S(1)}, bf16[2,144,128]{2,1,0:T(8,128)(2,1)S(1)}, u32[]{:S(2)}, u32[]{:S(2)}) collective-permute-start(bf16[2,144,128]{2,1,0:T(8,128)(2,1)S(1)} %slice.26), channel_id=1, source_target_pairs={{0,8},{1,9},{2,10},{3,11},{4,12},{5,13},{6,14},{7,15},{8,0},{9,1},... | collective-permute-start | bytes 221192 | tf_op jit(solution)/shard_map/ppermute | solution.py:345
  37.7 9.4 %collective-permute-start.10 = (bf16[128,128]{1,0:T(8,128)(2,1)S(1)}, bf16[128,128]{1,0:T(8,128)(2,1)S(1)}, u32[]{:S(2)}, u32[]{:S(2)}) collective-permute-start(bf16[128,128]{1,0:T(8,128)(2,1)S(1)} %get-tuple-element.37.refs_2_.refs_8_.refs_0_), channel_id=1, source_target_pairs={{0,1},{1,0},{2,3},{3,2},{4,5},{5,4},{6,7},{7,6},{8,9},{9,8},{10,11... | collective-permute-start | bytes 98312 | tf_op jit(solution)/shard_map/ppermute | solution.py:345
  40.0 7.1 %collective-permute-start.11 = (bf16[128,128]{1,0:T(8,128)(2,1)S(1)}, bf16[128,128]{1,0:T(8,128)(2,1)S(1)}, u32[]{:S(2)}, u32[]{:S(2)}) collective-permute-start(bf16[128,128]{1,0:T(8,128)(2,1)S(1)} %get-tuple-element.37.refs_2_.refs_8_.refs_0_), channel_id=1, source_target_pairs={{0,248},{1,249},{2,250},{3,251},{4,252},{5,253},{6,254},{7,255},{8... | collective-permute-start | bytes 98312 | tf_op jit(solution)/shard_map/ppermute | solution.py:345
  40.1 7.0 %collective-permute-start.12 = (bf16[128,128]{1,0:T(8,128)(2,1)S(1)}, bf16[128,128]{1,0:T(8,128)(2,1)S(1)}, u32[]{:S(2)}, u32[]{:S(2)}) collective-permute-start(bf16[128,128]{1,0:T(8,128)(2,1)S(1)} %get-tuple-element.37.refs_2_.refs_8_.refs_0_), channel_id=1, source_target_pairs={{0,249},{1,248},{2,251},{3,250},{4,253},{5,252},{6,255},{7,254},{8... | collective-permute-start | bytes 98312 | tf_op jit(solution)/shard_map/ppermute | solution.py:345
  47.2 11.0 %collective-permute-start.13 = (bf16[4,128,128]{2,1,0:T(8,128)(2,1)S(1)}, bf16[4,128,128]{2,1,0:T(8,128)(2,1)S(1)}, u32[]{:S(2)}, u32[]{:S(2)}) collective-permute-start(bf16[4,128,128]{2,1,0:T(8,128)(2,1)S(1)} %stack_second.1.refs_2_.refs_0_.refs_8_.refs_16_), channel_id=1, source_target_pairs={{0,6},{1,7},{2,0},{3,1},{4,2},{5,3},{6,4},{7,5},{8,14},{9,15},{10,... | collective-permute-start | bytes 393224 | tf_op jit(solution)/shard_map/ppermute | solution.py:345
  48.0 10.3 %collective-permute-start.14 = (bf16[4,128,128]{2,1,0:T(8,128)(2,1)S(1)}, bf16[4,128,128]{2,1,0:T(8,128)(2,1)S(1)}, u32[]{:S(2)}, u32[]{:S(2)}) collective-permute-start(bf16[4,128,128]{2,1,0:T(8,128)(2,1)S(1)} %stack_second.1.refs_2_.refs_0_.refs_8_.refs_16_), channel_id=1, source_target_pairs={{0,4},{1,5},{2,6},{3,7},{4,0},{5,1},{6,2},{7,3},{8,12},{9,13},{10,... | collective-permute-start | bytes 393224 | tf_op jit(solution)/shard_map/ppermute | solution.py:345
  49.4 9.7 %collective-permute-start.15 = (bf16[4,128,128]{2,1,0:T(8,128)(2,1)S(1)}, bf16[4,128,128]{2,1,0:T(8,128)(2,1)S(1)}, u32[]{:S(2)}, u32[]{:S(2)}) collective-permute-start(bf16[4,128,128]{2,1,0:T(8,128)(2,1)S(1)} %stack_second.1.refs_2_.refs_0_.refs_8_.refs_16_), channel_id=1, source_target_pairs={{0,2},{1,3},{2,4},{3,5},{4,6},{5,7},{6,0},{7,1},{8,10},{9,11},{10,... | collective-permute-start | bytes 393224 | tf_op jit(solution)/shard_map/ppermute | solution.py:345
  49.4 7.6 %collective-permute-start.16 = (bf16[2,128,128]{2,1,0:T(8,128)(2,1)S(1)}, bf16[2,128,128]{2,1,0:T(8,128)(2,1)S(1)}, u32[]{:S(2)}, u32[]{:S(2)}) collective-permute-start(bf16[2,128,128]{2,1,0:T(8,128)(2,1)S(1)} %slice.27), channel_id=1, source_target_pairs={{0,8},{1,9},{2,10},{3,11},{4,12},{5,13},{6,14},{7,15},{8,0},{9,1},... | collective-permute-start | bytes 196616 | tf_op jit(solution)/shard_map/ppermute | solution.py:345
  58.2 1.6 %collective-permute-start.17 = (bf16[2,128,128]{2,1,0:T(8,128)(2,1)S(1)}, bf16[2,128,128]{2,1,0:T(8,128)(2,1)S(1)}, u32[]{:S(2)}, u32[]{:S(2)}) collective-permute-start(bf16[2,128,128]{2,1,0:T(8,128)(2,1)S(1)} %pair_second.1), channel_id=1, source_target_pairs={{0,8},{1,9},{2,10},{3,11},{4,12},{5,13},{6,14},{7,15},{8,0},{9,1},... | collective-permute-start | bytes 196616 | tf_op jit(solution)/shard_map/ppermute | solution.py:345
  58.3 1.7 %collective-permute-start.18 = (bf16[2,128,128]{2,1,0:T(8,128)(2,1)S(1)}, bf16[2,128,128]{2,1,0:T(8,128)(2,1)S(1)}, u32[]{:S(2)}, u32[]{:S(2)}) collective-permute-start(bf16[2,128,128]{2,1,0:T(8,128)(2,1)S(1)} %slice.28), channel_id=1, source_target_pairs={{0,8},{1,9},{2,10},{3,11},{4,12},{5,13},{6,14},{7,15},{8,0},{9,1},... | collective-permute-start | bytes 196616 | tf_op jit(solution)/shard_map/ppermute | solution.py:345
  59.1 1.6 %collective-permute-start.19 = (bf16[2,128,128]{2,1,0:T(8,128)(2,1)S(1)}, bf16[2,128,128]{2,1,0:T(8,128)(2,1)S(1)}, u32[]{:S(2)}, u32[]{:S(2)}) collective-permute-start(bf16[2,128,128]{2,1,0:T(8,128)(2,1)S(1)} %slice.29), channel_id=1, source_target_pairs={{0,8},{1,9},{2,10},{3,11},{4,12},{5,13},{6,14},{7,15},{8,0},{9,1},... | collective-permute-start | bytes 196616 | tf_op jit(solution)/shard_map/ppermute | solution.py:345
  64.4 6.8 %collective-permute-start.20 = (f32[2,16,128]{2,1,0:T(8,128)S(1)}, f32[2,16,128]{2,1,0:T(8,128)S(1)}, u32[]{:S(2)}, u32[]{:S(2)}) collective-permute-start(f32[2,16,128]{2,1,0:T(8,128)S(1)} %second_rest.1.refs_2_.refs_5_), channel_id=1, source_target_pairs={{0,6},{1,7},{2,0},{3,1},{4,2},{5,3},{6,4},{7,5},{8,14},{9,15},{10,... | collective-permute-start | bytes 49160 | tf_op jit(solution)/shard_map/ppermute | solution.py:345
  66.6 4.6 %collective-permute-start.21 = (f32[2,16,128]{2,1,0:T(8,128)S(1)}, f32[2,16,128]{2,1,0:T(8,128)S(1)}, u32[]{:S(2)}, u32[]{:S(2)}) collective-permute-start(f32[2,16,128]{2,1,0:T(8,128)S(1)} %second_rest.1.refs_2_.refs_5_), channel_id=1, source_target_pairs={{0,4},{1,5},{2,6},{3,7},{4,0},{5,1},{6,2},{7,3},{8,12},{9,13},{10,... | collective-permute-start | bytes 49160 | tf_op jit(solution)/shard_map/ppermute | solution.py:345
  68.0 3.9 %collective-permute-start.22 = (f32[2,16,128]{2,1,0:T(8,128)S(1)}, f32[2,16,128]{2,1,0:T(8,128)S(1)}, u32[]{:S(2)}, u32[]{:S(2)}) collective-permute-start(f32[2,16,128]{2,1,0:T(8,128)S(1)} %second_rest.1.refs_2_.refs_5_), channel_id=1, source_target_pairs={{0,2},{1,3},{2,4},{3,5},{4,6},{5,7},{6,0},{7,1},{8,10},{9,11},{10,... | collective-permute-start | bytes 49160 | tf_op jit(solution)/shard_map/ppermute | solution.py:345
  73.2 2.5 %collective-permute-start.23 = (f32[32,512]{1,0:T(8,128)S(1)}, f32[32,512]{1,0:T(8,128)S(1)}, u32[]{:S(2)}, u32[]{:S(2)}) collective-permute-start(f32[32,512]{1,0:T(8,128)S(1)} %get-tuple-element.51), channel_id=1, source_target_pairs={{0,8},{1,9},{2,10},{3,11},{4,12},{5,13},{6,14},{7,15},{8,0},{9,1},... | collective-permute-start | bytes 196616 | tf_op jit(solution)/shard_map/ppermute | solution.py:345
  75.6 2.8 %collective-permute-start.26 = (bf16[32,512]{1,0:T(8,128)(2,1)S(1)}, bf16[32,512]{1,0:T(8,128)(2,1)S(1)}, u32[]{:S(2)}, u32[]{:S(2)}) collective-permute-start(bf16[32,512]{1,0:T(8,128)(2,1)S(1)} %get-tuple-element.52), channel_id=1, source_target_pairs={{0,192},{1,193},{2,194},{3,195},{4,196},{5,197},{6,198},{7,199},{8... | collective-permute-start | bytes 98312 | tf_op jit(solution)/shard_map/ppermute | solution.py:345
  75.7 4.4 %collective-permute-start.25 = (bf16[32,512]{1,0:T(8,128)(2,1)S(1)}, bf16[32,512]{1,0:T(8,128)(2,1)S(1)}, u32[]{:S(2)}, u32[]{:S(2)}) collective-permute-start(bf16[32,512]{1,0:T(8,128)(2,1)S(1)} %get-tuple-element.52), channel_id=1, source_target_pairs={{0,128},{1,129},{2,130},{3,131},{4,132},{5,133},{6,134},{7,135},{8... | collective-permute-start | bytes 98312 | tf_op jit(solution)/shard_map/ppermute | solution.py:345
  76.0 5.2 %collective-permute-start.24 = (bf16[32,512]{1,0:T(8,128)(2,1)S(1)}, bf16[32,512]{1,0:T(8,128)(2,1)S(1)}, u32[]{:S(2)}, u32[]{:S(2)}) collective-permute-start(bf16[32,512]{1,0:T(8,128)(2,1)S(1)} %get-tuple-element.52), channel_id=1, source_target_pairs={{0,64},{1,65},{2,66},{3,67},{4,68},{5,69},{6,70},{7,71},{8,72},{9,... | collective-permute-start | bytes 98312 | tf_op jit(solution)/shard_map/ppermute | solution.py:345
  81.3 4.7 %collective-permute-start.29 = (bf16[32,512]{1,0:T(8,128)(2,1)S(1)}, bf16[32,512]{1,0:T(8,128)(2,1)S(1)}, u32[]{:S(2)}, u32[]{:S(2)}) collective-permute-start(bf16[32,512]{1,0:T(8,128)(2,1)S(1)} %fusion), channel_id=1, source_target_pairs={{0,48},{1,49},{2,50},{3,51},{4,52},{5,53},{6,54},{7,55},{8,56},{9,... | collective-permute-start | bytes 98312 | tf_op jit(solution)/shard_map/ppermute | solution.py:345
  82.4 4.2 %collective-permute-start.28 = (bf16[32,512]{1,0:T(8,128)(2,1)S(1)}, bf16[32,512]{1,0:T(8,128)(2,1)S(1)}, u32[]{:S(2)}, u32[]{:S(2)}) collective-permute-start(bf16[32,512]{1,0:T(8,128)(2,1)S(1)} %fusion), channel_id=1, source_target_pairs={{0,32},{1,33},{2,34},{3,35},{4,36},{5,37},{6,38},{7,39},{8,40},{9,... | collective-permute-start | bytes 98312 | tf_op jit(solution)/shard_map/ppermute | solution.py:345
  82.4 4.2 %collective-permute-start.27 = (bf16[32,512]{1,0:T(8,128)(2,1)S(1)}, bf16[32,512]{1,0:T(8,128)(2,1)S(1)}, u32[]{:S(2)}, u32[]{:S(2)}) collective-permute-start(bf16[32,512]{1,0:T(8,128)(2,1)S(1)} %fusion), channel_id=1, source_target_pairs={{0,16},{1,17},{2,18},{3,19},{4,20},{5,21},{6,22},{7,23},{8,24},{9,... | collective-permute-start | bytes 98312 | tf_op jit(solution)/shard_map/ppermute | solution.py:345
  86.6 3.9 %collective-permute-start.30 = (f32[32,512]{1,0:T(8,128)S(1)}, f32[32,512]{1,0:T(8,128)S(1)}, u32[]{:S(2)}, u32[]{:S(2)}) collective-permute-start(f32[32,512]{1,0:T(8,128)S(1)} %add_add_fusion.refs_9_), channel_id=1, source_target_pairs={{0,8},{1,9},{2,10},{3,11},{4,12},{5,13},{6,14},{7,15},{8,0},{9,1},... | collective-permute-start | bytes 196616 | tf_op jit(solution)/shard_map/ppermute | solution.py:345
  (7 other events, 24.9 us)

commit v3 on v2

--- a/solution.py
+++ b/solution.py
@@ -226,8 +226,7 @@
 def partner_body(shift_ref, near_ref, ya, yb, ca, cb, na, nb, ga, gb, here_s):
     here_of(near_ref, 1, here_s)
 
-    @pl.loop(0, 2)
-    def _(h):
+    for h in range(2):
         basis_half(h, shift_ref, ya, ca, na, ga, here_s)
         basis_half(h, shift_ref, yb, cb, nb, gb, here_s)
 

time: 107 us -> 107 us (level)
  transfers between devices with their start and end apart: 31 -> 31, of which waited for: 12 -> 11; matrix products, arithmetic and copies ran while one was open for 0% -> 0% of each run, Pallas kernels for 16% -> 16%
where the time goes in v3:
time: 107 us
  starting transfers between devices  47.7 us (45%)
  Pallas kernels  28.9 us (27%)
  blocking collectives  14.8 us (14%)
  waiting for transfers between devices  12.7 us (12%)
  local copies, waits for them, and re-layouts  1.6 us (1%)
    ppermute x31, starting transfers between devices, move(): return lax.ppermute(x, AXES, pairs(lax.axis_size('slab'), target))  47.7 us
    pallas_call x22, Pallas kernels, call(): pl.pallas_call(lambda *refs: body(*refs[:n], *refs[n + m:]), out_shape=ou...  28.9 us
    all_to_all x1, blocking collectives, shards(): partial = lax.all_to_all(partial, 'kgrp', 0, 0)  14.8 us
    ppermute x31, waiting for transfers between devices, move(): return lax.ppermute(x, AXES, pairs(lax.axis_size('slab'), target))  12.7 us
  transfers between devices with their start and end apart: 31, of which 11 were waited for; matrix products, arithmetic and copies ran while one was open for 0% of the time, Pallas kernels for 16%

profile of v3, /device:TPU:1, one launch (start us, length us, event | category | flops | bytes accessed | tf_op | source)
XLA Modules:
  0.0 106.9 jit_solution(18241714321183210470)
XLA Ops:
  0.6 1.5 %pack.1 = (bf16[144,128]{1,0:T(8,128)(2,1)}, bf16[272,128]{1,0:T(8,128)(2,1)}) custom-call(bf16[128,128]{1,0:T(8,128)(2,1)} %refs_0_.2, f32[3,128]{1,0:T(4,128)} %refs_1_.3, s32[64,128]{1,0:T(8,128)} %bitcast.6, s32[1,128]{1,0:T(1,128)} %bitcast.7), custom_call_target="tpu_custom_call" | custom-call | bytes 1048576 | tf_op jit(solution)/shard_map/pack/pallas_call | solution.py:57
  2.1 3.0 %collective-permute-start.1 = (bf16[144,128]{1,0:T(8,128)(2,1)}, bf16[144,128]{1,0:T(8,128)(2,1)S(1)}, u32[]{:S(2)}, u32[]{:S(2)}) collective-permute-start(bf16[144,128]{1,0:T(8,128)(2,1)} %get-tuple-element.28.refs_0_), channel_id=1, source_target_pairs={{0,248},{1,249},{2,250},{3,251},{4,252},{5,253},{6,254},{7,255},{8... | collective-permute-start | bytes 110600 | tf_op jit(solution)/shard_map/ppermute | solution.py:344
  5.1 5.3 %collective-permute-start.2 = (bf16[144,128]{1,0:T(8,128)(2,1)}, bf16[144,128]{1,0:T(8,128)(2,1)S(1)}, u32[]{:S(2)}, u32[]{:S(2)}) collective-permute-start(bf16[144,128]{1,0:T(8,128)(2,1)} %get-tuple-element.28.refs_0_), channel_id=1, source_target_pairs={{0,249},{1,248},{2,251},{3,250},{4,253},{5,252},{6,255},{7,254},{8... | collective-permute-start | bytes 110600 | tf_op jit(solution)/shard_map/ppermute | solution.py:344
  13.9 1.7 %counts.1 = (f32[6,128,128]{2,1,0:T(8,128)S(1)}, f32[6,128,128]{2,1,0:T(8,128)S(1)}, f32[6,128,128]{2,1,0:T(8,128)S(1)}, f32[6,128,128]{2,1,0:T(8,128)S(1)}) custom-call(s32[16]{0:T(128)S(1)} %get-tuple-element.27.refs_0_, bf16[272,128]{1,0:T(8,128)(2,1)S(1)} %copy-done.6), custom_call_target="tpu_custom_call" | custom-call | flops 1000000000 | bytes 1048576 | tf_op jit(solution)/shard_map/counts/pallas_call | solution.py:57
  15.7 2.6 %collective-permute-done.refs_1_ = bf16[272,128]{1,0:T(8,128)(2,1)S(1)} collective-permute-done((bf16[272,128]{1,0:T(8,128)(2,1)}, bf16[272,128]{1,0:T(8,128)(2,1)S(1)}, u32[]{:S(2)}, u32[]{:S(2)}) %collective-permute-start) | collective-permute-done | bytes 69664 | tf_op jit(solution)/shard_map/ppermute | solution.py:344
  18.3 2.8 %collective-permute-start.3 = (bf16[4,144,128]{2,1,0:T(8,128)(2,1)S(1)}, bf16[4,144,128]{2,1,0:T(8,128)(2,1)S(1)}, u32[]{:S(2)}, u32[]{:S(2)}) collective-permute-start(bf16[4,144,128]{2,1,0:T(8,128)(2,1)S(1)} %stack_first.1.refs_1_.refs_0_.refs_2_), channel_id=1, source_target_pairs={{0,6},{1,7},{2,0},{3,1},{4,2},{5,3},{6,4},{7,5},{8,14},{9,15},{10,... | collective-permute-start | bytes 442376 | tf_op jit(solution)/shard_map/ppermute | solution.py:344
  22.2 4.3 %collective-permute-start.6 = (bf16[2,144,128]{2,1,0:T(8,128)(2,1)S(1)}, bf16[2,144,128]{2,1,0:T(8,128)(2,1)S(1)}, u32[]{:S(2)}, u32[]{:S(2)}) collective-permute-start(bf16[2,144,128]{2,1,0:T(8,128)(2,1)S(1)} %slice.24), channel_id=1, source_target_pairs={{0,8},{1,9},{2,10},{3,11},{4,12},{5,13},{6,14},{7,15},{8,0},{9,1},... | collective-permute-start | bytes 221192 | tf_op jit(solution)/shard_map/ppermute | solution.py:344
  26.4 1.7 %partner_counts.1 = (f32[6,128,128]{2,1,0:T(8,128)S(1)}, f32[6,128,128]{2,1,0:T(8,128)S(1)}, f32[6,128,128]{2,1,0:T(8,128)S(1)}, f32[6,128,128]{2,1,0:T(8,128)S(1)}) custom-call(s32[16]{0:T(128)S(1)} %get-tuple-element.27.refs_0_, bf16[272,128]{1,0:T(8,128)(2,1)S(1)} %collective-permute-done.refs_1_), custom_call_target="tpu_custom_call" | custom-call | flops 1000000000 | bytes 1048576 | tf_op jit(solution)/shard_map/partner_counts/pallas_call | solution.py:57
  28.2 2.1 %first_0.1 = (bf16[1024,768]{1,0:T(8,128)(2,1)S(1)}, f32[128,128]{1,0:T(8,128)S(1)}) custom-call(f32[3]{0:T(128)S(1)} %get-tuple-element.31.refs_0_, bf16[4,144,128]{2,1,0:T(8,128)(2,1)S(1)} %stack_first.1.refs_1_.refs_0_.refs_2_, bf16[2,144,128]{2,1,0:T(8,128)(2,1)S(1)} %collective-permute-done.6.refs_2_.refs_4_, ...), custom_call_target="tpu_custom_call" | custom-call | flops 1000000000 | bytes 1048576 | tf_op jit(solution)/shard_map/first_0/pallas_call | solution.py:57
  31.5 1.5 %collective-permute-start.9 = (bf16[2,144,128]{2,1,0:T(8,128)(2,1)S(1)}, bf16[2,144,128]{2,1,0:T(8,128)(2,1)S(1)}, u32[]{:S(2)}, u32[]{:S(2)}) collective-permute-start(bf16[2,144,128]{2,1,0:T(8,128)(2,1)S(1)} %slice.26), channel_id=1, source_target_pairs={{0,8},{1,9},{2,10},{3,11},{4,12},{5,13},{6,14},{7,15},{8,0},{9,1},... | collective-permute-start | bytes 221192 | tf_op jit(solution)/shard_map/ppermute | solution.py:344
  33.9 3.8 %first_rest.1 = (bf16[1024,768]{1,0:T(8,128)(2,1)S(1)}, bf16[1024,768]{1,0:T(8,128)(2,1)S(1)}, bf16[1024,768]{1,0:T(8,128)(2,1)S(1)}, bf16[128,128]{1,0:T(8,128)(2,1)S(1)}) custom-call(f32[3]{0:T(128)S(1)} %get-tuple-element.31.refs_0_, bf16[4,144,128]{2,1,0:T(8,128)(2,1)S(1)} %stack_first.1.refs_1_.refs_0_.refs_2_, ...), custom_call_target="tpu_custom_call" | custom-call | flops 1000000000 | bytes 1048576 | tf_op jit(solution)/shard_map/first_rest/pallas_call | solution.py:57
  37.7 2.4 %collective-permute-start.10 = (bf16[128,128]{1,0:T(8,128)(2,1)S(1)}, bf16[128,128]{1,0:T(8,128)(2,1)S(1)}, u32[]{:S(2)}, u32[]{:S(2)}) collective-permute-start(bf16[128,128]{1,0:T(8,128)(2,1)S(1)} %get-tuple-element.37.refs_2_.refs_8_.refs_0_), channel_id=1, source_target_pairs={{0,1},{1,0},{2,3},{3,2},{4,5},{5,4},{6,7},{7,6},{8,9},{9,8},{10,11... | collective-permute-start | bytes 98312 | tf_op jit(solution)/shard_map/ppermute | solution.py:344
  40.1 3.6 %collective-permute-start.12 = (bf16[128,128]{1,0:T(8,128)(2,1)S(1)}, bf16[128,128]{1,0:T(8,128)(2,1)S(1)}, u32[]{:S(2)}, u32[]{:S(2)}) collective-permute-start(bf16[128,128]{1,0:T(8,128)(2,1)S(1)} %get-tuple-element.37.refs_2_.refs_8_.refs_0_), channel_id=1, source_target_pairs={{0,249},{1,248},{2,251},{3,250},{4,253},{5,252},{6,255},{7,254},{8... | collective-permute-start | bytes 98312 | tf_op jit(solution)/shard_map/ppermute | solution.py:344
  44.9 2.0 %partner_0.1 = (bf16[1024,768]{1,0:T(8,128)(2,1)S(1)}, bf16[1024,768]{1,0:T(8,128)(2,1)S(1)}) custom-call(f32[3]{0:T(128)S(1)} %get-tuple-element.31.refs_0_, bf16[4,144,128]{2,1,0:T(8,128)(2,1)S(1)} %stack_first.1.refs_1_.refs_0_.refs_2_, bf16[4,144,128]{2,1,0:T(8,128)(2,1)S(1)} %stack_first.1.refs_1_.refs_0_.refs_2_, ...), custom_call_target="tpu_custom_call" | custom-call | flops 1000000000 | bytes 1048576 | tf_op jit(solution)/shard_map/partner_0/pallas_call | solution.py:57
  47.8 1.4 %collective-permute-start.14 = (bf16[4,128,128]{2,1,0:T(8,128)(2,1)S(1)}, bf16[4,128,128]{2,1,0:T(8,128)(2,1)S(1)}, u32[]{:S(2)}, u32[]{:S(2)}) collective-permute-start(bf16[4,128,128]{2,1,0:T(8,128)(2,1)S(1)} %stack_second.1.refs_2_.refs_0_.refs_8_.refs_16_), channel_id=1, source_target_pairs={{0,4},{1,5},{2,6},{3,7},{4,0},{5,1},{6,2},{7,3},{8,12},{9,13},{10,... | collective-permute-start | bytes 393224 | tf_op jit(solution)/shard_map/ppermute | solution.py:344
  49.2 4.4 %collective-permute-start.16 = (bf16[2,128,128]{2,1,0:T(8,128)(2,1)S(1)}, bf16[2,128,128]{2,1,0:T(8,128)(2,1)S(1)}, u32[]{:S(2)}, u32[]{:S(2)}) collective-permute-start(bf16[2,128,128]{2,1,0:T(8,128)(2,1)S(1)} %slice.27), channel_id=1, source_target_pairs={{0,8},{1,9},{2,10},{3,11},{4,12},{5,13},{6,14},{7,15},{8,0},{9,1},... | collective-permute-start | bytes 196616 | tf_op jit(solution)/shard_map/ppermute | solution.py:344
  54.8 2.0 %partner_2.1 = (bf16[1024,768]{1,0:T(8,128)(2,1)S(1)}, bf16[1024,768]{1,0:T(8,128)(2,1)S(1)}) custom-call(f32[3]{0:T(128)S(1)} %get-tuple-element.31.refs_0_, bf16[4,144,128]{2,1,0:T(8,128)(2,1)S(1)} %stack_first.1.refs_1_.refs_0_.refs_2_, bf16[4,144,128]{2,1,0:T(8,128)(2,1)S(1)} %collective-permute-done.4.refs_3_.refs_2_.refs_0_, ...), custom_call_target="tpu_custom_call" | custom-call | flops 1000000000 | bytes 1048576 | tf_op jit(solution)/shard_map/partner_2/pallas_call | solution.py:57
  60.7 3.6 %second_rest.1.refs_2_.refs_5_ = f32[2,16,128]{2,1,0:T(8,128)S(1)} custom-call(s32[16]{0:T(128)S(1)} %get-tuple-element.27.refs_0_, bf16[4,128,128]{2,1,0:T(8,128)(2,1)S(1)} %collective-permute-done.13.refs_0_.refs_1_, bf16[4,128,128]{2,1,0:T(8,128)(2,1)S(1)} %collective-permute-done.14.refs_2_, bf16[4,128,128]{2,1,0:T(8,128)(2,1)S(1)} %collective-permute-done.15.refs_3_, ...), custom_call_target="tpu_custom_call" | custom-call | flops 1000000000 | bytes 1048576 | tf_op jit(solution)/shard_map/second_rest/pallas_call | solution.py:57
  64.4 2.0 %collective-permute-start.20 = (f32[2,16,128]{2,1,0:T(8,128)S(1)}, f32[2,16,128]{2,1,0:T(8,128)S(1)}, u32[]{:S(2)}, u32[]{:S(2)}) collective-permute-start(f32[2,16,128]{2,1,0:T(8,128)S(1)} %second_rest.1.refs_2_.refs_5_), channel_id=1, source_target_pairs={{0,6},{1,7},{2,0},{3,1},{4,2},{5,3},{6,4},{7,5},{8,14},{9,15},{10,... | collective-permute-start | bytes 49160 | tf_op jit(solution)/shard_map/ppermute | solution.py:344
  66.4 1.2 %collective-permute-start.21 = (f32[2,16,128]{2,1,0:T(8,128)S(1)}, f32[2,16,128]{2,1,0:T(8,128)S(1)}, u32[]{:S(2)}, u32[]{:S(2)}) collective-permute-start(f32[2,16,128]{2,1,0:T(8,128)S(1)} %second_rest.1.refs_2_.refs_5_), channel_id=1, source_target_pairs={{0,4},{1,5},{2,6},{3,7},{4,0},{5,1},{6,2},{7,3},{8,12},{9,13},{10,... | collective-permute-start | bytes 49160 | tf_op jit(solution)/shard_map/ppermute | solution.py:344
  68.4 1.2 %phases_2.1.refs_3_ = bf16[2048,256]{1,0:T(8,128)(2,1)S(1)} custom-call(bf16[4,144,128]{2,1,0:T(8,128)(2,1)S(1)} %collective-permute-done.4.refs_3_.refs_2_.refs_0_, bf16[1024,24]{1,0:T(8,128)(2,1)S(1)} %modes.1.refs_1_, f32[2,16,128]{2,1,0:T(8,128)S(1)} %second_rest.1.refs_2_.refs_5_), custom_call_target="tpu_custom_call" | custom-call | flops 1000000000 | bytes 1048576 | tf_op jit(solution)/shard_map/phases_2/pallas_call | solution.py:57
  69.6 1.2 %phases_3.1.refs_4_ = bf16[2048,256]{1,0:T(8,128)(2,1)S(1)} custom-call(bf16[4,144,128]{2,1,0:T(8,128)(2,1)S(1)} %collective-permute-done.5.refs_4_.refs_3_.refs_0_, bf16[1024,24]{1,0:T(8,128)(2,1)S(1)} %modes.1.refs_1_, f32[2,16,128]{2,1,0:T(8,128)S(1)} %second_rest.1.refs_2_.refs_5_), custom_call_target="tpu_custom_call" | custom-call | flops 1000000000 | bytes 1048576 | tf_op jit(solution)/shard_map/phases_3/pallas_call | solution.py:57
  71.7 1.3 %structure.1 = (f32[32,512]{1,0:T(8,128)S(1)}, f32[32,512]{1,0:T(8,128)S(1)}) custom-call(s32[1,512]{1,0:T(1,128)S(1)} %get-tuple-element.49.refs_0_, bf16[2048,256]{1,0:T(8,128)(2,1)S(1)} %phases_0.1.refs_5_.refs_3_.refs_1_, bf16[2048,256]{1,0:T(8,128)(2,1)S(1)} %phases_1.1.refs_4_.refs_2_, bf16[2048,256]{1,0:T(8,128)(2,1)S(1)} %phases_2.1.refs_3_, ...), custom_call_target="tpu_custom_call" | custom-call | flops 100000000 | bytes 1048576 | tf_op jit(solution)/shard_map/structure/pallas_call | solution.py:57
  73.0 1.4 %collective-permute-start.23 = (f32[32,512]{1,0:T(8,128)S(1)}, f32[32,512]{1,0:T(8,128)S(1)}, u32[]{:S(2)}, u32[]{:S(2)}) collective-permute-start(f32[32,512]{1,0:T(8,128)S(1)} %get-tuple-element.51), channel_id=1, source_target_pairs={{0,8},{1,9},{2,10},{3,11},{4,12},{5,13},{6,14},{7,15},{8,0},{9,1},... | collective-permute-start | bytes 196616 | tf_op jit(solution)/shard_map/ppermute | solution.py:344
  75.4 1.4 %collective-permute-start.24 = (bf16[32,512]{1,0:T(8,128)(2,1)S(1)}, bf16[32,512]{1,0:T(8,128)(2,1)S(1)}, u32[]{:S(2)}, u32[]{:S(2)}) collective-permute-start(bf16[32,512]{1,0:T(8,128)(2,1)S(1)} %get-tuple-element.52), channel_id=1, source_target_pairs={{0,64},{1,65},{2,66},{3,67},{4,68},{5,69},{6,70},{7,71},{8,72},{9,... | collective-permute-start | bytes 98312 | tf_op jit(solution)/shard_map/ppermute | solution.py:344
  76.8 1.3 %collective-permute-done.26 = bf16[32,512]{1,0:T(8,128)(2,1)S(1)} collective-permute-done((bf16[32,512]{1,0:T(8,128)(2,1)S(1)}, bf16[32,512]{1,0:T(8,128)(2,1)S(1)}, u32[]{:S(2)}, u32[]{:S(2)}) %collective-permute-start.26) | collective-permute-done | bytes 32800 | tf_op jit(solution)/shard_map/ppermute | solution.py:344
  78.1 1.6 %collective-permute-done.25 = bf16[32,512]{1,0:T(8,128)(2,1)S(1)} collective-permute-done((bf16[32,512]{1,0:T(8,128)(2,1)S(1)}, bf16[32,512]{1,0:T(8,128)(2,1)S(1)}, u32[]{:S(2)}, u32[]{:S(2)}) %collective-permute-start.25) | collective-permute-done | bytes 32800 | tf_op jit(solution)/shard_map/ppermute | solution.py:344
  80.9 1.3 %collective-permute-start.29 = (bf16[32,512]{1,0:T(8,128)(2,1)S(1)}, bf16[32,512]{1,0:T(8,128)(2,1)S(1)}, u32[]{:S(2)}, u32[]{:S(2)}) collective-permute-start(bf16[32,512]{1,0:T(8,128)(2,1)S(1)} %fusion), channel_id=1, source_target_pairs={{0,48},{1,49},{2,50},{3,51},{4,52},{5,53},{6,54},{7,55},{8,56},{9,... | collective-permute-start | bytes 98312 | tf_op jit(solution)/shard_map/ppermute | solution.py:344
  82.2 2.3 %collective-permute-start.27 = (bf16[32,512]{1,0:T(8,128)(2,1)S(1)}, bf16[32,512]{1,0:T(8,128)(2,1)S(1)}, u32[]{:S(2)}, u32[]{:S(2)}) collective-permute-start(bf16[32,512]{1,0:T(8,128)(2,1)S(1)} %fusion), channel_id=1, source_target_pairs={{0,16},{1,17},{2,18},{3,19},{4,20},{5,21},{6,22},{7,23},{8,24},{9,... | collective-permute-start | bytes 98312 | tf_op jit(solution)/shard_map/ppermute | solution.py:344
  86.3 3.0 %collective-permute-start.30 = (f32[32,512]{1,0:T(8,128)S(1)}, f32[32,512]{1,0:T(8,128)S(1)}, u32[]{:S(2)}, u32[]{:S(2)}) collective-permute-start(f32[32,512]{1,0:T(8,128)S(1)} %add_add_fusion.refs_9_), channel_id=1, source_target_pairs={{0,8},{1,9},{2,10},{3,11},{4,12},{5,13},{6,14},{7,15},{8,0},{9,1},... | collective-permute-start | bytes 196616 | tf_op jit(solution)/shard_map/ppermute | solution.py:344
  90.2 1.3 %respond.1 = f32[8,24,128]{2,1,0:T(8,128)S(1)} custom-call(s32[16]{0:T(128)S(1)} %get-tuple-element.27.refs_0_, bf16[2048,256]{1,0:T(8,128)(2,1)S(1)} %phases_0.1.refs_5_.refs_3_.refs_1_, bf16[2048,256]{1,0:T(8,128)(2,1)S(1)} %phases_1.1.refs_4_.refs_2_, bf16[2048,256]{1,0:T(8,128)(2,1)S(1)} %phases_2.1.refs_3_, bf16[2048,256]{1,0:T(8,128)(2,1)S(1)} %phases_3.1.refs_4_, ...), custom_call_target="tpu_custom_call" | custom-call | flops 100000000 | bytes 1048576 | tf_op jit(solution)/shard_map/respond/pallas_call | solution.py:57
  91.5 14.8 %all_to_all.5.refs_0_ = f32[8,24,128]{2,1,0:T(8,128)S(1)} all-to-all(f32[8,24,128]{2,1,0:T(8,128)S(1)} %respond.1), channel_id=1, replica_groups=mesh['slab'=32,'kgrp'=8] {'kgrp'}, dimensions={0} | all-to-all | bytes 196608 | tf_op jit(solution)/shard_map/all_to_all | solution.py:468
  (79 shorter events, 21.0 us)
Async XLA Ops:
  2.1 13.5 %collective-permute-start.1 = (bf16[144,128]{1,0:T(8,128)(2,1)}, bf16[144,128]{1,0:T(8,128)(2,1)S(1)}, u32[]{:S(2)}, u32[]{:S(2)}) collective-permute-start(bf16[144,128]{1,0:T(8,128)(2,1)} %get-tuple-element.28.refs_0_), channel_id=1, source_target_pairs={{0,248},{1,249},{2,250},{3,251},{4,252},{5,253},{6,254},{7,255},{8... | collective-permute-start | bytes 110600 | tf_op jit(solution)/shard_map/ppermute | solution.py:344
  5.1 10.5 %collective-permute-start.2 = (bf16[144,128]{1,0:T(8,128)(2,1)}, bf16[144,128]{1,0:T(8,128)(2,1)S(1)}, u32[]{:S(2)}, u32[]{:S(2)}) collective-permute-start(bf16[144,128]{1,0:T(8,128)(2,1)} %get-tuple-element.28.refs_0_), channel_id=1, source_target_pairs={{0,249},{1,248},{2,251},{3,250},{4,253},{5,252},{6,255},{7,254},{8... | collective-permute-start | bytes 110600 | tf_op jit(solution)/shard_map/ppermute | solution.py:344
  10.4 7.9 %collective-permute-start = (bf16[272,128]{1,0:T(8,128)(2,1)}, bf16[272,128]{1,0:T(8,128)(2,1)S(1)}, u32[]{:S(2)}, u32[]{:S(2)}) collective-permute-start(bf16[272,128]{1,0:T(8,128)(2,1)} %get-tuple-element.29.refs_1_), channel_id=1, source_target_pairs={{0,1},{1,0},{2,3},{3,2},{4,5},{5,4},{6,7},{7,6},{8,9},{9,8},{10,11... | collective-permute-start | bytes 208904 | tf_op jit(solution)/shard_map/ppermute | solution.py:344
  18.3 12.1 %collective-permute-start.3 = (bf16[4,144,128]{2,1,0:T(8,128)(2,1)S(1)}, bf16[4,144,128]{2,1,0:T(8,128)(2,1)S(1)}, u32[]{:S(2)}, u32[]{:S(2)}) collective-permute-start(bf16[4,144,128]{2,1,0:T(8,128)(2,1)S(1)} %stack_first.1.refs_1_.refs_0_.refs_2_), channel_id=1, source_target_pairs={{0,6},{1,7},{2,0},{3,1},{4,2},{5,3},{6,4},{7,5},{8,14},{9,15},{10,... | collective-permute-start | bytes 442376 | tf_op jit(solution)/shard_map/ppermute | solution.py:344
  21.1 9.4 %collective-permute-start.4 = (bf16[4,144,128]{2,1,0:T(8,128)(2,1)S(1)}, bf16[4,144,128]{2,1,0:T(8,128)(2,1)S(1)}, u32[]{:S(2)}, u32[]{:S(2)}) collective-permute-start(bf16[4,144,128]{2,1,0:T(8,128)(2,1)S(1)} %stack_first.1.refs_1_.refs_0_.refs_2_), channel_id=1, source_target_pairs={{0,4},{1,5},{2,6},{3,7},{4,0},{5,1},{6,2},{7,3},{8,12},{9,13},{10,... | collective-permute-start | bytes 442376 | tf_op jit(solution)/shard_map/ppermute | solution.py:344
  21.4 10.0 %collective-permute-start.5 = (bf16[4,144,128]{2,1,0:T(8,128)(2,1)S(1)}, bf16[4,144,128]{2,1,0:T(8,128)(2,1)S(1)}, u32[]{:S(2)}, u32[]{:S(2)}) collective-permute-start(bf16[4,144,128]{2,1,0:T(8,128)(2,1)S(1)} %stack_first.1.refs_1_.refs_0_.refs_2_), channel_id=1, source_target_pairs={{0,2},{1,3},{2,4},{3,5},{4,6},{5,7},{6,0},{7,1},{8,10},{9,11},{10,... | collective-permute-start | bytes 442376 | tf_op jit(solution)/shard_map/ppermute | solution.py:344
  22.1 6.0 %copy-start.4 = (f32[2,8,128]{2,1,0:T(8,128)S(1)}, f32[2,8,128]{2,1,0:T(8,128)}, u32[]{:S(2)}) copy-start(f32[2,8,128]{2,1,0:T(8,128)} %refs_14_.3) | copy-start | bytes 24580
  22.2 6.0 %collective-permute-start.6 = (bf16[2,144,128]{2,1,0:T(8,128)(2,1)S(1)}, bf16[2,144,128]{2,1,0:T(8,128)(2,1)S(1)}, u32[]{:S(2)}, u32[]{:S(2)}) collective-permute-start(bf16[2,144,128]{2,1,0:T(8,128)(2,1)S(1)} %slice.24), channel_id=1, source_target_pairs={{0,8},{1,9},{2,10},{3,11},{4,12},{5,13},{6,14},{7,15},{8,0},{9,1},... | collective-permute-start | bytes 221192 | tf_op jit(solution)/shard_map/ppermute | solution.py:344
  30.4 2.7 %collective-permute-start.7 = (bf16[2,144,128]{2,1,0:T(8,128)(2,1)S(1)}, bf16[2,144,128]{2,1,0:T(8,128)(2,1)S(1)}, u32[]{:S(2)}, u32[]{:S(2)}) collective-permute-start(bf16[2,144,128]{2,1,0:T(8,128)(2,1)S(1)} %pair_first.1), channel_id=1, source_target_pairs={{0,8},{1,9},{2,10},{3,11},{4,12},{5,13},{6,14},{7,15},{8,0},{9,1},... | collective-permute-start | bytes 221192 | tf_op jit(solution)/shard_map/ppermute | solution.py:344
  30.5 2.6 %collective-permute-start.8 = (bf16[2,144,128]{2,1,0:T(8,128)(2,1)S(1)}, bf16[2,144,128]{2,1,0:T(8,128)(2,1)S(1)}, u32[]{:S(2)}, u32[]{:S(2)}) collective-permute-start(bf16[2,144,128]{2,1,0:T(8,128)(2,1)S(1)} %slice.25), channel_id=1, source_target_pairs={{0,8},{1,9},{2,10},{3,11},{4,12},{5,13},{6,14},{7,15},{8,0},{9,1},... | collective-permute-start | bytes 221192 | tf_op jit(solution)/shard_map/ppermute | solution.py:344
  31.5 2.4 %collective-permute-start.9 = (bf16[2,144,128]{2,1,0:T(8,128)(2,1)S(1)}, bf16[2,144,128]{2,1,0:T(8,128)(2,1)S(1)}, u32[]{:S(2)}, u32[]{:S(2)}) collective-permute-start(bf16[2,144,128]{2,1,0:T(8,128)(2,1)S(1)} %slice.26), channel_id=1, source_target_pairs={{0,8},{1,9},{2,10},{3,11},{4,12},{5,13},{6,14},{7,15},{8,0},{9,1},... | collective-permute-start | bytes 221192 | tf_op jit(solution)/shard_map/ppermute | solution.py:344
  37.7 9.2 %collective-permute-start.10 = (bf16[128,128]{1,0:T(8,128)(2,1)S(1)}, bf16[128,128]{1,0:T(8,128)(2,1)S(1)}, u32[]{:S(2)}, u32[]{:S(2)}) collective-permute-start(bf16[128,128]{1,0:T(8,128)(2,1)S(1)} %get-tuple-element.37.refs_2_.refs_8_.refs_0_), channel_id=1, source_target_pairs={{0,1},{1,0},{2,3},{3,2},{4,5},{5,4},{6,7},{7,6},{8,9},{9,8},{10,11... | collective-permute-start | bytes 98312 | tf_op jit(solution)/shard_map/ppermute | solution.py:344
  40.0 6.9 %collective-permute-start.11 = (bf16[128,128]{1,0:T(8,128)(2,1)S(1)}, bf16[128,128]{1,0:T(8,128)(2,1)S(1)}, u32[]{:S(2)}, u32[]{:S(2)}) collective-permute-start(bf16[128,128]{1,0:T(8,128)(2,1)S(1)} %get-tuple-element.37.refs_2_.refs_8_.refs_0_), channel_id=1, source_target_pairs={{0,248},{1,249},{2,250},{3,251},{4,252},{5,253},{6,254},{7,255},{8... | collective-permute-start | bytes 98312 | tf_op jit(solution)/shard_map/ppermute | solution.py:344
  40.1 6.8 %collective-permute-start.12 = (bf16[128,128]{1,0:T(8,128)(2,1)S(1)}, bf16[128,128]{1,0:T(8,128)(2,1)S(1)}, u32[]{:S(2)}, u32[]{:S(2)}) collective-permute-start(bf16[128,128]{1,0:T(8,128)(2,1)S(1)} %get-tuple-element.37.refs_2_.refs_8_.refs_0_), channel_id=1, source_target_pairs={{0,249},{1,248},{2,251},{3,250},{4,253},{5,252},{6,255},{7,254},{8... | collective-permute-start | bytes 98312 | tf_op jit(solution)/shard_map/ppermute | solution.py:344
  47.0 11.0 %collective-permute-start.13 = (bf16[4,128,128]{2,1,0:T(8,128)(2,1)S(1)}, bf16[4,128,128]{2,1,0:T(8,128)(2,1)S(1)}, u32[]{:S(2)}, u32[]{:S(2)}) collective-permute-start(bf16[4,128,128]{2,1,0:T(8,128)(2,1)S(1)} %stack_second.1.refs_2_.refs_0_.refs_8_.refs_16_), channel_id=1, source_target_pairs={{0,6},{1,7},{2,0},{3,1},{4,2},{5,3},{6,4},{7,5},{8,14},{9,15},{10,... | collective-permute-start | bytes 393224 | tf_op jit(solution)/shard_map/ppermute | solution.py:344
  47.8 10.3 %collective-permute-start.14 = (bf16[4,128,128]{2,1,0:T(8,128)(2,1)S(1)}, bf16[4,128,128]{2,1,0:T(8,128)(2,1)S(1)}, u32[]{:S(2)}, u32[]{:S(2)}) collective-permute-start(bf16[4,128,128]{2,1,0:T(8,128)(2,1)S(1)} %stack_second.1.refs_2_.refs_0_.refs_8_.refs_16_), channel_id=1, source_target_pairs={{0,4},{1,5},{2,6},{3,7},{4,0},{5,1},{6,2},{7,3},{8,12},{9,13},{10,... | collective-permute-start | bytes 393224 | tf_op jit(solution)/shard_map/ppermute | solution.py:344
  49.2 9.5 %collective-permute-start.15 = (bf16[4,128,128]{2,1,0:T(8,128)(2,1)S(1)}, bf16[4,128,128]{2,1,0:T(8,128)(2,1)S(1)}, u32[]{:S(2)}, u32[]{:S(2)}) collective-permute-start(bf16[4,128,128]{2,1,0:T(8,128)(2,1)S(1)} %stack_second.1.refs_2_.refs_0_.refs_8_.refs_16_), channel_id=1, source_target_pairs={{0,2},{1,3},{2,4},{3,5},{4,6},{5,7},{6,0},{7,1},{8,10},{9,11},{10,... | collective-permute-start | bytes 393224 | tf_op jit(solution)/shard_map/ppermute | solution.py:344
  49.2 7.6 %collective-permute-start.16 = (bf16[2,128,128]{2,1,0:T(8,128)(2,1)S(1)}, bf16[2,128,128]{2,1,0:T(8,128)(2,1)S(1)}, u32[]{:S(2)}, u32[]{:S(2)}) collective-permute-start(bf16[2,128,128]{2,1,0:T(8,128)(2,1)S(1)} %slice.27), channel_id=1, source_target_pairs={{0,8},{1,9},{2,10},{3,11},{4,12},{5,13},{6,14},{7,15},{8,0},{9,1},... | collective-permute-start | bytes 196616 | tf_op jit(solution)/shard_map/ppermute | solution.py:344
  58.0 1.8 %collective-permute-start.17 = (bf16[2,128,128]{2,1,0:T(8,128)(2,1)S(1)}, bf16[2,128,128]{2,1,0:T(8,128)(2,1)S(1)}, u32[]{:S(2)}, u32[]{:S(2)}) collective-permute-start(bf16[2,128,128]{2,1,0:T(8,128)(2,1)S(1)} %pair_second.1), channel_id=1, source_target_pairs={{0,8},{1,9},{2,10},{3,11},{4,12},{5,13},{6,14},{7,15},{8,0},{9,1},... | collective-permute-start | bytes 196616 | tf_op jit(solution)/shard_map/ppermute | solution.py:344
  58.2 1.7 %collective-permute-start.18 = (bf16[2,128,128]{2,1,0:T(8,128)(2,1)S(1)}, bf16[2,128,128]{2,1,0:T(8,128)(2,1)S(1)}, u32[]{:S(2)}, u32[]{:S(2)}) collective-permute-start(bf16[2,128,128]{2,1,0:T(8,128)(2,1)S(1)} %slice.28), channel_id=1, source_target_pairs={{0,8},{1,9},{2,10},{3,11},{4,12},{5,13},{6,14},{7,15},{8,0},{9,1},... | collective-permute-start | bytes 196616 | tf_op jit(solution)/shard_map/ppermute | solution.py:344
  58.7 2.0 %collective-permute-start.19 = (bf16[2,128,128]{2,1,0:T(8,128)(2,1)S(1)}, bf16[2,128,128]{2,1,0:T(8,128)(2,1)S(1)}, u32[]{:S(2)}, u32[]{:S(2)}) collective-permute-start(bf16[2,128,128]{2,1,0:T(8,128)(2,1)S(1)} %slice.29), channel_id=1, source_target_pairs={{0,8},{1,9},{2,10},{3,11},{4,12},{5,13},{6,14},{7,15},{8,0},{9,1},... | collective-permute-start | bytes 196616 | tf_op jit(solution)/shard_map/ppermute | solution.py:344
  64.4 6.5 %collective-permute-start.20 = (f32[2,16,128]{2,1,0:T(8,128)S(1)}, f32[2,16,128]{2,1,0:T(8,128)S(1)}, u32[]{:S(2)}, u32[]{:S(2)}) collective-permute-start(f32[2,16,128]{2,1,0:T(8,128)S(1)} %second_rest.1.refs_2_.refs_5_), channel_id=1, source_target_pairs={{0,6},{1,7},{2,0},{3,1},{4,2},{5,3},{6,4},{7,5},{8,14},{9,15},{10,... | collective-permute-start | bytes 49160 | tf_op jit(solution)/shard_map/ppermute | solution.py:344
  66.4 4.4 %collective-permute-start.21 = (f32[2,16,128]{2,1,0:T(8,128)S(1)}, f32[2,16,128]{2,1,0:T(8,128)S(1)}, u32[]{:S(2)}, u32[]{:S(2)}) collective-permute-start(f32[2,16,128]{2,1,0:T(8,128)S(1)} %second_rest.1.refs_2_.refs_5_), channel_id=1, source_target_pairs={{0,4},{1,5},{2,6},{3,7},{4,0},{5,1},{6,2},{7,3},{8,12},{9,13},{10,... | collective-permute-start | bytes 49160 | tf_op jit(solution)/shard_map/ppermute | solution.py:344
  67.6 4.1 %collective-permute-start.22 = (f32[2,16,128]{2,1,0:T(8,128)S(1)}, f32[2,16,128]{2,1,0:T(8,128)S(1)}, u32[]{:S(2)}, u32[]{:S(2)}) collective-permute-start(f32[2,16,128]{2,1,0:T(8,128)S(1)} %second_rest.1.refs_2_.refs_5_), channel_id=1, source_target_pairs={{0,2},{1,3},{2,4},{3,5},{4,6},{5,7},{6,0},{7,1},{8,10},{9,11},{10,... | collective-permute-start | bytes 49160 | tf_op jit(solution)/shard_map/ppermute | solution.py:344
  73.0 2.3 %collective-permute-start.23 = (f32[32,512]{1,0:T(8,128)S(1)}, f32[32,512]{1,0:T(8,128)S(1)}, u32[]{:S(2)}, u32[]{:S(2)}) collective-permute-start(f32[32,512]{1,0:T(8,128)S(1)} %get-tuple-element.51), channel_id=1, source_target_pairs={{0,8},{1,9},{2,10},{3,11},{4,12},{5,13},{6,14},{7,15},{8,0},{9,1},... | collective-permute-start | bytes 196616 | tf_op jit(solution)/shard_map/ppermute | solution.py:344
  75.3 2.8 %collective-permute-start.26 = (bf16[32,512]{1,0:T(8,128)(2,1)S(1)}, bf16[32,512]{1,0:T(8,128)(2,1)S(1)}, u32[]{:S(2)}, u32[]{:S(2)}) collective-permute-start(bf16[32,512]{1,0:T(8,128)(2,1)S(1)} %get-tuple-element.52), channel_id=1, source_target_pairs={{0,192},{1,193},{2,194},{3,195},{4,196},{5,197},{6,198},{7,199},{8... | collective-permute-start | bytes 98312 | tf_op jit(solution)/shard_map/ppermute | solution.py:344
  75.3 4.4 %collective-permute-start.25 = (bf16[32,512]{1,0:T(8,128)(2,1)S(1)}, bf16[32,512]{1,0:T(8,128)(2,1)S(1)}, u32[]{:S(2)}, u32[]{:S(2)}) collective-permute-start(bf16[32,512]{1,0:T(8,128)(2,1)S(1)} %get-tuple-element.52), channel_id=1, source_target_pairs={{0,128},{1,129},{2,130},{3,131},{4,132},{5,133},{6,134},{7,135},{8... | collective-permute-start | bytes 98312 | tf_op jit(solution)/shard_map/ppermute | solution.py:344
  75.4 5.4 %collective-permute-start.24 = (bf16[32,512]{1,0:T(8,128)(2,1)S(1)}, bf16[32,512]{1,0:T(8,128)(2,1)S(1)}, u32[]{:S(2)}, u32[]{:S(2)}) collective-permute-start(bf16[32,512]{1,0:T(8,128)(2,1)S(1)} %get-tuple-element.52), channel_id=1, source_target_pairs={{0,64},{1,65},{2,66},{3,67},{4,68},{5,69},{6,70},{7,71},{8,72},{9,... | collective-permute-start | bytes 98312 | tf_op jit(solution)/shard_map/ppermute | solution.py:344
  80.9 4.7 %collective-permute-start.29 = (bf16[32,512]{1,0:T(8,128)(2,1)S(1)}, bf16[32,512]{1,0:T(8,128)(2,1)S(1)}, u32[]{:S(2)}, u32[]{:S(2)}) collective-permute-start(bf16[32,512]{1,0:T(8,128)(2,1)S(1)} %fusion), channel_id=1, source_target_pairs={{0,48},{1,49},{2,50},{3,51},{4,52},{5,53},{6,54},{7,55},{8,56},{9,... | collective-permute-start | bytes 98312 | tf_op jit(solution)/shard_map/ppermute | solution.py:344
  82.2 4.0 %collective-permute-start.28 = (bf16[32,512]{1,0:T(8,128)(2,1)S(1)}, bf16[32,512]{1,0:T(8,128)(2,1)S(1)}, u32[]{:S(2)}, u32[]{:S(2)}) collective-permute-start(bf16[32,512]{1,0:T(8,128)(2,1)S(1)} %fusion), channel_id=1, source_target_pairs={{0,32},{1,33},{2,34},{3,35},{4,36},{5,37},{6,38},{7,39},{8,40},{9,... | collective-permute-start | bytes 98312 | tf_op jit(solution)/shard_map/ppermute | solution.py:344
  82.2 4.0 %collective-permute-start.27 = (bf16[32,512]{1,0:T(8,128)(2,1)S(1)}, bf16[32,512]{1,0:T(8,128)(2,1)S(1)}, u32[]{:S(2)}, u32[]{:S(2)}) collective-permute-start(bf16[32,512]{1,0:T(8,128)(2,1)S(1)} %fusion), channel_id=1, source_target_pairs={{0,16},{1,17},{2,18},{3,19},{4,20},{5,21},{6,22},{7,23},{8,24},{9,... | collective-permute-start | bytes 98312 | tf_op jit(solution)/shard_map/ppermute | solution.py:344
  86.3 3.9 %collective-permute-start.30 = (f32[32,512]{1,0:T(8,128)S(1)}, f32[32,512]{1,0:T(8,128)S(1)}, u32[]{:S(2)}, u32[]{:S(2)}) collective-permute-start(f32[32,512]{1,0:T(8,128)S(1)} %add_add_fusion.refs_9_), channel_id=1, source_target_pairs={{0,8},{1,9},{2,10},{3,11},{4,12},{5,13},{6,14},{7,15},{8,0},{9,1},... | collective-permute-start | bytes 196616 | tf_op jit(solution)/shard_map/ppermute | solution.py:344
  (7 other events, 25.1 us)
